TPU v7x, 32 devices: a whole 2x2x4 slice. The times are simulated.
32 devices in a mesh: ctx: 16 (over z, y, core), fsdp: 2 (over x).
Axes of the slice: x: 2, y: 2, z: 4, core: 2. Of those that a mesh axis runs over, the one named last changes fastest.
Arguments:
- tokens: bfloat16 [24, 1024, 896], P('fsdp', 'ctx'), may hold values from -6 to 6
- positions: int32 [24, 1024], P('fsdp', 'ctx'), may hold values from 0 to 1023, as said below
- cotangent: bfloat16 [24, 1024, 896], P('fsdp', 'ctx'), may hold values from -6 to 6
- query_weight: bfloat16 [896, 896], P('fsdp'), may hold values from -0.1875 to 0.1875
- key_weight: bfloat16 [896, 128], P('fsdp'), may hold values from -0.1875 to 0.1875
- value_weight: bfloat16 [896, 128], P('fsdp'), may hold values from -0.1875 to 0.1875
- out_weight: bfloat16 [896, 896], P('fsdp'), may hold values from -0.75 to 0.75
- gate_weight: bfloat16 [896, 4864], P('fsdp'), may hold values from -0.1875 to 0.1875
- up_weight: bfloat16 [896, 4864], P('fsdp'), may hold values from -0.1875 to 0.1875
- down_weight: bfloat16 [4864, 896], P('fsdp'), may hold values from -0.078125 to 0.078125
- query_bias: bfloat16 [896], P('fsdp'), may hold values from -3 to 3
- key_bias: bfloat16 [128], P('fsdp'), may hold values from -3 to 3
- value_bias: bfloat16 [128], P('fsdp'), may hold values from -3 to 3
- first_gain: bfloat16 [896], P('fsdp'), may hold values from 0.099609375 to 1.8984375
- second_gain: bfloat16 [896], P('fsdp'), may hold values from 0.099609375 to 1.8984375
Outputs:
- mixed: bfloat16 [24, 1024, 896], P('fsdp', 'ctx')
- grad_tokens: float32 [24, 1024, 896], P('fsdp', 'ctx')
- grad_query_weight: float32 [896, 896], P('fsdp')
- grad_key_weight: float32 [896, 128], P('fsdp')
- grad_value_weight: float32 [896, 128], P('fsdp')
- grad_out_weight: float32 [896, 896], P('fsdp')
- grad_gate_weight: float32 [896, 4864], P('fsdp')
- grad_up_weight: float32 [896, 4864], P('fsdp')
- grad_down_weight: float32 [4864, 896], P('fsdp')
- grad_query_bias: float32 [896], P('fsdp')
- grad_key_bias: float32 [128], P('fsdp')
- grad_value_bias: float32 [128], P('fsdp')
- grad_first_gain: float32 [896], P('fsdp')
- grad_second_gain: float32 [896], P('fsdp')
Inputs may be any that keep to these rules, and one draw needn't show every extreme that they name: Each sequence's row is an ordering of 0 to 1023 built from blocks of 32 consecutive positions in rising order; each run of 64 stored entries that one index of ctx holds is block p followed by block 31 - p, with p differing from run to run.
All inputs are finite; a program needn't handle non-finite values.
Results may differ from a plain program's by a relative error of at most 0.02.
Values may be sent and summed in bfloat16 or wider, within the bound.
No kernel may reach another device: no remote copies, remote signals or barrier semaphores. Data moves between devices by JAX's collectives and lax.ppermute only.
A program may use at most 256 MiB of HBM per device.

v0:
```python
import jax
import jax.numpy as jnp
from jax import lax
from jax.sharding import PartitionSpec as P

Q_HEADS = 14
KV_HEADS = 2
HEAD_DIM = 64


epsilon = 1e-06
theta = 1000000.0


def rms_scale(rows, gain):
    inverse = lax.rsqrt(jnp.mean(rows * rows, axis=-1, keepdims=True) + epsilon)
    return rows * inverse * gain


def rope_tables(places, half):
    freq = theta ** (-jnp.arange(half, dtype=jnp.float32) / half)
    angles = places.astype(jnp.float32)[..., None] * freq
    return (jnp.cos(angles), jnp.sin(angles))


def rotate(values, cosine, sine):
    half = values.shape[-1] // 2
    front = values[..., :half]
    back = values[..., half:]
    cos_b = cosine[..., None, :]
    sin_b = sine[..., None, :]
    return jnp.concatenate([front * cos_b - back * sin_b, back * cos_b + front * sin_b], axis=-1)


def unrotate(grads, cosine, sine):
    half = grads.shape[-1] // 2
    front = grads[..., :half]
    back = grads[..., half:]
    cos_b = cosine[..., None, :]
    sin_b = sine[..., None, :]
    return jnp.concatenate([front * cos_b + back * sin_b, back * cos_b - front * sin_b], axis=-1)


def matmul(left, right):
    return jnp.dot(left, right, preferred_element_type=jnp.float32)


def body(
    tokens,
    positions,
    cotangent,
    query_weight,
    key_weight,
    value_weight,
    out_weight,
    gate_weight,
    up_weight,
    down_weight,
    query_bias,
    key_bias,
    value_bias,
    first_gain,
    second_gain,
):
    gathered = (
        lax.all_gather(query_weight, "fsdp", axis=0, tiled=True),
        lax.all_gather(key_weight, "fsdp", axis=0, tiled=True),
        lax.all_gather(value_weight, "fsdp", axis=0, tiled=True),
        lax.all_gather(out_weight, "fsdp", axis=0, tiled=True),
        lax.all_gather(gate_weight, "fsdp", axis=0, tiled=True),
        lax.all_gather(up_weight, "fsdp", axis=0, tiled=True),
        lax.all_gather(down_weight, "fsdp", axis=0, tiled=True),
        lax.all_gather(query_bias, "fsdp", axis=0, tiled=True),
        lax.all_gather(key_bias, "fsdp", axis=0, tiled=True),
        lax.all_gather(value_bias, "fsdp", axis=0, tiled=True),
        lax.all_gather(first_gain, "fsdp", axis=0, tiled=True),
        lax.all_gather(second_gain, "fsdp", axis=0, tiled=True),
    )
    (
        query_full,
        key_full,
        value_full,
        out_full,
        gate_full,
        up_full,
        down_full,
        qbias_full,
        kbias_full,
        vbias_full,
        fgain_full,
        sgain_full,
    ) = gathered
    seq_count, local, width = tokens.shape
    rows = seq_count * local
    group = Q_HEADS // KV_HEADS
    scale = HEAD_DIM ** (-0.5)
    kv_width = key_full.shape[1]
    inputs = tokens.reshape(rows, width).astype(jnp.float32)
    first_gain32 = fgain_full.astype(jnp.float32)
    first_low = rms_scale(inputs, first_gain32).astype(jnp.bfloat16)
    query_pre = matmul(first_low, query_full) + qbias_full.astype(jnp.float32)
    key_pre = matmul(first_low, key_full) + kbias_full.astype(jnp.float32)
    value_low = (matmul(first_low, value_full) + vbias_full.astype(jnp.float32)).astype(
        jnp.bfloat16
    )
    cosine, sine = rope_tables(positions.reshape(rows), HEAD_DIM // 2)
    query_rot = rotate(query_pre.reshape(rows, Q_HEADS, HEAD_DIM), cosine, sine).astype(
        jnp.bfloat16
    )
    key_rot = rotate(key_pre.reshape(rows, KV_HEADS, HEAD_DIM), cosine, sine).astype(jnp.bfloat16)
    key_places = lax.all_gather(positions, "ctx", axis=1, tiled=True)
    key_all, value_all = (
        lax.all_gather(key_rot.reshape(seq_count, local, kv_width), "ctx", axis=1, tiled=True),
        lax.all_gather(value_low.reshape(seq_count, local, kv_width), "ctx", axis=1, tiled=True),
    )
    query_seqs = query_rot.reshape(seq_count, local, Q_HEADS, HEAD_DIM)

    def scores_of(query_seq, key_seq, own_places, far_places):
        query_groups = query_seq.reshape(local, KV_HEADS, group, HEAD_DIM)
        key_heads = key_seq.reshape(-1, KV_HEADS, HEAD_DIM)
        raw = jnp.einsum(
            "qgjd,kgd->gjqk", query_groups, key_heads, preferred_element_type=jnp.float32
        )
        allowed = far_places[None, :] <= own_places[:, None]
        return (raw * scale, allowed)

    def attend(items):
        query_seq, key_seq, value_seq, own_places, far_places = items
        scaled, allowed = scores_of(query_seq, key_seq, own_places, far_places)
        masked = jnp.where(allowed[None, None], scaled, -1000000000.0)
        top = jnp.max(masked, axis=-1, keepdims=True)
        expo = jnp.exp(masked - top)
        total = jnp.sum(expo, axis=-1, keepdims=True)
        probs = expo / total
        value_heads = value_seq.reshape(-1, KV_HEADS, HEAD_DIM)
        result = jnp.einsum(
            "gjqk,kgd->qgjd",
            probs.astype(jnp.bfloat16),
            value_heads,
            preferred_element_type=jnp.float32,
        )
        return (result.reshape(local, Q_HEADS * HEAD_DIM), (top + jnp.log(total))[..., 0])

    attn_seqs, log_totals = lax.map(attend, (query_seqs, key_all, value_all, positions, key_places))
    attn_low = attn_seqs.reshape(rows, width).astype(jnp.bfloat16)
    middle = inputs + matmul(attn_low, out_full)
    second_gain32 = sgain_full.astype(jnp.float32)
    second_low = rms_scale(middle, second_gain32).astype(jnp.bfloat16)
    gate = matmul(second_low, gate_full)
    up_part = matmul(second_low, up_full)
    hidden_low = (jax.nn.silu(gate) * up_part).astype(jnp.bfloat16)
    mixed = (
        (middle + matmul(hidden_low, down_full))
        .astype(jnp.bfloat16)
        .reshape(seq_count, local, width)
    )
    regathered = (
        lax.all_gather(query_weight, "fsdp", axis=0, tiled=True),
        lax.all_gather(key_weight, "fsdp", axis=0, tiled=True),
        lax.all_gather(value_weight, "fsdp", axis=0, tiled=True),
        lax.all_gather(out_weight, "fsdp", axis=0, tiled=True),
        lax.all_gather(gate_weight, "fsdp", axis=0, tiled=True),
        lax.all_gather(up_weight, "fsdp", axis=0, tiled=True),
        lax.all_gather(down_weight, "fsdp", axis=0, tiled=True),
        lax.all_gather(query_bias, "fsdp", axis=0, tiled=True),
        lax.all_gather(key_bias, "fsdp", axis=0, tiled=True),
        lax.all_gather(value_bias, "fsdp", axis=0, tiled=True),
        lax.all_gather(first_gain, "fsdp", axis=0, tiled=True),
        lax.all_gather(second_gain, "fsdp", axis=0, tiled=True),
    )
    query_back, key_back, value_back, out_back, gate_back, up_back, down_back = regathered[:7]
    grad_in = cotangent.reshape(rows, width).astype(jnp.float32)
    grad_in_low = grad_in.astype(jnp.bfloat16)
    grad_down = matmul(hidden_low.T, grad_in_low)
    grad_hidden = matmul(grad_in_low, down_back.T)
    _, pull_mix = jax.vjp(lambda left, right: jax.nn.silu(left) * right, gate, up_part)
    grad_gate32, grad_up32 = pull_mix(grad_hidden)
    grad_gate_low = grad_gate32.astype(jnp.bfloat16)
    grad_up_low = grad_up32.astype(jnp.bfloat16)
    grad_gate_w = matmul(second_low.T, grad_gate_low)
    grad_up_w = matmul(second_low.T, grad_up_low)
    grad_second = matmul(grad_gate_low, gate_back.T) + matmul(grad_up_low, up_back.T)
    _, pull_second = jax.vjp(rms_scale, middle, second_gain32)
    grad_middle_part, grad_sgain = pull_second(grad_second)
    grad_middle = grad_in + grad_middle_part
    grad_branch_low = grad_middle.astype(jnp.bfloat16)
    grad_out_w = matmul(attn_low.T, grad_branch_low)
    grad_attn = (
        matmul(grad_branch_low, out_back.T).astype(jnp.bfloat16).reshape(seq_count, local, width)
    )

    def attend_back(items):
        query_seq, key_seq, value_seq, own_places, far_places, log_total, grad_seq = items
        scaled, allowed = scores_of(query_seq, key_seq, own_places, far_places)
        probs = jnp.where(allowed[None, None], jnp.exp(scaled - log_total[..., None]), 0.0)
        value_heads = value_seq.reshape(-1, KV_HEADS, HEAD_DIM)
        key_heads = key_seq.reshape(-1, KV_HEADS, HEAD_DIM)
        query_groups = query_seq.reshape(local, KV_HEADS, group, HEAD_DIM)
        grad_groups = grad_seq.reshape(local, KV_HEADS, group, HEAD_DIM)
        grad_probs = jnp.einsum(
            "qgjd,kgd->gjqk", grad_groups, value_heads, preferred_element_type=jnp.float32
        )
        inner = jnp.sum(probs * grad_probs, axis=-1, keepdims=True)
        grad_raw = (probs * (grad_probs - inner) * scale).astype(jnp.bfloat16)
        grad_query_seq = jnp.einsum(
            "gjqk,kgd->qgjd", grad_raw, key_heads, preferred_element_type=jnp.float32
        )
        grad_key_seq = jnp.einsum(
            "gjqk,qgjd->kgd", grad_raw, query_groups, preferred_element_type=jnp.float32
        )
        grad_value_seq = jnp.einsum(
            "gjqk,qgjd->kgd",
            probs.astype(jnp.bfloat16),
            grad_groups,
            preferred_element_type=jnp.float32,
        )
        return (
            grad_query_seq.reshape(local, Q_HEADS * HEAD_DIM),
            grad_key_seq.reshape(-1, kv_width),
            grad_value_seq.reshape(-1, kv_width),
        )

    grad_query_rot, grad_key_all, grad_value_all = lax.map(
        attend_back, (query_seqs, key_all, value_all, positions, key_places, log_totals, grad_attn)
    )
    grad_key_own, grad_value_own = (
        lax.psum_scatter(grad_key_all, "ctx", scatter_dimension=1, tiled=True),
        lax.psum_scatter(grad_value_all, "ctx", scatter_dimension=1, tiled=True),
    )
    grad_query_low = (
        unrotate(grad_query_rot.reshape(rows, Q_HEADS, HEAD_DIM), cosine, sine)
        .reshape(rows, width)
        .astype(jnp.bfloat16)
    )
    grad_key_low = (
        unrotate(grad_key_own.reshape(rows, KV_HEADS, HEAD_DIM), cosine, sine)
        .reshape(rows, kv_width)
        .astype(jnp.bfloat16)
    )
    grad_value_low = grad_value_own.reshape(rows, kv_width).astype(jnp.bfloat16)
    grad_qbias = jnp.sum(grad_query_low.astype(jnp.float32), axis=0)
    grad_kbias = jnp.sum(grad_key_low.astype(jnp.float32), axis=0)
    grad_vbias = jnp.sum(grad_value_low.astype(jnp.float32), axis=0)
    grad_query_w = matmul(first_low.T, grad_query_low)
    grad_key_w = matmul(first_low.T, grad_key_low)
    grad_value_w = matmul(first_low.T, grad_value_low)
    grad_first = (
        matmul(grad_query_low, query_back.T)
        + matmul(grad_key_low, key_back.T)
        + matmul(grad_value_low, value_back.T)
    )
    _, pull_first = jax.vjp(rms_scale, inputs, first_gain32)
    grad_input_part, grad_fgain = pull_first(grad_first)
    grad_tokens = (grad_middle + grad_input_part).reshape(seq_count, local, width)
    owned = (
        lax.psum_scatter(grad_query_w, "fsdp", scatter_dimension=0, tiled=True),
        lax.psum_scatter(grad_key_w, "fsdp", scatter_dimension=0, tiled=True),
        lax.psum_scatter(grad_value_w, "fsdp", scatter_dimension=0, tiled=True),
        lax.psum_scatter(grad_out_w, "fsdp", scatter_dimension=0, tiled=True),
        lax.psum_scatter(grad_gate_w, "fsdp", scatter_dimension=0, tiled=True),
        lax.psum_scatter(grad_up_w, "fsdp", scatter_dimension=0, tiled=True),
        lax.psum_scatter(grad_down, "fsdp", scatter_dimension=0, tiled=True),
        lax.psum_scatter(grad_qbias, "fsdp", scatter_dimension=0, tiled=True),
        lax.psum_scatter(grad_kbias, "fsdp", scatter_dimension=0, tiled=True),
        lax.psum_scatter(grad_vbias, "fsdp", scatter_dimension=0, tiled=True),
        lax.psum_scatter(grad_fgain, "fsdp", scatter_dimension=0, tiled=True),
        lax.psum_scatter(grad_sgain, "fsdp", scatter_dimension=0, tiled=True),
    )
    summed = lax.psum(
        (
            owned[0],
            owned[1],
            owned[2],
            owned[3],
            owned[4],
            owned[5],
            owned[6],
            owned[7],
            owned[8],
            owned[9],
            owned[10],
            owned[11],
        ),
        "ctx",
    )
    return (
        mixed,
        grad_tokens,
        summed[0],
        summed[1],
        summed[2],
        summed[3],
        summed[4],
        summed[5],
        summed[6],
        summed[7],
        summed[8],
        summed[9],
        summed[10],
        summed[11],
    )


def solution(mesh):
    in_specs = (
        P("fsdp", "ctx", None),
        P("fsdp", "ctx"),
        P("fsdp", "ctx", None),
        P("fsdp", None),
        P("fsdp", None),
        P("fsdp", None),
        P("fsdp", None),
        P("fsdp", None),
        P("fsdp", None),
        P("fsdp", None),
        P("fsdp"),
        P("fsdp"),
        P("fsdp"),
        P("fsdp"),
        P("fsdp"),
    )
    out_specs = (
        P("fsdp", "ctx", None),
        P("fsdp", "ctx", None),
        P("fsdp", None),
        P("fsdp", None),
        P("fsdp", None),
        P("fsdp", None),
        P("fsdp", None),
        P("fsdp", None),
        P("fsdp", None),
        P("fsdp"),
        P("fsdp"),
        P("fsdp"),
        P("fsdp"),
        P("fsdp"),
    )
    return jax.shard_map(body, mesh=mesh, in_specs=in_specs, out_specs=out_specs, check_vma=False)
```

profile of v0, /device:TPU:1, one launch (start us, length us, event | category | flops | bytes accessed | tf_op | source)
XLA Modules:
  0.0 2664.5 jit_solution(4405652974889453418)
XLA Ops:
  50.0 25.4 all-gather
  108.0 28.3 %all-gather.9.cloned.1.call-done = bf16[12,1024,128]{2,1,0:T(8,128)(2,1)} async-done(((bf16[12,64,128]{2,1,0:T(8,128)(2,1)}), bf16[12,1024,128]{2,1,0:T(8,128)(2,1)}) %all-gather.9.cloned.1.call-update) | async-done | bytes 3145744 | tf_op jit(solution)/shard_map/all_gather | solution.py:114
  141.0 64.3 %while.26 = (s32[]{:T(128)}, bf16[12,64,896]{2,1,0:T(8,128)(2,1)S(1)}, f32[12,2,7,64]{3,2,1,0:T(8,128)S(1)}, bf16[12,1024,128]{1,2,0:T(8,128)(2,1)}, s32[12,1024...) while((s32[]{:T(128)}, ...), condition=%wide.region_4.5_spmd, body=%wide.region_1.4_spmd.sunk | while | flops 245955712 | bytes 13818229 | solution.py:144
  210.9 64.4 %all-gather.17.cloned.1.call-done = bf16[896,4864]{1,0:T(8,128)(2,1)} async-done(((bf16[448,4864]{1,0:T(8,128)(2,1)}), bf16[896,4864]{1,0:T(8,128)(2,1)}) %all-gather.17.cloned.1.call-update) | async-done | bytes 8716304 | tf_op jit(solution)/shard_map/all_gather | solution.py:70
  275.3 14.2 fusion.45
  289.5 97.3 %all-gather.19.cloned.1.call-done = bf16[896,4864]{1,0:T(8,128)(2,1)} async-done(((bf16[448,4864]{1,0:T(8,128)(2,1)}), bf16[896,4864]{1,0:T(8,128)(2,1)}) %all-gather.19.cloned.1.call-update) | async-done | bytes 8716304 | tf_op jit(solution)/shard_map/all_gather | solution.py:71
  386.9 14.6 fusion.46
  401.4 97.1 %all-gather.21.cloned.1.call-done = bf16[4864,896]{1,0:T(8,128)(2,1)} async-done(((bf16[2432,896]{1,0:T(8,128)(2,1)}), bf16[4864,896]{1,0:T(8,128)(2,1)}) %all-gather.21.cloned.1.call-update) | async-done | bytes 8716304 | tf_op jit(solution)/shard_map/all_gather | solution.py:72
  498.6 24.9 multiply_convert_fusion
  523.5 14.0 fusion.47
  556.1 640.1 %while.27 = (s32[]{:T(128)}, f32[12,64,896]{1,0,2:T(8,128)}, f32[12,1024,128]{2,0,1:T(8,128)}, f32[12,1024,128]{2,1,0:T(8,128)}, bf16[12,1024,128]{1,2,0:T(8,128...) while((s32[]{:T(128)}, f32[12,64,896]{1,0,2:T(8,128)}, ...), condition=%wide.region_9.10_spmd, body=%wide.region_7.9_spmd.sunk | while | flops 600116992 | bytes 34758556 | solution.py:223
  571.4 14.8 dynamic_update_slice.30
  592.6 13.4 dynamic_update_slice.29
  624.7 14.8 dynamic_update_slice.30
  645.9 13.4 dynamic_update_slice.29
  678.1 14.8 dynamic_update_slice.30
  699.3 13.4 dynamic_update_slice.29
  731.4 14.8 dynamic_update_slice.30
  752.6 13.4 dynamic_update_slice.29
  784.7 14.8 dynamic_update_slice.30
  805.9 13.4 dynamic_update_slice.29
  838.1 14.8 dynamic_update_slice.30
  859.2 13.4 dynamic_update_slice.29
  891.4 14.8 dynamic_update_slice.30
  912.6 13.4 dynamic_update_slice.29
  944.7 14.8 dynamic_update_slice.30
  965.9 13.4 dynamic_update_slice.29
  998.1 14.8 dynamic_update_slice.30
  1019.3 13.4 dynamic_update_slice.29
  1051.4 14.8 dynamic_update_slice.30
  1072.6 13.4 dynamic_update_slice.29
  1104.7 14.8 dynamic_update_slice.30
  1125.9 13.4 dynamic_update_slice.29
  1158.0 14.8 dynamic_update_slice.30
  1179.2 13.4 dynamic_update_slice.29
  1219.6 81.5 %reduce-scatter.10.cloned.1.call-done = f32[12,64,128]{2,0,1:T(8,128)} async-done(((f32[12,1024,128]{2,0,1:T(8,128)}), f32[12,64,128]{2,0,1:T(8,128)}) %reduce-scatter.10.cloned.1.call-update) | async-done | bytes 393232 | tf_op jit(solution)/shard_map/reduce_scatter | solution.py:227
  1311.4 77.9 %reduce-scatter.12.cloned.1.call-done = f32[12,64,128]{2,1,0:T(8,128)} async-done(((f32[12,1024,128]{2,1,0:T(8,128)}), f32[12,64,128]{2,1,0:T(8,128)}) %reduce-scatter.12.cloned.1.call-update) | async-done | bytes 393232 | tf_op jit(solution)/shard_map/reduce_scatter | solution.py:228
  1406.3 13.1 fusion.53
  1420.7 14.6 fusion.54
  1435.4 46.4 %reduce-scatter.20.cloned.1.call-done = f32[448,896]{1,0:T(8,128)} async-done(((f32[896,896]{1,0:T(8,128)}), f32[448,896]{1,0:T(8,128)}) %reduce-scatter.20.cloned.1.call-update) | async-done | bytes 1605648 | tf_op jit(solution)/shard_map/reduce_scatter | solution.py:259
  1481.8 16.6 reduce-scatter.16.cloned.1.call-done
  1498.4 16.7 reduce-scatter.18.cloned.1.call-done
  1515.1 198.5 %reduce-scatter.22.cloned.1.call-done = f32[448,4864]{1,0:T(8,128)} async-done(((f32[896,4864]{1,0:T(8,128)}), f32[448,4864]{1,0:T(8,128)}) %reduce-scatter.22.cloned.1.call-update) | async-done | bytes 8716304 | tf_op jit(solution)/shard_map/reduce_scatter | solution.py:260
  1713.6 198.4 %reduce-scatter.24.cloned.1.call-done = f32[448,4864]{1,0:T(8,128)} async-done(((f32[896,4864]{1,0:T(8,128)}), f32[448,4864]{1,0:T(8,128)}) %reduce-scatter.24.cloned.1.call-update) | async-done | bytes 8716304 | tf_op jit(solution)/shard_map/reduce_scatter | solution.py:261
  1912.0 198.5 %reduce-scatter.26.cloned.1.call-done = f32[2432,896]{1,0:T(8,128)} async-done(((f32[4864,896]{1,0:T(8,128)}), f32[2432,896]{1,0:T(8,128)}) %reduce-scatter.26.cloned.1.call-update) | async-done | bytes 8716304 | tf_op jit(solution)/shard_map/reduce_scatter | solution.py:262
  2116.9 13.6 add_convert_fusion
  2141.6 34.0 %all-reduce.10 = (f32[448]{0:T(512)}, f32[64]{0:T(128)}, f32[64]{0:T(128)}, f32[448]{0:T(512)}, f32[448]{0:T(512)}) all-reduce(f32[448]{0:T(512)S(1)} %dynamic-slice.6, f32[64]{0:T(128)S(1)} %dynamic-slice.8, f32[64]{0:T(128)S(1)} %dynamic-slice.10, f32[448]{0:T(512)S(1)} %dynamic-slice.12, ...), channel_id=1, replica_groups=mesh['ctx'=16,'fsdp'=2] {'ctx'}, use_global_device_ids=true, to_apply=%region_29.30 | all-reduce | flops 1472 | bytes 11776 | tf_op jit(solution)/shard_map/psum | solution.py:269
  2180.6 453.4 %all-reduce.16.cloned.1.call-done = (f32[448,896]{1,0:T(8,128)}, f32[448,128]{1,0:T(8,128)}, f32[448,128]{1,0:T(8,128)}, f32[448,896]{1,0:T(8,128)}, f32[448,486...) async-done(((f32[448,896]{1,0:T(8,128)}, f32[448,128]{1,0:T(8,128)}, f32[448,128]{1,0:T(8,128)}, f32[448,896]{1,0:T(8,128)}, f32[448,4864]{1,0:T(8,128)}, ...) | async-done | bytes 29818896 | tf_op jit(solution)/shard_map/psum | solution.py:269
  (543 shorter events, 562.2 us)
Async XLA Ops:
  7.2 21.4 copy-start
  7.2 68.4 %all-gather.13.cloned.1.call-start = ((), (), s32[]{:S(2)}) async-start(), calls=%async_computation.11 | async-start | bytes 2408448 | tf_op jit(solution)/shard_map/all_gather | solution.py:66
  7.9 95.5 %all-gather.11.cloned.1.call-start = ((), (), s32[]{:S(2)}) async-start(), calls=%async_computation.10 | async-start | bytes 3342336 | tf_op jit(solution)/shard_map/all_gather | solution.py:113
  16.1 13.5 copy-start.12
  27.9 1.7 copy-start.28
  28.0 1.7 copy-start.30
  29.0 2.9 copy-start.35
  33.7 7.2 copy-start.9
  34.8 12.6 copy-start.10
  40.9 95.4 %all-gather.9.cloned.1.call-start = ((), (), s32[]{:S(2)}) async-start(), calls=%async_computation.9 | async-start | bytes 3342336 | tf_op jit(solution)/shard_map/all_gather | solution.py:114
  46.2 2.4 copy-start.14
  47.4 157.9 %all-gather.15.cloned.1.call-start = ((), (), s32[]{:S(2)}) async-start(), calls=%async_computation.12 | async-start | bytes 2408448 | tf_op jit(solution)/shard_map/all_gather | solution.py:69
  48.0 227.3 %all-gather.17.cloned.1.call-start = ((), (), s32[]{:S(2)}) async-start(), calls=%async_computation.13 | async-start | bytes 13074432 | tf_op jit(solution)/shard_map/all_gather | solution.py:70
  48.6 338.3 %all-gather.19.cloned.1.call-start = ((), (), s32[]{:S(2)}) async-start(), calls=%async_computation.14 | async-start | bytes 13074432 | tf_op jit(solution)/shard_map/all_gather | solution.py:71
  49.2 449.4 %all-gather.21.cloned.1.call-start = ((), (), s32[]{:S(2)}) async-start(), calls=%async_computation.15 | async-start | bytes 13074432 | tf_op jit(solution)/shard_map/all_gather | solution.py:72
  49.9 1251.2 %reduce-scatter.10.cloned.1.call-start = ((), (), s32[]{:S(2)}) async-start(), calls=%async_computation.16 | async-start | bytes 8912896 | tf_op jit(solution)/shard_map/reduce_scatter | solution.py:227
  80.3 3.6 copy-start.18
  80.3 3.6 copy-start.20
  108.0 33.0 %copy-start.37 = (bf16[12,64,896]{2,1,0:T(8,128)(2,1)S(1)}, bf16[12,64,896]{2,1,0:T(8,128)(2,1)}, u32[]{:S(2)}) copy-start(bf16[12,64,896]{2,1,0:T(8,128)(2,1)} %custom-call) | copy-start | bytes 4128772
  205.3 3.8 copy-start.38
  289.5 209.0 %copy-start.22 = (bf16[12,64,896]{2,1,0:T(8,128)(2,1)S(1)}, bf16[12,64,896]{2,1,0:T(8,128)(2,1)}, u32[]{:S(2)}) copy-start(bf16[12,64,896]{2,1,0:T(8,128)(2,1)} %param.21) | copy-start | bytes 4128772
  523.5 14.0 copy-start.2
  523.5 14.0 copy-start.5
  550.2 3.0 copy-start.36
  553.2 2.8 copy-start.3
  1196.2 193.1 %reduce-scatter.12.cloned.1.call-start = ((), (), s32[]{:S(2)}) async-start(), calls=%async_computation.17 | async-start | bytes 6684672 | tf_op jit(solution)/shard_map/reduce_scatter | solution.py:228
  1197.0 238.5 %reduce-scatter.14.cloned.1.call-start = ((), (), s32[]{:S(2)}) async-start(), calls=%async_computation.18 | async-start | bytes 4816896 | tf_op jit(solution)/shard_map/reduce_scatter | solution.py:256
  1199.1 7.2 copy-start.19
  1199.1 7.2 copy-start.21
  1206.3 3.9 copy-start.8
  1213.6 268.2 %reduce-scatter.20.cloned.1.call-start = ((), (), s32[]{:S(2)}) async-start(), calls=%async_computation.21 | async-start | bytes 4816896 | tf_op jit(solution)/shard_map/reduce_scatter | solution.py:259
  1219.6 278.9 %reduce-scatter.16.cloned.1.call-start = ((), (), s32[]{:S(2)}) async-start(), calls=%async_computation.19 | async-start | bytes 688128 | tf_op jit(solution)/shard_map/reduce_scatter | solution.py:257
  1311.4 203.8 %reduce-scatter.18.cloned.1.call-start = ((), (), s32[]{:S(2)}) async-start(), calls=%async_computation.20 | async-start | bytes 688128 | tf_op jit(solution)/shard_map/reduce_scatter | solution.py:258
  1393.1 320.5 %reduce-scatter.22.cloned.1.call-start = ((), (), s32[]{:S(2)}) async-start(), calls=%async_computation.22 | async-start | bytes 26148864 | tf_op jit(solution)/shard_map/reduce_scatter | solution.py:260
  1406.2 505.8 %reduce-scatter.24.cloned.1.call-start = ((), (), s32[]{:S(2)}) async-start(), calls=%async_computation.23 | async-start | bytes 26148864 | tf_op jit(solution)/shard_map/reduce_scatter | solution.py:261
  1419.4 691.1 %reduce-scatter.26.cloned.1.call-start = ((), (), s32[]{:S(2)}) async-start(), calls=%async_computation.24 | async-start | bytes 26148864 | tf_op jit(solution)/shard_map/reduce_scatter | solution.py:262
  1435.4 1198.6 %all-reduce.16.cloned.1.call-start = ((), (), s32[]{:S(2)}) async-start(), calls=%async_computation.25 | async-start | bytes 59637760 | tf_op jit(solution)/shard_map/psum | solution.py:269
  2112.0 4.9 copy-start.6
  2116.9 13.7 copy-start.13
  2130.6 1.8 copy-start.11
  2132.4 43.2 %copy-start.33 = (f32[768]{0:T(1024)S(1)}, f32[768]{0:T(1024)}, u32[]{:S(2)}) copy-start(f32[768]{0:T(1024)} %copy-done.32) | copy-start | bytes 9220
  2634.0 2.8 copy-start.27
  2634.0 3.5 copy-start.26
  2634.0 4.2 copy-start.16
  2639.3 8.6 copy-start.7
  2639.3 13.0 slice-start
  2639.3 14.6 slice-start.1
  2647.9 6.1 slice-start.2
  (11 other events, 12.5 us)
Sparse Core Ops, SparseCore 0:
  9.6 29.8 all-gather.12
  41.6 47.9 all-gather.10
  92.3 43.9 all-gather.8
  137.8 25.9 all-gather.14
  165.2 110.0 all-gather.16
  276.7 110.0 all-gather.18
  388.4 110.0 all-gather.20
  1196.4 104.7 reduce-scatter.9
  1305.1 84.2 reduce-scatter.11
  1391.5 43.8 reduce-scatter.13
  1437.7 44.0 reduce-scatter.19
  1484.6 13.7 reduce-scatter.15
  1501.3 13.8 reduce-scatter.17
  1517.4 196.1 reduce-scatter.21
  1715.8 196.1 reduce-scatter.23
  1914.3 196.1 reduce-scatter.25
  2116.2 517.7 all-reduce.15
where the time goes:
time: 2680 us; the launch traced here: 2660 us
  waiting for transfers between devices  1580 us (59%)
  local copies, waits for them, and re-layouts  498 us (19%)
  matrix products  439 us (16%)
  blocking collectives  80.7 us (3%)
  other arithmetic  47.4 us (2%)
    psum x1, waiting for transfers between devices, body(): lax.psum((owned[0], owned[1], owned[2], owned[3], owned[4], owned[5], own...  453 us
    reduce_scatter x1, waiting for transfers between devices, body(): lax.psum_scatter(grad_gate_w, 'fsdp', scatter_dimension=0, tiled=True)  199 us
    reduce_scatter x1, waiting for transfers between devices, body(): lax.psum_scatter(grad_down, 'fsdp', scatter_dimension=0, tiled=True)  198 us
    reduce_scatter x1, waiting for transfers between devices, body(): lax.psum_scatter(grad_up_w, 'fsdp', scatter_dimension=0, tiled=True)  198 us
    dynamic_update_slice x48, local copies, waits for them, and re-layouts, body(): lax.map(attend_back, (query_seqs, key_all, value_all, positions, key_plac...  194 us
    dot_general x21, matrix products, matmul(): return jnp.dot(left, right, preferred_element_type=jnp.float32)  171 us
    dynamic_update_slice x36, local copies, waits for them, and re-layouts, body(): lax.map(attend, (query_seqs, key_all, value_all, positions, key_places))  163 us
    all_gather x1, waiting for transfers between devices, body(): lax.all_gather(up_weight, 'fsdp', axis=0, tiled=True)  97.3 us
  transfers between devices with their start and end apart: 17, of which 13 were waited for; matrix products, arithmetic and copies ran while one was open for 10% of the time, Pallas kernels for 0%

commit v1 on v0

v1 whole, which is shorter than its diff:
```python
import functools

import jax
import jax.numpy as jnp
from jax import lax
from jax.experimental import pallas as pl
from jax.experimental.pallas import tpu as pltpu
from jax.sharding import Mesh, PartitionSpec as P

Q_HEADS = 14
KV_HEADS = 2
HEAD_DIM = 64
GROUP = Q_HEADS // KV_HEADS
HALF = HEAD_DIM // 2
BLK = 32
CORES = 2
Q_WIDTH = GROUP * HEAD_DIM

epsilon = 1e-06
theta = 1000000.0
scale = HEAD_DIM ** (-0.5)

BF = jnp.bfloat16
F32 = jnp.float32
CHIPS = ("cz", "cy")
VMEM = 56 * 1024 * 1024
SWAP = [(0, 1), (1, 0)]
NT = (((1,), (1,)), ((), ()))
TN = (((0,), (0,)), ((), ()))


def swap(values, axis):
    return lax.ppermute(values, axis, SWAP)


def dot(left, right, dims=(((1,), (0,)), ((), ()))):
    return lax.dot_general(left, right, dims, preferred_element_type=F32)


def rms_scale(rows, gain):
    inverse = lax.rsqrt(jnp.mean(rows * rows, axis=-1, keepdims=True) + epsilon)
    return rows * inverse * gain


def project_kernel(x_ref, gain_ref, w_ref, b_ref, cos_ref, sin_ref, first_ref, q_ref, kv_ref):
    rows = x_ref[...].astype(F32)
    first = rms_scale(rows, gain_ref[...]).astype(BF)
    first_ref[...] = first
    pre = dot(first, w_ref[...]) + b_ref[...]
    turned = Q_WIDTH + HEAD_DIM
    cosine = jnp.concatenate([cos_ref[...]] * (turned // 128), axis=1)
    sine = jnp.concatenate([sin_ref[...]] * (turned // 128), axis=1)
    front = pre[:, :turned]
    lane = lax.broadcasted_iota(jnp.int32, front.shape, 1) % HEAD_DIM
    other = jnp.where(
        lane < HALF, pltpu.roll(front, turned - HALF, 1), pltpu.roll(front, HALF, 1)
    )
    rot = front * cosine + other * sine
    q_ref[...] = (rot[:, :Q_WIDTH] * scale).astype(BF)
    kv_ref[...] = jnp.concatenate([rot[:, Q_WIDTH:], pre[:, turned:]], axis=1).astype(BF)


def project(rows, gain, weight, bias, cosine, sine):
    count, width = rows.shape
    wide = weight.shape[1]
    step = 256
    row_block = lambda n: pl.BlockSpec((step, n), lambda i: (i, 0))
    whole = lambda a, b: pl.BlockSpec((a, b), lambda i: (0, 0))
    return pl.pallas_call(
        project_kernel,
        grid=(count // step,),
        in_specs=[
            row_block(width),
            whole(1, width),
            whole(width, wide),
            whole(1, wide),
            row_block(128),
            row_block(128),
        ],
        out_specs=[row_block(width), row_block(Q_WIDTH), row_block(2 * HEAD_DIM)],
        out_shape=[
            jax.ShapeDtypeStruct((count, width), BF),
            jax.ShapeDtypeStruct((count, Q_WIDTH), BF),
            jax.ShapeDtypeStruct((count, 2 * HEAD_DIM), BF),
        ],
        compiler_params=pltpu.CompilerParams(vmem_limit_bytes=VMEM),
        cost_estimate=pl.CostEstimate(
            flops=2 * count * width * wide, bytes_accessed=count * width * 4, transcendentals=0
        ),
    )(rows, gain, weight, bias, cosine, sine)


def stack_heads(flat):
    return jnp.concatenate(
        [flat[:, h * HEAD_DIM : (h + 1) * HEAD_DIM] for h in range(GROUP)], axis=0
    )


def fill_bias(offset, starts_ref, qpos_ref, bias_ref):
    own = qpos_ref[0]
    inside = lax.broadcasted_iota(jnp.int32, (BLK, own.shape[1]), 0)
    seq = pl.program_id(0) + offset
    for j in range(bias_ref.shape[0] // BLK):
        far = inside + starts_ref[seq, j]
        bias_ref[j * BLK : (j + 1) * BLK, :] = jnp.where(far <= own, 0.0, -1e30)


def query_chunks(local):
    total = GROUP * local
    return [(lo, min(lo + 2 * local, total)) for lo in range(0, total, 2 * local)]


def attend_kernel(offset, starts_ref, qpos_ref, q_ref, kv_ref, o_ref, lse_ref, bias_ref):
    local = 2 * q_ref.shape[2]
    keys = bias_ref.shape[0]
    fill_bias(offset, starts_ref, qpos_ref, bias_ref)
    kv = kv_ref[...].reshape(keys, 2 * HEAD_DIM)
    key = kv[:, :HEAD_DIM]
    value_t = kv.astype(F32).T[HEAD_DIM:].astype(BF)
    query = stack_heads(q_ref[...].reshape(local, Q_WIDTH))
    heads = []
    for lo, hi in query_chunks(local):
        bias = jnp.concatenate([bias_ref[...]] * ((hi - lo) // local), axis=1)
        scores = dot(key, query[lo:hi], NT) + bias
        top = jnp.max(scores, axis=0, keepdims=True)
        expo = jnp.exp(scores - top)
        total = jnp.sum(expo, axis=0, keepdims=True)
        out = dot(value_t, expo.astype(BF)) / total
        lse_ref[0, :, lo:hi] = top + jnp.log(total)
        heads += [out[:, at : at + local].T for at in range(0, hi - lo, local)]
    o_ref[...] = jnp.concatenate(heads, axis=1).astype(BF).reshape(o_ref.shape)


def attend_back_kernel(
    offset,
    starts_ref,
    qpos_ref,
    q_ref,
    kv_ref,
    do_ref,
    lse_ref,
    cos_ref,
    sin_ref,
    dq_ref,
    dkv_ref,
    bias_ref,
    probs_ref,
    grads_ref,
):
    local = 2 * q_ref.shape[2]
    keys = bias_ref.shape[0]
    fill_bias(offset, starts_ref, qpos_ref, bias_ref)
    kv = kv_ref[...].reshape(keys, 2 * HEAD_DIM)
    key = kv[:, :HEAD_DIM]
    value = kv[:, HEAD_DIM:]
    key_t = kv.astype(F32).T[:HEAD_DIM].astype(BF)
    query = stack_heads(q_ref[...].reshape(local, Q_WIDTH))
    grad_o = stack_heads(do_ref[...].reshape(local, Q_WIDTH))
    cosine = cos_ref[0]
    sine = sin_ref[0]
    heads = []
    for lo, hi in query_chunks(local):
        bias = jnp.concatenate([bias_ref[...]] * ((hi - lo) // local), axis=1)
        scores = dot(key, query[lo:hi], NT) + bias
        probs = jnp.exp(scores - lse_ref[0, :, lo:hi])
        probs_ref[:, lo:hi] = probs.astype(BF)
        grad_p = dot(value, grad_o[lo:hi], NT)
        inner = jnp.sum(probs * grad_p, axis=0, keepdims=True)
        grad_s = (probs * (grad_p - inner)).astype(BF)
        grads_ref[:, lo:hi] = grad_s
        grad_q = dot(key_t, grad_s) * scale
        for at in range(0, hi - lo, local):
            front = grad_q[:HALF, at : at + local]
            back = grad_q[HALF:, at : at + local]
            turned = jnp.concatenate(
                [front * cosine + back * sine, back * cosine - front * sine], axis=0
            )
            heads.append(turned.T)
    dq_ref[...] = jnp.concatenate(heads, axis=1).astype(BF).reshape(dq_ref.shape)
    grad_k = dot(grads_ref[...], query)
    grad_v = dot(probs_ref[...], grad_o)
    dkv_ref[...] = jnp.concatenate([grad_k, grad_v], axis=1).astype(BF).reshape(dkv_ref.shape)


def attention(back, offset, seqs, starts, qpos, q, kv, *more):
    run = q.shape[2]
    chips = kv.shape[0]
    local = 2 * run
    keys = chips * local
    total = GROUP * local
    q_spec = pl.BlockSpec((2, 1, run, Q_WIDTH), lambda s, st: (0, s + offset, 0, 0))
    part_spec = pl.BlockSpec((2, 1, run, Q_WIDTH), lambda s, st: (0, s, 0, 0))
    kv_block = (chips, 2, 1, run, 2 * HEAD_DIM)
    kv_spec = pl.BlockSpec(kv_block, lambda s, st: (0, 0, s + offset, 0, 0))
    kv_part_spec = pl.BlockSpec(kv_block, lambda s, st: (0, 0, s, 0, 0))
    lse_spec = pl.BlockSpec((1, 1, total), lambda s, st: (s + offset, 0, 0))
    qpos_spec = pl.BlockSpec((1, 1, local), lambda s, st: (s + offset, 0, 0))
    turn_spec = pl.BlockSpec((1, HALF, local), lambda s, st: (s + offset, 0, 0))
    in_specs = [qpos_spec, q_spec, kv_spec]
    scratch = [pltpu.VMEM((keys, local), F32)]
    part_shape = jax.ShapeDtypeStruct((2, seqs, run, Q_WIDTH), BF)
    if back:
        in_specs += [q_spec, lse_spec, turn_spec, turn_spec]
        out_specs = [part_spec, kv_part_spec]
        kv_shape = kv.shape[:2] + (seqs,) + kv.shape[3:]
        out_shape = [part_shape, jax.ShapeDtypeStruct(kv_shape, BF)]
        scratch += [pltpu.VMEM((keys, total), BF)] * 2
    else:
        out_specs = [part_spec, lse_spec]
        out_shape = [part_shape, jax.ShapeDtypeStruct((seqs, 1, total), F32)]
    passes = 5 if back else 2
    return pl.pallas_call(
        functools.partial(attend_back_kernel if back else attend_kernel, offset),
        grid_spec=pltpu.PrefetchScalarGridSpec(
            num_scalar_prefetch=1,
            grid=(seqs,),
            in_specs=in_specs,
            out_specs=out_specs,
            scratch_shapes=scratch,
        ),
        out_shape=out_shape,
        compiler_params=pltpu.CompilerParams(vmem_limit_bytes=VMEM),
        cost_estimate=pl.CostEstimate(
            flops=8 * passes * seqs * keys * total * HEAD_DIM,
            bytes_accessed=seqs * keys * 512,
            transcendentals=seqs * keys * total,
        ),
    )(starts, qpos, q, kv, *more)


def mlp_kernel(s_ref, c_ref, g_ref, u_ref, d_ref, hid_ref, gg_ref, gu_ref, mix_ref, gs_ref):
    rows = s_ref[...]
    grad = c_ref[...]
    wide = g_ref.shape[1]
    for lo in range(0, wide, 256):
        hi = min(lo + 256, wide)
        gate = dot(rows, g_ref[:, lo:hi])
        up = dot(rows, u_ref[:, lo:hi])
        grad_hidden = dot(grad, d_ref[lo:hi, :], NT)
        sig = 1.0 / (1.0 + jnp.exp(-gate))
        silu = gate * sig
        hid_ref[:, lo:hi] = (silu * up).astype(BF)
        gg_ref[:, lo:hi] = (grad_hidden * up * (sig * (1.0 + gate * (1.0 - sig)))).astype(BF)
        gu_ref[:, lo:hi] = (grad_hidden * silu).astype(BF)
    mix_ref[...] = dot(hid_ref[...], d_ref[...]).astype(BF)
    gs_ref[...] = (dot(gg_ref[...], g_ref[...], NT) + dot(gu_ref[...], u_ref[...], NT)).astype(BF)


def mlp(rows, grad, gate_w, up_w, down_w):
    count, width = rows.shape
    wide = gate_w.shape[1]
    step = 256
    row_block = lambda n: pl.BlockSpec((step, n), lambda i: (i, 0))
    whole = lambda a, b: pl.BlockSpec((a, b), lambda i: (0, 0))
    shape = lambda n: jax.ShapeDtypeStruct((count, n), BF)
    return pl.pallas_call(
        mlp_kernel,
        grid=(count // step,),
        in_specs=[
            row_block(width),
            row_block(width),
            whole(width, wide),
            whole(width, wide),
            whole(wide, width),
        ],
        out_specs=[row_block(wide)] * 3 + [row_block(width)] * 2,
        out_shape=[shape(wide)] * 3 + [shape(width)] * 2,
        compiler_params=pltpu.CompilerParams(vmem_limit_bytes=VMEM),
        cost_estimate=pl.CostEstimate(
            flops=12 * count * width * wide,
            bytes_accessed=count * (wide * 6 + width * 8),
            transcendentals=count * wide,
        ),
    )(rows, grad, gate_w, up_w, down_w)


def weight_grad_kernel(a_near, a_far, b_near, b_far, out_ref, acc_ref):
    step = pl.program_id(0)
    steps = pl.num_programs(0)

    @pl.when(step == 0)
    def _():
        acc_ref[...] = dot(a_near[...], b_near[...], TN)

    @pl.when(jnp.logical_and(step > 0, step < steps // 2))
    def _():
        acc_ref[...] += dot(a_near[...], b_near[...], TN)

    @pl.when(jnp.logical_and(step >= steps // 2, step < steps - 1))
    def _():
        acc_ref[...] += dot(a_far[...], b_far[...], TN)

    @pl.when(step == steps - 1)
    def _():
        out_ref[...] = (acc_ref[...] + dot(a_far[...], b_far[...], TN)).astype(BF)


def weight_grad(near, far):
    (a_near, b_near), (a_far, b_far) = near, far
    count, high = a_near.shape
    wide = b_near.shape[1]
    half = 2
    step = count // half
    near_block = lambda n: pl.BlockSpec((step, n), lambda i: (jnp.minimum(i, half - 1), 0))
    far_block = lambda n: pl.BlockSpec((step, n), lambda i: (jnp.maximum(i - half, 0), 0))
    return pl.pallas_call(
        weight_grad_kernel,
        grid=(2 * half,),
        in_specs=[near_block(high), far_block(high), near_block(wide), far_block(wide)],
        out_specs=pl.BlockSpec((high, wide), lambda i: (0, 0)),
        out_shape=jax.ShapeDtypeStruct((high, wide), BF),
        scratch_shapes=[pltpu.VMEM((high, wide), F32)],
        compiler_params=pltpu.CompilerParams(vmem_limit_bytes=VMEM),
        cost_estimate=pl.CostEstimate(
            flops=4 * count * high * wide,
            bytes_accessed=4 * count * (high + wide),
            transcendentals=0,
        ),
    )(a_near, a_far, b_near, b_far)


def gather_small(values, axis, size):
    out = values[None]
    index = lax.axis_index(axis)
    bit = 1
    while bit < size:
        other = lax.ppermute(out, axis, [(i, i ^ bit) for i in range(size)])
        low = (index & bit) == 0
        out = jnp.where(
            low, jnp.concatenate([out, other], axis=0), jnp.concatenate([other, out], axis=0)
        )
        bit *= 2
    return out


def line_part(values, at):
    at = jnp.clip(at, 0, values.shape[0] - 1)
    return lax.dynamic_index_in_dim(values, at, 0, keepdims=False).astype(F32)


def line_load(values, axis, step, arrived):
    size = values.shape[0]
    index = lax.axis_index(axis)
    far = size - 1 - step
    up, down = line_part(values, index + far), line_part(values, index - far)
    if step:
        up, down = up + arrived[0].astype(F32), down + arrived[1].astype(F32)
    return up.astype(BF), down.astype(BF)


def line_send(load, axis, size, step):
    far = size - 1 - step
    right = [(i, i + 1) for i in range(size - 1) if i <= step]
    left = [(i + 1, i) for i in range(size - 1) if i + 1 >= far]
    return lax.ppermute(load[0], axis, right), lax.ppermute(load[1], axis, left)


def line_total(values, axis, arrived):
    own = line_part(values, lax.axis_index(axis))
    return (own + arrived[0].astype(F32) + arrived[1].astype(F32)).astype(BF)


def line_gather(values, axis, size):
    index = lax.axis_index(axis)
    right = left = values
    rights, lefts = [], []
    for step in range(size - 1):
        right = lax.ppermute(right, axis, [(i, i + 1) for i in range(size - 1) if i >= step])
        left = lax.ppermute(
            left, axis, [(i + 1, i) for i in range(size - 1) if i + 1 <= size - 1 - step]
        )
        rights.append(right)
        lefts.append(left)
    row = jnp.stack(rights[::-1] + [values] + lefts)
    return lax.dynamic_slice_in_dim(row, size - 1 - index, size, 0)


def pair_sum(values, axis, size):
    bit = 1
    while bit < size:
        other = lax.ppermute(values, axis, [(i, i ^ bit) for i in range(size)])
        values = (values.astype(F32) + other.astype(F32)).astype(values.dtype)
        bit *= 2
    return values


def after(first, *rest):
    return lax.optimization_barrier((first, *rest))[1:]


def make_body(sizes):
    cz, outer = sizes["cz"], sizes["outer"]
    chips = cz * sizes["cy"]
    owners = 2 * outer

    def ordered(axis, own, other):
        low = lax.axis_index(axis) == 0
        return jnp.where(low, own, other), jnp.where(low, other, own)

    def gather_rows(values):
        rows = values.shape[0]
        if outer > 1:
            values = lax.all_gather(values, "outer", axis=0)
        else:
            values = values[None]
        both = jnp.stack(ordered("pair", values, swap(values, "pair")), axis=1)
        return both.reshape((owners * rows,) + values.shape[2:])

    def sum_owners(values):
        split = values.reshape(outer, 2, -1, values.shape[1])
        if outer > 1:
            split = lax.psum_scatter(split, "outer", scatter_dimension=0)
        else:
            split = split[0]
        low = lax.axis_index("pair") == 0
        keep = jnp.where(low, split[0], split[1])
        send = jnp.where(low, split[1], split[0])
        return (keep.astype(F32) + swap(send, "pair").astype(F32)).astype(BF)

    def gather_chips(values):
        return lax.all_gather(values, CHIPS, axis=0)

    def scatter_chips(values):
        return lax.psum_scatter(values, CHIPS, scatter_dimension=0)

    def sum_chips(values):
        return pair_sum(pair_sum(values, "cy", 2), "cz", cz)

    def body(
        tokens,
        positions,
        cotangent,
        query_weight,
        key_weight,
        value_weight,
        out_weight,
        gate_weight,
        up_weight,
        down_weight,
        query_bias,
        key_bias,
        value_bias,
        first_gain,
        second_gain,
    ):
        core0 = lax.axis_index("core") == 0
        pair = lax.axis_index("pair")
        quarter = 2 * lax.axis_index("cy") + lax.axis_index("core")
        seqs, run, width = tokens.shape
        rows = seqs * run
        ff = gate_weight.shape[1]
        part = down_weight.shape[0]
        window = min(part, -(-part // 512) * 128)
        begins = [min(q * window, part - window) for q in range(4)]
        skips = [min(q * window - begins[q], window) for q in range(4)]
        slab = gate_weight.shape[0]

        def heads_of(values, each):
            return jnp.where(core0, values[..., :each], values[..., each:])

        turned = Q_WIDTH + HEAD_DIM
        kv_rows = key_bias.shape[0]
        vectors = jnp.concatenate([query_bias, key_bias, value_bias, first_gain, second_gain])
        lanes = vectors.shape[0]
        wide = turned + HEAD_DIM
        lines = -(-lanes // wide)
        vectors = jnp.concatenate([vectors, jnp.zeros((16 * wide - lanes,), BF)]).reshape(16, wide)
        qkv_local = jnp.concatenate(
            [
                jnp.concatenate(
                    [
                        heads_of(query_weight, Q_WIDTH),
                        heads_of(key_weight, HEAD_DIM),
                        heads_of(value_weight, HEAD_DIM),
                    ],
                    axis=1,
                ),
                vectors,
            ]
        )
        tokens_far = swap(tokens, "core")
        def by_quarter(choices):
            out = choices[3]
            for q in range(3):
                out = jnp.where(quarter == q, choices[q], out)
            return out

        def columns(values, q):
            at = [owner * part + begins[q] for owner in range(owners)]
            return jnp.concatenate([values[:, a : a + window] for a in at], axis=1)

        inside = lax.broadcasted_iota(jnp.int32, (1, owners * window), 1) % window
        skip = by_quarter([jnp.int32(n) for n in skips])

        def units(values):
            full = by_quarter([columns(values, q) for q in range(4)])
            return jnp.where(inside < skip, jnp.zeros((), BF), full)

        gate_own = units(gate_weight)
        up_own = units(up_weight)
        down_own = by_quarter([down_weight[at : at + window] for at in begins])
        qkv_all = gather_rows(qkv_local)
        qkv_all, gate_own, up_own, out_own, down_own = lax.optimization_barrier(
            (qkv_all, gate_own, up_own, out_weight, down_own)
        )
        qkv_all = qkv_all.reshape(owners, slab + 16, wide)
        qkv = qkv_all[:, :slab].reshape(owners * slab, wide)
        vectors = qkv_all[:, slab:].reshape(owners, -1)

        def vector_of(at, size):
            return vectors[:, at : at + size].reshape(-1)

        qb = vector_of(0, slab)
        kb = vector_of(slab, kv_rows)
        vb = vector_of(slab + kv_rows, kv_rows)
        fgain = vector_of(slab + 2 * kv_rows, slab).astype(F32)
        sgain = vector_of(2 * slab + 2 * kv_rows, slab).astype(F32)
        bias = jnp.concatenate(
            [heads_of(qb, Q_WIDTH), heads_of(kb, HEAD_DIM), heads_of(vb, HEAD_DIM)]
        ).astype(F32)[None]
        out_full = gather_rows(out_own)
        out_w = jnp.where(core0, out_full[:Q_WIDTH], out_full[Q_WIDTH:])
        down_w = gather_rows(down_own)
        gate_w = gather_rows(gate_own)
        up_w = gather_rows(up_own)

        places = jnp.stack([positions, swap(positions, "core")])
        firsts = places[:, :, ::BLK]
        starts = gather_small(gather_small(firsts, "cy", 2), "cz", cz)
        starts = starts.transpose(3, 0, 1, 2, 4).reshape(seqs, -1)
        qpos = places.transpose(1, 0, 2).reshape(seqs, 1, 2 * run)
        freq = theta ** (-jnp.arange(HALF, dtype=F32) / HALF)
        angles = places.reshape(2 * rows, 1).astype(F32) * freq
        cosine, sine = jnp.cos(angles), jnp.sin(angles)
        cos_wide = jnp.concatenate([cosine] * 4, axis=1)
        sin_wide = jnp.concatenate([-sine, sine] * 2, axis=1)

        def turned_rows(table):
            table = table.reshape(2, seqs, run, HALF).transpose(1, 3, 0, 2)
            return table.reshape(seqs, HALF, 2 * run)

        own_rows = tokens.reshape(rows, width)
        chip_rows = jnp.concatenate([own_rows, tokens_far.reshape(rows, width)])
        first, q, kv = project(
            chip_rows, fgain[None], qkv, bias, cos_wide, sin_wide
        )
        q = q.reshape(2, seqs, run, Q_WIDTH)
        kv = kv.reshape(2, seqs, run, 2 * HEAD_DIM)
        cut = seqs // 2
        kv_all = gather_chips(kv)
        kv_all, out_w, down_w, gate_w, cot_late = lax.optimization_barrier(
            (kv_all, out_w, down_w, gate_w, cotangent)
        )
        grad_own = cot_late.reshape(rows, width)
        far_grad = swap(grad_own, "cy")
        attn, lse = attention(False, 0, seqs, starts, qpos, q, kv_all)
        attn_rows = attn.reshape(2 * rows, Q_WIDTH)
        attn_rows, up_w, far_grad = lax.optimization_barrier((attn_rows, up_w, far_grad))
        attn_part = dot(attn_rows, out_w).astype(BF)
        inputs = own_rows.astype(F32)
        middle = (
            inputs
            + attn_part[:rows].astype(F32)
            + swap(attn_part[rows:], "core").astype(F32)
        )

        second = rms_scale(middle, sgain).astype(BF)
        near_c = jnp.concatenate([grad_own, swap(grad_own, "core")])
        far_c = jnp.concatenate([far_grad, swap(far_grad, "core")])
        far_second = swap(second, "cy")
        near_s = jnp.concatenate([second, swap(second, "core")])
        near_h, near_g, near_u, near_mix, near_gs = mlp(near_s, near_c, gate_w, up_w, down_w)
        far_second, near_h, near_g, near_u, near_mix, near_gs = lax.optimization_barrier(
            (far_second, near_h, near_g, near_u, near_mix, near_gs)
        )
        far_s = jnp.concatenate([far_second, swap(far_second, "core")])
        far_h, far_g, far_u, far_mix, far_gs = mlp(far_s, far_c, gate_w, up_w, down_w)

        def sum_back(near, far):
            far_own = far[:rows].astype(F32) + swap(far[rows:], "core").astype(F32)
            near_own = near[:rows].astype(F32) + swap(near[rows:], "core").astype(F32)
            return near_own + swap(far_own.astype(BF), "cy").astype(F32)

        grad_second = sum_back(near_gs, far_gs)
        near_gs, far_gs, near_g, near_u, near_h = lax.optimization_barrier(
            (near_gs, far_gs, near_g, near_u, near_h)
        )
        grad_down_w = weight_grad((near_h, near_c), (far_h, far_c))
        grad_gate_w = weight_grad((near_s, near_g), (far_s, far_g))
        grad_up_w = weight_grad((near_s, near_u), (far_s, far_u))
        sums = [sum_owners(values) for values in (grad_down_w, grad_gate_w, grad_up_w)]
        each = slab // cz
        line = jnp.concatenate([v.reshape(cz, each, owners * window) for v in sums], axis=1)

        _, pull_second = jax.vjp(rms_scale, middle, sgain)
        grad_middle_part, grad_sgain = pull_second(grad_second)
        grad_middle = grad_own.astype(F32) + grad_middle_part
        grad_branch = grad_middle.astype(BF)
        grad_branch = jnp.concatenate([grad_branch, swap(grad_branch, "core")])
        grad_out_w = dot(attn_rows, grad_branch, TN).astype(BF)
        grad_attn = dot(grad_branch, out_w, NT).astype(BF).reshape(2, seqs, run, Q_WIDTH)

        cos_t, sin_t = turned_rows(cosine), turned_rows(sine)

        arrived = None
        parts = []
        for step in range(cz - 1):
            loads = line_load(line, "cz", step, arrived)
            if step < 2:
                loads, grad_attn = lax.optimization_barrier((loads, grad_attn))
                grad_q_part, grad_kv_part = attention(
                    True,
                    step * cut,
                    seqs - cut if step else cut,
                    starts,
                    qpos,
                    q,
                    kv_all,
                    grad_attn,
                    lse,
                    cos_t,
                    sin_t,
                )
            arrived = line_send(loads, "cz", cz, step)
            if step < 2:
                grad_q_part, grad_kv_part, arrived = lax.optimization_barrier(
                    (grad_q_part, grad_kv_part, arrived)
                )
                parts.append((grad_q_part, scatter_chips(grad_kv_part)))
        (grad_q_near, grad_kv_near), (grad_q_far, grad_kv_far) = parts
        grad_q_near, near_mix, far_mix = lax.optimization_barrier((grad_q_near, near_mix, far_mix))
        mixed = (middle + sum_back(near_mix, far_mix)).astype(BF).reshape(seqs, run, width)
        grad_q = jnp.concatenate([grad_q_near, grad_q_far], axis=1).reshape(2 * rows, Q_WIDTH)
        grad_q_w = dot(first, grad_q, TN).astype(BF)
        grad_kv = jnp.concatenate([grad_kv_near, grad_kv_far], axis=1)
        grad_kv = grad_kv.reshape(2 * rows, 2 * HEAD_DIM).astype(F32)
        front = grad_kv[:, :HALF]
        back = grad_kv[:, HALF:HEAD_DIM]
        grad_kv = jnp.concatenate(
            [front * cosine + back * sine, back * cosine - front * sine, grad_kv[:, HEAD_DIM:]],
            axis=1,
        ).astype(BF)
        grad_qkv = jnp.concatenate([grad_q, grad_kv], axis=1)
        grad_kv_w = dot(first, grad_kv, TN).astype(BF)
        grad_biases = jnp.sum(grad_qkv.astype(F32), axis=0)
        grad_first_part = dot(grad_qkv, qkv, NT).astype(BF)
        grad_first = grad_first_part[:rows].astype(F32) + swap(
            grad_first_part[rows:], "core"
        ).astype(F32)
        _, pull_first = jax.vjp(rms_scale, inputs, fgain)
        grad_input_part, grad_fgain = pull_first(grad_first)
        grad_tokens = (grad_middle + grad_input_part).reshape(seqs, run, width)

        mine = line_total(line, "cz", arrived)
        mine_down = line_gather(mine[:each], "cz", cz).reshape(window, width)
        near, far = ordered("cy", mine_down, swap(mine_down, "cy"))
        both = jnp.stack([near, far])
        low, high = ordered("core", both, swap(both, "core"))
        down_parts = [low[0], high[0], low[1], high[1]]
        out_down = jnp.concatenate(
            [w[n:] for w, n in zip(down_parts, skips) if n < window]
        ).astype(F32)

        def full_columns(values):
            every = lax.all_gather(values, CHIPS + ("core",), axis=0)
            every = every.reshape(cz, 4, each, owners * window)
            pieces = [
                every[:, q, :, owner * window + skips[q] : (owner + 1) * window]
                for owner in range(owners)
                for q in range(4)
                if skips[q] < window
            ]
            return jnp.concatenate(pieces, axis=2).reshape(slab, ff).astype(F32)

        out_gate = full_columns(mine[each : 2 * each])
        out_up = full_columns(mine[2 * each :])

        def own_rows_of(values):
            return sum_chips(sum_owners(values))

        def both_cores(values):
            return [v.astype(F32) for v in ordered("core", values, swap(values, "core"))]

        all_out = jnp.concatenate(ordered("core", grad_out_w, swap(grad_out_w, "core")))
        early = sum_owners(jnp.concatenate([all_out, grad_q_w], axis=1))
        early = jnp.concatenate(
            [heads_of(early[:, :width], width // 2), early[:, width:]], axis=1
        )
        low_early, high_early = both_cores(sum_chips(early))
        out_out = jnp.concatenate([low_early[:, : width // 2], high_early[:, : width // 2]], axis=1)
        out_query = jnp.concatenate(
            [low_early[:, width // 2 :], high_early[:, width // 2 :]], axis=1
        )
        low_kv, high_kv = both_cores(own_rows_of(grad_kv_w))
        out_key = jnp.concatenate([low_kv[:, :HEAD_DIM], high_kv[:, :HEAD_DIM]], axis=1)
        out_value = jnp.concatenate([low_kv[:, HEAD_DIM:], high_kv[:, HEAD_DIM:]], axis=1)

        zeros = jnp.zeros((), F32)

        def spread(values):
            return jnp.concatenate(
                [jnp.where(core0, values, zeros), jnp.where(core0, zeros, values)]
            )

        vector = jnp.concatenate(
            [
                spread(grad_biases[:Q_WIDTH]),
                spread(grad_biases[Q_WIDTH:turned]),
                spread(grad_biases[turned:]),
                grad_fgain,
                grad_sgain,
            ]
        )
        vector = pair_sum(pair_sum(sum_chips(vector), "core", CORES), "pair", 2)
        if outer > 1:
            vector = pair_sum(vector, "outer", outer)
        owner = 2 * lax.axis_index("outer") + pair
        vectors = []
        at = 0
        for size in (width, KV_HEADS * HEAD_DIM, KV_HEADS * HEAD_DIM, width, width):
            each = size // owners
            vectors.append(lax.dynamic_slice(vector, (at + owner * each,), (each,)))
            at += size
        return (
            mixed,
            grad_tokens,
            out_query,
            out_key,
            out_value,
            out_out,
            out_gate,
            out_up,
            out_down,
            *vectors,
        )

    return body


def solution(mesh):
    ctx, fsdp = mesh.shape["ctx"], mesh.shape["fsdp"]
    sizes = {"cz": ctx // (2 * CORES), "cy": 2, "core": CORES, "outer": fsdp // 2, "pair": 2}
    fine = Mesh(mesh.devices.reshape(tuple(sizes.values())), tuple(sizes))
    ctx_axes = ("cz", "cy", "core")
    fsdp_axes = ("outer", "pair")
    in_specs = (
        P(fsdp_axes, ctx_axes, None),
        P(fsdp_axes, ctx_axes),
        P(fsdp_axes, ctx_axes, None),
        *[P(fsdp_axes, None)] * 7,
        *[P(fsdp_axes)] * 5,
    )
    out_specs = (
        P(fsdp_axes, ctx_axes, None),
        P(fsdp_axes, ctx_axes, None),
        *[P(fsdp_axes, None)] * 7,
        *[P(fsdp_axes)] * 5,
    )
    return jax.shard_map(
        make_body(sizes), mesh=fine, in_specs=in_specs, out_specs=out_specs, check_vma=False
    )
```

time: 2680 us -> 766 us (0.29)
  waiting for transfers between devices: 1580 us -> 224 us
  matrix products: 439 us -> 18.4 us
  local copies, waits for them, and re-layouts: 498 us -> 79.2 us
  Pallas kernels: 0 us -> 207 us
  other arithmetic: 47.4 us -> 134 us
  blocking collectives: 80.7 us -> 0 us
  starting transfers between devices: 0.68 us -> 76.5 us
    reduce_scatter x9 -> x2, waiting for transfers between devices: 834 us -> 0.01 us  [scatter_chips(): return lax.psum_scatter(values, CHIPS, scatter_dimension=0)]
    psum x1 -> x0, waiting for transfers between devices: 453 us -> none  [body(): lax.psum((owned[0], owned[1], owned[2], owned[3], owned[4], owned[5], own...]
    dot_general x105 -> x6, matrix products: 439 us -> 18.4 us  [dot(): return lax.dot_general(left, right, dims, preferred_element_type=F32)]
    dynamic_update_slice x84 -> x0, local copies, waits for them, and re-layouts: 358 us -> none  [the longest x48 194 us: body(): lax.map(attend_back, (query_seqs, key_all, value_all, positions, key_plac...]
    all_gather x7 -> x3, waiting for transfers between devices: 287 us -> 0.04 us  [the longest x2 0.04 us: full_columns(): every = lax.all_gather(values, CHIPS + ('core',), axis=0)]
    ppermute x0 -> x58, waiting for transfers between devices: none -> 224 us  [the longest x32 111 us: swap(): return lax.ppermute(values, axis, SWAP)]
    pallas_call x0 -> x9, Pallas kernels: none -> 207 us  [the longest x3 87.6 us: attention(): pl.pallas_call(functools.partial(attend_back_kernel if back else attend_k...]
    ppermute x0 -> x58, starting transfers between devices: none -> 76 us  [the longest x32 28.8 us: swap(): return lax.ppermute(values, axis, SWAP)]
  transfers between devices with their start and end apart: 17 -> 63, of which waited for: 13 -> 26; matrix products, arithmetic and copies ran while one was open for 10% -> 26% of each run, Pallas kernels for 0% -> 26%
where the time goes in v1:
time: 766 us; the launch traced here: 754 us
  waiting for transfers between devices  224 us (29%)
  Pallas kernels  207 us (27%)
  other arithmetic  134 us (17%)
  local copies, waits for them, and re-layouts  79.2 us (10%)
  starting transfers between devices  76.5 us (10%)
  matrix products  18.4 us (2%)
  between operations  15.2 us (2%)
    ppermute x32, waiting for transfers between devices, swap(): return lax.ppermute(values, axis, SWAP)  111 us
    pallas_call x3, Pallas kernels, attention(): pl.pallas_call(functools.partial(attend_back_kernel if back else attend_k...  87.6 us
    ppermute x11, waiting for transfers between devices, pair_sum(): other = lax.ppermute(values, axis, [(i, i ^ bit) for i in range(size)])  74.6 us
    pallas_call x2, Pallas kernels, mlp(): pl.pallas_call(mlp_kernel, grid=(count // step,), in_specs=[row_block(wid...  71.8 us
    pallas_call x3, Pallas kernels, weight_grad(): pl.pallas_call(weight_grad_kernel, grid=(2 * half,), in_specs=[near_block...  39 us
    ppermute x32, starting transfers between devices, swap(): return lax.ppermute(values, axis, SWAP)  28.8 us
    dot_general x6, matrix products, dot(): return lax.dot_general(left, right, dims, preferred_element_type=F32)  18.4 us
    unnamed x152, local copies, waits for them, and re-layouts  15.8 us
  transfers between devices with their start and end apart: 63, of which 26 were waited for; matrix products, arithmetic and copies ran while one was open for 26% of the time, Pallas kernels for 26%

profile of v1, /device:TPU:1, one launch (start us, length us, event | category | flops | bytes accessed | tf_op | source)
XLA Modules:
  0.0 754.1 jit_solution(17971988465324818067)
XLA Ops:
  7.8 3.5 concatenate.197
  17.5 4.1 fusion.47
  31.6 2.8 fusion.19
  42.0 3.1 pad_maximum_fusion.1.x_ref
  45.1 8.7 %shard_map.254 = (bf16[1536,896]{1,0:T(8,128)(2,1)}, bf16[1536,448]{1,0:T(8,128)(2,1)}, bf16[1536,128]{1,0:T(8,128)(2,1)}) custom-call(bf16[1536,896]{1,0:T(8,128)(2,1)} %pad_maximum_fusion.1.x_ref, f32[1,896]{1,0:T(1,128)} %reshape.430.gain_ref, bf16[896,576]{1,0:T(8,128)(2,1)} %bitcast.219, f32[1,576]{1,0:T(1,128)} %maximum_convert_fusion.1.b_ref, ...), custom_call_target="tpu_custom_call" | custom-call | flops 1585446912 | bytes 5505024 | tf_op jit(solution)/shard_map/pallas_call | solution.py:69
  66.9 30.5 %collective-permute-done.6 = bf16[1,448,896]{2,1,0:T(8,128)(2,1)} collective-permute-done((bf16[1,448,896]{2,1,0:T(8,128)(2,1)S(1)}, bf16[1,448,896]{2,1,0:T(8,128)(2,1)}, u32[]{:S(2)}, u32[]{:S(2)}) %collective-permute-start.6) | collective-permute-done | bytes 802848 | tf_op jit(solution)/shard_map/ppermute | solution.py:33
  102.7 19.3 %collective-permute-done.8 = bf16[1,448,1280]{2,1,0:T(8,128)(2,1)} collective-permute-done((bf16[1,448,1280]{2,1,0:T(8,128)(2,1)}, bf16[1,448,1280]{2,1,0:T(8,128)(2,1)}, u32[]{:S(2)}, u32[]{:S(2)}) %collective-permute-start.8) | collective-permute-done | bytes 1146912 | tf_op jit(solution)/shard_map/ppermute | solution.py:33
  126.1 20.4 %collective-permute-done.9 = bf16[1,448,1280]{2,1,0:T(8,128)(2,1)} collective-permute-done((bf16[1,448,1280]{2,1,0:T(8,128)(2,1)S(1)}, bf16[1,448,1280]{2,1,0:T(8,128)(2,1)}, u32[]{:S(2)}, u32[]{:S(2)}) %collective-permute-start.9) | collective-permute-done | bytes 1146912 | tf_op jit(solution)/shard_map/ppermute | solution.py:33
  149.5 36.3 %shard_map.255 = (bf16[2,12,64,448]{3,2,1,0:T(8,128)(2,1)}, f32[12,1,896]{2,1,0:T(1,128)}) custom-call(s32[12,32]{1,0:T(8,128)} %copy.111.starts_ref, s32[12,1,128]{2,1,0:T(1,128)} %reshape.407.qpos_ref, bf16[2,12,64,448]{3,2,1,0:T(8,128)(2,1)} %bitcast.231, bf16[8,2,12,64,128]{4,3,2,1,0:T(8,128)(2,1)} %all-gather.6.cloned.1.call-done.kv_ref), custom_call_target="tpu_custom_call" | custom-call | flops 11274289152 | bytes 6291456 | tf_op jit(solution)/shard_map/pallas_call | solution.py:212
  185.9 3.2 convolution_convert_fusion.1
  195.2 2.9 multiply_reduce_fusion.3
  199.6 3.1 pad_maximum_fusion.3.c_ref.b_near
  205.7 30.2 %shard_map.256 = (bf16[1536,1280]{1,0:T(8,128)(2,1)}, bf16[1536,1280]{1,0:T(8,128)(2,1)}, bf16[1536,1280]{1,0:T(8,128)(2,1)}, bf16[1536,896]{1,0:T(8,128)(2,1)}, bf16[1536,896]{1,0:T(8,128)(2,1)}) custom-call(bf16[1536,896]{1,0:T(8,128)(2,1)} %pad_maximum_fusion.2.s_ref.a_near, bf16[1536,896]{1,0:T(8,128)(2,1)} %pad_maximum_fusion.3.c_ref.b_near, ...), custom_call_target="tpu_custom_call" | custom-call | flops 21139292160 | bytes 22806528 | tf_op jit(solution)/shard_map/pallas_call | solution.py:256
  251.2 41.6 %shard_map.257 = (bf16[1536,1280]{1,0:T(8,128)(2,1)}, bf16[1536,1280]{1,0:T(8,128)(2,1)}, bf16[1536,1280]{1,0:T(8,128)(2,1)}, bf16[1536,896]{1,0:T(8,128)(2,1)}, bf16[1536,896]{1,0:T(8,128)(2,1)}) custom-call(bf16[1536,896]{1,0:T(8,128)(2,1)} %constant_dynamic-update-slice_fusion.s_ref.a_far, bf16[1536,896]{1,0:T(8,128)(2,1)} %copy-done.44, ...), custom_call_target="tpu_custom_call" | custom-call | flops 21139292160 | bytes 22806528 | tf_op jit(solution)/shard_map/pallas_call | solution.py:256
  295.8 12.6 %shard_map.260 = bf16[896,1280]{1,0:T(8,128)(2,1)} custom-call(bf16[1536,896]{1,0:T(8,128)(2,1)} %pad_maximum_fusion.2.s_ref.a_near, bf16[1536,896]{1,0:T(8,128)(2,1)} %constant_dynamic-update-slice_fusion.s_ref.a_far, bf16[1536,1280]{1,0:T(8,128)(2,1)} %get-tuple-element.103.b_near, bf16[1536,1280]{1,0:T(8,128)(2,1)} %get-tuple-element.104.b_far), custom_call_target="tpu_custom_call" | custom-call | flops 7046430720 | bytes 13369344 | tf_op jit(solution)/shard_map/pallas_call | solution.py:306
  311.4 12.5 %shard_map.259 = bf16[896,1280]{1,0:T(8,128)(2,1)} custom-call(bf16[1536,896]{1,0:T(8,128)(2,1)} %pad_maximum_fusion.2.s_ref.a_near, bf16[1536,896]{1,0:T(8,128)(2,1)} %constant_dynamic-update-slice_fusion.s_ref.a_far, bf16[1536,1280]{1,0:T(8,128)(2,1)} %get-tuple-element.101.b_near, bf16[1536,1280]{1,0:T(8,128)(2,1)} %get-tuple-element.102.b_far), custom_call_target="tpu_custom_call" | custom-call | flops 7046430720 | bytes 13369344 | tf_op jit(solution)/shard_map/pallas_call | solution.py:306
  323.9 2.9 broadcast_select_fusion.4
  331.0 13.9 %shard_map.258 = bf16[1280,896]{1,0:T(8,128)(2,1)} custom-call(bf16[1536,1280]{1,0:T(8,128)(2,1)} %get-tuple-element.99.a_near, bf16[1536,1280]{1,0:T(8,128)(2,1)} %get-tuple-element.100.a_far, bf16[1536,896]{1,0:T(8,128)(2,1)} %pad_maximum_fusion.3.c_ref.b_near, bf16[1536,896]{1,0:T(8,128)(2,1)} %copy-done.44), custom_call_target="tpu_custom_call" | custom-call | flops 7046430720 | bytes 13369344 | tf_op jit(solution)/shard_map/pallas_call | solution.py:306
  349.9 12.2 %collective-permute-done.22 = bf16[768,896]{1,0:T(8,128)(2,1)} collective-permute-done((bf16[768,896]{1,0:T(8,128)(2,1)}, bf16[768,896]{1,0:T(8,128)(2,1)}, u32[]{:S(2)}, u32[]{:S(2)}) %collective-permute-start.22) | collective-permute-done | bytes 1376288 | tf_op jit(solution)/shard_map/ppermute | solution.py:33
  362.2 3.0 multiply_reduce_fusion
  365.2 5.0 fusion.39
  371.7 15.6 %collective-permute-done.17 = bf16[640,896]{1,0:T(8,128)(2,1)S(1)} collective-permute-done((bf16[640,896]{1,0:T(8,128)(2,1)S(1)}, bf16[640,896]{1,0:T(8,128)(2,1)S(1)}, u32[]{:S(2)}, u32[]{:S(2)}) %collective-permute-start.17) | collective-permute-done | bytes 1146912 | tf_op jit(solution)/shard_map/ppermute | solution.py:33
  388.7 3.3 reshape.420
  398.1 4.5 convolution_convert_fusion.2
  405.1 4.2 collective-permute-start.24
  410.9 25.6 %shard_map.261 = (bf16[2,6,64,448]{3,2,1,0:T(8,128)(2,1)}, bf16[8,2,6,64,128]{4,3,2,1,0:T(8,128)(2,1)}) custom-call(s32[12,32]{1,0:T(8,128)} %copy.111.starts_ref, s32[12,1,128]{2,1,0:T(1,128)} %reshape.407.qpos_ref, bf16[2,12,64,448]{3,2,1,0:T(8,128)(2,1)} %bitcast.232, bf16[8,2,12,64,128]{4,3,2,1,0:T(8,128)(2,1)} %all-gather.6.cloned.1.call-done.kv_ref, ...), custom_call_target="tpu_custom_call" | custom-call | flops 14092861440 | bytes 3145728 | tf_op jit(solution)/shard_map/pallas_call | solution.py:212
  442.8 25.7 %shard_map.262 = (bf16[2,6,64,448]{3,2,1,0:T(8,128)(2,1)}, bf16[8,2,6,64,128]{4,3,2,1,0:T(8,128)(2,1)}) custom-call(s32[12,32]{1,0:T(8,128)} %copy.111.starts_ref, s32[12,1,128]{2,1,0:T(1,128)} %reshape.407.qpos_ref, bf16[2,12,64,448]{3,2,1,0:T(8,128)(2,1)} %bitcast.233, bf16[8,2,12,64,128]{4,3,2,1,0:T(8,128)(2,1)} %all-gather.6.cloned.1.call-done.kv_ref, ...), custom_call_target="tpu_custom_call" | custom-call | flops 14092861440 | bytes 3145728 | tf_op jit(solution)/shard_map/pallas_call | solution.py:212
  470.5 3.5 fusion.9
  475.3 8.6 %collective-permute-start.43 = (bf16[336,1280]{1,0:T(8,128)(2,1)}, bf16[336,1280]{1,0:T(8,128)(2,1)}, u32[]{:S(2)}, u32[]{:S(2)}) collective-permute-start(bf16[336,1280]{1,0:T(8,128)(2,1)} %get-tuple-element.172), channel_id=1, source_target_pairs={{0,8},{8,16},{16,24},{1,9},{9,17},{17,25},{2,10},{10,18},{18,26},{... | collective-permute-start | bytes 2580488 | tf_op jit(solution)/shard_map/ppermute | solution.py:355
  483.9 3.8 fusion.14
  489.4 15.5 %collective-permute-done.44 = bf16[336,1280]{1,0:T(8,128)(2,1)} collective-permute-done((bf16[336,1280]{1,0:T(8,128)(2,1)}, bf16[336,1280]{1,0:T(8,128)(2,1)}, u32[]{:S(2)}, u32[]{:S(2)}) %collective-permute-start.44) | collective-permute-done | bytes 860192 | tf_op jit(solution)/shard_map/ppermute | solution.py:355
  530.0 4.2 collective-permute-start.45
  538.3 4.6 collective-permute-done.45
  546.6 10.4 %collective-permute-done.33 = bf16[448,1344]{1,0:T(8,128)(2,1)} collective-permute-done((bf16[448,1344]{1,0:T(8,128)(2,1)}, bf16[448,1344]{1,0:T(8,128)(2,1)}, u32[]{:S(2)}, u32[]{:S(2)}) %collective-permute-start.33) | collective-permute-done | bytes 1204256 | tf_op jit(solution)/shard_map/ppermute | solution.py:33
  563.2 9.6 %collective-permute-done.50 = bf16[112,1280]{1,0:T(8,128)(2,1)S(1)} collective-permute-done((bf16[112,1280]{1,0:T(8,128)(2,1)S(1)}, bf16[112,1280]{1,0:T(8,128)(2,1)S(1)}, u32[]{:S(2)}, u32[]{:S(2)}) %collective-permute-start.50) | collective-permute-done | bytes 286752 | tf_op jit(solution)/shard_map/ppermute | solution.py:369
  573.9 3.2 reshape.429
  578.9 13.2 %collective-permute-done.34 = bf16[448,896]{1,0:T(8,128)(2,1)} collective-permute-done((bf16[448,896]{1,0:T(8,128)(2,1)}, bf16[448,896]{1,0:T(8,128)(2,1)}, u32[]{:S(2)}, u32[]{:S(2)}) %collective-permute-start.34) | collective-permute-done | bytes 802848 | tf_op jit(solution)/shard_map/ppermute | solution.py:381
  601.6 3.8 add_convert_fusion
  605.4 19.6 %collective-permute-done.35 = bf16[448,896]{1,0:T(8,128)(2,1)S(1)} collective-permute-done((bf16[448,896]{1,0:T(8,128)(2,1)}, bf16[448,896]{1,0:T(8,128)(2,1)S(1)}, u32[]{:S(2)}, u32[]{:S(2)}) %collective-permute-start.35) | collective-permute-done | bytes 802848 | tf_op jit(solution)/shard_map/ppermute | solution.py:381
  626.3 4.5 collective-permute-start.36
  634.0 4.3 collective-permute-start.52
  639.7 3.6 fusion.21
  645.8 3.2 convolution_convert_fusion
  656.6 19.3 %collective-permute-done.40 = bf16[448,128]{1,0:T(8,128)(2,1)S(1)} collective-permute-done((bf16[448,128]{1,0:T(8,128)(2,1)S(1)}, bf16[448,128]{1,0:T(8,128)(2,1)S(1)}, u32[]{:S(2)}, u32[]{:S(2)}) %collective-permute-start.40) | collective-permute-done | bytes 114720 | tf_op jit(solution)/shard_map/ppermute | solution.py:381
  676.0 13.0 %collective-permute-done.41 = bf16[448,128]{1,0:T(8,128)(2,1)S(1)} collective-permute-done((bf16[448,128]{1,0:T(8,128)(2,1)S(1)}, bf16[448,128]{1,0:T(8,128)(2,1)S(1)}, u32[]{:S(2)}, u32[]{:S(2)}) %collective-permute-start.41) | collective-permute-done | bytes 114720 | tf_op jit(solution)/shard_map/ppermute | solution.py:381
  719.0 10.3 %maximum_convert_fusion = f32[2432,896]{1,0:T(8,128)} fusion(bf16[512,896]{1,0:T(8,128)(2,1)S(1)} %slice_bitcast_fusion.3, bf16[640,896]{1,0:T(8,128)(2,1)S(1)} %get-tuple-element.179, bf16[640,896]{1,0:T(8,128)(2,1)S(1)} %slice_bitcast_fusion.1, bf16[640,896]{1,0:T(8,128)(2,1)S(1)} %get-tuple-element.178), kind=kLoop, calls=%fused_computation.4 | loop fusion | flops 17432576 | bytes 13074432 | tf_op jit(solution)/shard_map/convert_element_type | solution.py:662
  738.7 4.1 convert_element_type.429
  743.3 4.1 convert_element_type.430
  (399 shorter events, 221.9 us)
Async XLA Ops:
  7.2 117.7 %all-gather.6.cloned.1.call-start = ((), (), s32[]{:S(2)}) async-start(), calls=%async_computation.2 | async-start | bytes 3538944 | tf_op jit(solution)/shard_map/all_gather | solution.py:421
  7.2 23.7 %collective-permute-start = (s32[12,64]{1,0:T(8,128)}, s32[12,64]{1,0:T(8,128)S(1)}, u32[]{:S(2)}, u32[]{:S(2)}) collective-permute-start(s32[12,64]{1,0:T(8,128)} %param.16), channel_id=1, source_target_pairs={{0,2},{2,0},{1,3},{3,1},{4,6},{6,4},{5,7},{7,5},{8,10},{10,8},{9,1... | collective-permute-start | bytes 9224 | tf_op jit(solution)/shard_map/ppermute | solution.py:33
  7.3 34.6 %collective-permute-start.4 = (bf16[12,64,896]{2,1,0:T(8,128)(2,1)}, bf16[12,64,896]{2,1,0:T(8,128)(2,1)}, u32[]{:S(2)}, u32[]{:S(2)}) collective-permute-start(bf16[12,64,896]{2,1,0:T(8,128)(2,1)} %param.15), channel_id=1, source_target_pairs={{0,2},{2,0},{1,3},{3,1},{4,6},{6,4},{5,7},{7,5},{8,10},{10,8},{9,1... | collective-permute-start | bytes 4128776 | tf_op jit(solution)/shard_map/ppermute | solution.py:33
  15.2 21.7 %collective-permute-start.5 = (bf16[1,464,576]{1,2,0:T(8,128)(2,1)}, bf16[1,464,576]{1,2,0:T(8,128)(2,1)}, u32[]{:S(2)}, u32[]{:S(2)}) collective-permute-start(bf16[1,464,576]{1,2,0:T(8,128)(2,1)} %copy.107), channel_id=1, source_target_pairs={{0,1},{1,0},{2,3},{3,2},{4,5},{5,4},{6,7},{7,6},{8,9},{9,8},{10,11... | collective-permute-start | bytes 1603592 | tf_op jit(solution)/shard_map/ppermute | solution.py:33
  53.8 584.5 %reduce-scatter.3.cloned.1.call-start = ((), (), s32[]{:S(2)}) async-start(), calls=%async_computation.3 | async-start | bytes 1769472 | tf_op jit(solution)/shard_map/reduce_scatter | solution.py:424
  53.9 45.6 %collective-permute-start.7 = (bf16[1,640,896]{2,1,0:T(8,128)(2,1)S(1)}, bf16[1,640,896]{2,1,0:T(8,128)(2,1)}, u32[]{:S(2)}, u32[]{:S(2)}) collective-permute-start(bf16[1,640,896]{2,1,0:T(8,128)(2,1)S(1)} %bitcast.183), channel_id=1, source_target_pairs={{0,1},{1,0},{2,3},{3,2},{4,5},{5,4},{6,7},{7,6},{8,9},{9,8},{10,11... | collective-permute-start | bytes 3440648 | tf_op jit(solution)/shard_map/ppermute | solution.py:33
  54.0 43.4 %collective-permute-start.6 = (bf16[1,448,896]{2,1,0:T(8,128)(2,1)S(1)}, bf16[1,448,896]{2,1,0:T(8,128)(2,1)}, u32[]{:S(2)}, u32[]{:S(2)}) collective-permute-start(bf16[1,448,896]{2,1,0:T(8,128)(2,1)S(1)} %bitcast.221), channel_id=1, source_target_pairs={{0,1},{1,0},{2,3},{3,2},{4,5},{5,4},{6,7},{7,6},{8,9},{9,8},{10,11... | collective-permute-start | bytes 2408456 | tf_op jit(solution)/shard_map/ppermute | solution.py:33
  55.4 66.5 %collective-permute-start.8 = (bf16[1,448,1280]{2,1,0:T(8,128)(2,1)}, bf16[1,448,1280]{2,1,0:T(8,128)(2,1)}, u32[]{:S(2)}, u32[]{:S(2)}) collective-permute-start(bf16[1,448,1280]{2,1,0:T(8,128)(2,1)} %bitcast.185), channel_id=1, source_target_pairs={{0,1},{1,0},{2,3},{3,2},{4,5},{5,4},{6,7},{7,6},{8,9},{9,8},{10,11... | collective-permute-start | bytes 3440648 | tf_op jit(solution)/shard_map/ppermute | solution.py:33
  65.6 80.9 %collective-permute-start.9 = (bf16[1,448,1280]{2,1,0:T(8,128)(2,1)S(1)}, bf16[1,448,1280]{2,1,0:T(8,128)(2,1)}, u32[]{:S(2)}, u32[]{:S(2)}) collective-permute-start(bf16[1,448,1280]{2,1,0:T(8,128)(2,1)S(1)} %bitcast.184), channel_id=1, source_target_pairs={{0,1},{1,0},{2,3},{3,2},{4,5},{5,4},{6,7},{7,6},{8,9},{9,8},{10,11... | collective-permute-start | bytes 3440648 | tf_op jit(solution)/shard_map/ppermute | solution.py:33
  124.9 60.9 %collective-permute-start.10 = (bf16[768,896]{1,0:T(8,128)(2,1)}, bf16[768,896]{1,0:T(8,128)(2,1)}, u32[]{:S(2)}, u32[]{:S(2)}) collective-permute-start(bf16[768,896]{1,0:T(8,128)(2,1)} %bitcast.33), channel_id=1, source_target_pairs={{0,4},{4,0},{1,5},{5,1},{2,6},{6,2},{3,7},{7,3},{8,12},{12,8},{9,1... | collective-permute-start | bytes 4128776 | tf_op jit(solution)/shard_map/ppermute | solution.py:33
  193.0 6.6 collective-permute-start.14
  199.5 43.7 %collective-permute-start.16 = (bf16[768,896]{1,0:T(8,128)(2,1)}, bf16[768,896]{1,0:T(8,128)(2,1)}, u32[]{:S(2)}, u32[]{:S(2)}) collective-permute-start(bf16[768,896]{1,0:T(8,128)(2,1)} %collective-permute-done.10), channel_id=1, source_target_pairs={{0,2},{2,0},{1,3},{3,1},{4,6},{6,4},{5,7},{7,5},{8,10},{10,8},{9,1... | collective-permute-start | bytes 4128776 | tf_op jit(solution)/shard_map/ppermute | solution.py:33
  202.7 33.2 %collective-permute-start.12 = (bf16[768,896]{1,0:T(8,128)(2,1)S(1)}, bf16[768,896]{1,0:T(8,128)(2,1)}, u32[]{:S(2)}, u32[]{:S(2)}) collective-permute-start(bf16[768,896]{1,0:T(8,128)(2,1)S(1)} %multiply_convert_fusion), channel_id=1, source_target_pairs={{0,4},{4,0},{1,5},{5,1},{2,6},{6,2},{3,7},{7,3},{8,12},{12,8},{9,1... | collective-permute-start | bytes 4128776 | tf_op jit(solution)/shard_map/ppermute | solution.py:33
  236.0 12.7 %collective-permute-start.15 = (bf16[768,896]{1,0:T(8,128)(2,1)}, bf16[768,896]{1,0:T(8,128)(2,1)}, u32[]{:S(2)}, u32[]{:S(2)}) collective-permute-start(bf16[768,896]{1,0:T(8,128)(2,1)} %collective-permute-done.12), channel_id=1, source_target_pairs={{0,2},{2,0},{1,3},{3,1},{4,6},{6,4},{5,7},{7,5},{8,10},{10,8},{9,1... | collective-permute-start | bytes 4128776 | tf_op jit(solution)/shard_map/ppermute | solution.py:33
  246.1 103.8 %collective-permute-start.20 = (bf16[768,896]{1,0:T(8,128)(2,1)}, bf16[768,896]{1,0:T(8,128)(2,1)S(1)}, u32[]{:S(2)}, u32[]{:S(2)}) collective-permute-start(bf16[768,896]{1,0:T(8,128)(2,1)} %slice.391), channel_id=1, source_target_pairs={{0,2},{2,0},{1,3},{3,1},{4,6},{6,4},{5,7},{7,5},{8,10},{10,8},{9,1... | collective-permute-start | bytes 4128776 | tf_op jit(solution)/shard_map/ppermute | solution.py:33
  295.4 32.6 %collective-permute-start.21 = (bf16[768,896]{1,0:T(8,128)(2,1)}, bf16[768,896]{1,0:T(8,128)(2,1)}, u32[]{:S(2)}, u32[]{:S(2)}) collective-permute-start(bf16[768,896]{1,0:T(8,128)(2,1)} %slice.393), channel_id=1, source_target_pairs={{0,2},{2,0},{1,3},{3,1},{4,6},{6,4},{5,7},{7,5},{8,10},{10,8},{9,1... | collective-permute-start | bytes 4128776 | tf_op jit(solution)/shard_map/ppermute | solution.py:33
  311.1 35.7 %collective-permute-start.19 = (bf16[448,1280]{1,0:T(8,128)(2,1)}, bf16[448,1280]{1,0:T(8,128)(2,1)}, u32[]{:S(2)}, u32[]{:S(2)}) collective-permute-start(bf16[448,1280]{1,0:T(8,128)(2,1)} %broadcast_select_fusion.3), channel_id=1, source_target_pairs={{0,1},{1,0},{2,3},{3,2},{4,5},{5,4},{6,7},{7,6},{8,9},{9,8},{10,11... | collective-permute-start | bytes 3440648 | tf_op jit(solution)/shard_map/ppermute | solution.py:33
  326.8 65.3 %collective-permute-start.18 = (bf16[448,1280]{1,0:T(8,128)(2,1)}, bf16[448,1280]{1,0:T(8,128)(2,1)}, u32[]{:S(2)}, u32[]{:S(2)}) collective-permute-start(bf16[448,1280]{1,0:T(8,128)(2,1)} %broadcast_select_fusion.4), channel_id=1, source_target_pairs={{0,1},{1,0},{2,3},{3,2},{4,5},{5,4},{6,7},{7,6},{8,9},{9,8},{10,11... | collective-permute-start | bytes 3440648 | tf_op jit(solution)/shard_map/ppermute | solution.py:33
  330.8 31.4 %collective-permute-start.22 = (bf16[768,896]{1,0:T(8,128)(2,1)}, bf16[768,896]{1,0:T(8,128)(2,1)}, u32[]{:S(2)}, u32[]{:S(2)}) collective-permute-start(bf16[768,896]{1,0:T(8,128)(2,1)} %add_convert_fusion.2), channel_id=1, source_target_pairs={{0,4},{4,0},{1,5},{5,1},{2,6},{6,2},{3,7},{7,3},{8,12},{12,8},{9,1... | collective-permute-start | bytes 4128776 | tf_op jit(solution)/shard_map/ppermute | solution.py:33
  346.8 40.5 %collective-permute-start.17 = (bf16[640,896]{1,0:T(8,128)(2,1)S(1)}, bf16[640,896]{1,0:T(8,128)(2,1)S(1)}, u32[]{:S(2)}, u32[]{:S(2)}) collective-permute-start(bf16[640,896]{1,0:T(8,128)(2,1)S(1)} %broadcast_select_fusion.5), channel_id=1, source_target_pairs={{0,1},{1,0},{2,3},{3,2},{4,5},{5,4},{6,7},{7,6},{8,9},{9,8},{10,11... | collective-permute-start | bytes 3440648 | tf_op jit(solution)/shard_map/ppermute | solution.py:33
  370.2 27.9 %collective-permute-start.23 = (bf16[768,896]{1,0:T(8,128)(2,1)}, bf16[768,896]{1,0:T(8,128)(2,1)}, u32[]{:S(2)}, u32[]{:S(2)}) collective-permute-start(bf16[768,896]{1,0:T(8,128)(2,1)} %get-tuple-element.134), channel_id=1, source_target_pairs={{0,2},{2,0},{1,3},{3,1},{4,6},{6,4},{5,7},{7,5},{8,10},{10,8},{9,1... | collective-permute-start | bytes 4128776 | tf_op jit(solution)/shard_map/ppermute | solution.py:33
  405.1 31.4 %collective-permute-start.24 = (bf16[336,1280]{1,0:T(8,128)(2,1)}, bf16[336,1280]{1,0:T(8,128)(2,1)}, u32[]{:S(2)}, u32[]{:S(2)}) collective-permute-start(bf16[336,1280]{1,0:T(8,128)(2,1)} %get-tuple-element.109), channel_id=1, source_target_pairs={{0,8},{1,9},{2,10},{3,11},{4,12},{5,13},{6,14},{7,15}} | collective-permute-start | bytes 2580488 | tf_op jit(solution)/shard_map/ppermute | solution.py:355
  409.3 27.2 %collective-permute-start.25 = (bf16[336,1280]{1,0:T(8,128)(2,1)}, bf16[336,1280]{1,0:T(8,128)(2,1)}, u32[]{:S(2)}, u32[]{:S(2)}) collective-permute-start(bf16[336,1280]{1,0:T(8,128)(2,1)} %get-tuple-element.110), channel_id=1, source_target_pairs={{24,16},{25,17},{26,18},{27,19},{28,20},{29,21},{30,22},{31,23}} | collective-permute-start | bytes 2580488 | tf_op jit(solution)/shard_map/ppermute | solution.py:355
  436.5 201.8 %reduce-scatter.5.cloned.1.call-start = ((), (), s32[]{:S(2)}) async-start(), calls=%async_computation.4 | async-start | bytes 1769472 | tf_op jit(solution)/shard_map/reduce_scatter | solution.py:424
  438.9 31.5 %collective-permute-start.29 = (bf16[336,1280]{1,0:T(8,128)(2,1)S(1)}, bf16[336,1280]{1,0:T(8,128)(2,1)}, u32[]{:S(2)}, u32[]{:S(2)}) collective-permute-start(bf16[336,1280]{1,0:T(8,128)(2,1)S(1)} %get-tuple-element.122), channel_id=1, source_target_pairs={{0,8},{8,16},{1,9},{9,17},{2,10},{10,18},{3,11},{11,19},{4,12},{12... | collective-permute-start | bytes 2580488 | tf_op jit(solution)/shard_map/ppermute | solution.py:355
  441.2 29.3 %collective-permute-start.30 = (bf16[336,1280]{1,0:T(8,128)(2,1)S(1)}, bf16[336,1280]{1,0:T(8,128)(2,1)}, u32[]{:S(2)}, u32[]{:S(2)}) collective-permute-start(bf16[336,1280]{1,0:T(8,128)(2,1)S(1)} %get-tuple-element.123), channel_id=1, source_target_pairs={{16,8},{24,16},{17,9},{25,17},{18,10},{26,18},{19,11},{27,19},{20,... | collective-permute-start | bytes 2580488 | tf_op jit(solution)/shard_map/ppermute | solution.py:355
  470.4 258.9 %all-gather.8.cloned.1.call-start = ((), (), s32[]{:S(2)}) async-start(), calls=%async_computation.5 | async-start | bytes 4874240 | tf_op jit(solution)/shard_map/all_gather | solution.py:665
  474.0 30.9 %collective-permute-start.44 = (bf16[336,1280]{1,0:T(8,128)(2,1)}, bf16[336,1280]{1,0:T(8,128)(2,1)}, u32[]{:S(2)}, u32[]{:S(2)}) collective-permute-start(bf16[336,1280]{1,0:T(8,128)(2,1)} %get-tuple-element.173), channel_id=1, source_target_pairs={{8,0},{16,8},{24,16},{9,1},{17,9},{25,17},{10,2},{18,10},{26,18},{... | collective-permute-start | bytes 2580488 | tf_op jit(solution)/shard_map/ppermute | solution.py:355
  475.3 31.4 %collective-permute-start.43 = (bf16[336,1280]{1,0:T(8,128)(2,1)}, bf16[336,1280]{1,0:T(8,128)(2,1)}, u32[]{:S(2)}, u32[]{:S(2)}) collective-permute-start(bf16[336,1280]{1,0:T(8,128)(2,1)} %get-tuple-element.172), channel_id=1, source_target_pairs={{0,8},{8,16},{16,24},{1,9},{9,17},{17,25},{2,10},{10,18},{18,26},{... | collective-permute-start | bytes 2580488 | tf_op jit(solution)/shard_map/ppermute | solution.py:355
  487.7 23.2 %collective-permute-start.32 = (bf16[448,896]{1,0:T(8,128)(2,1)S(1)}, bf16[448,896]{1,0:T(8,128)(2,1)}, u32[]{:S(2)}, u32[]{:S(2)}) collective-permute-start(bf16[448,896]{1,0:T(8,128)(2,1)S(1)} %fusion.14), channel_id=1, source_target_pairs={{0,2},{2,0},{1,3},{3,1},{4,6},{6,4},{5,7},{7,5},{8,10},{10,8},{9,1... | collective-permute-start | bytes 2408456 | tf_op jit(solution)/shard_map/ppermute | solution.py:33
  510.6 223.2 %all-gather.10.cloned.1.call-start = ((), (), s32[]{:S(2)}) async-start(), calls=%async_computation.6 | async-start | bytes 4874240 | tf_op jit(solution)/shard_map/all_gather | solution.py:665
  514.7 20.8 %collective-permute-start.27 = (bf16[768,896]{1,0:T(8,128)(2,1)}, bf16[768,896]{1,0:T(8,128)(2,1)}, u32[]{:S(2)}, u32[]{:S(2)}) collective-permute-start(bf16[768,896]{1,0:T(8,128)(2,1)} %slice.397), channel_id=1, source_target_pairs={{0,2},{2,0},{1,3},{3,1},{4,6},{6,4},{5,7},{7,5},{8,10},{10,8},{9,1... | collective-permute-start | bytes 4128776 | tf_op jit(solution)/shard_map/ppermute | solution.py:33
  527.3 29.7 %collective-permute-start.33 = (bf16[448,1344]{1,0:T(8,128)(2,1)}, bf16[448,1344]{1,0:T(8,128)(2,1)}, u32[]{:S(2)}, u32[]{:S(2)}) collective-permute-start(bf16[448,1344]{1,0:T(8,128)(2,1)} %broadcast_select_fusion.2), channel_id=1, source_target_pairs={{0,1},{1,0},{2,3},{3,2},{4,5},{5,4},{6,7},{7,6},{8,9},{9,8},{10,11... | collective-permute-start | bytes 3612680 | tf_op jit(solution)/shard_map/ppermute | solution.py:33
  530.0 71.6 %collective-permute-start.26 = (bf16[768,896]{1,0:T(8,128)(2,1)}, bf16[768,896]{1,0:T(8,128)(2,1)}, u32[]{:S(2)}, u32[]{:S(2)}) collective-permute-start(bf16[768,896]{1,0:T(8,128)(2,1)} %slice.395), channel_id=1, source_target_pairs={{0,2},{2,0},{1,3},{3,1},{4,6},{6,4},{5,7},{7,5},{8,10},{10,8},{9,1... | collective-permute-start | bytes 4128776 | tf_op jit(solution)/shard_map/ppermute | solution.py:33
  530.0 12.9 %collective-permute-start.45 = (bf16[112,1280]{1,0:T(8,128)(2,1)S(1)}, bf16[112,1280]{1,0:T(8,128)(2,1)S(1)}, u32[]{:S(2)}, u32[]{:S(2)}) collective-permute-start(bf16[112,1280]{1,0:T(8,128)(2,1)S(1)} %copy-done.45), channel_id=1, source_target_pairs={{0,8},{8,16},{16,24},{1,9},{9,17},{17,25},{2,10},{10,18},{18,26},{... | collective-permute-start | bytes 860168 | tf_op jit(solution)/shard_map/ppermute | solution.py:368
  534.2 11.0 %collective-permute-start.48 = (bf16[112,1280]{1,0:T(8,128)(2,1)S(1)}, bf16[112,1280]{1,0:T(8,128)(2,1)S(1)}, u32[]{:S(2)}, u32[]{:S(2)}) collective-permute-start(bf16[112,1280]{1,0:T(8,128)(2,1)S(1)} %copy-done.45), channel_id=1, source_target_pairs={{8,0},{16,8},{24,16},{9,1},{17,9},{25,17},{10,2},{18,10},{26,18},{... | collective-permute-start | bytes 860168 | tf_op jit(solution)/shard_map/ppermute | solution.py:369
  538.3 63.2 %collective-permute-start.28 = (bf16[768,896]{1,0:T(8,128)(2,1)}, bf16[768,896]{1,0:T(8,128)(2,1)}, u32[]{:S(2)}, u32[]{:S(2)}) collective-permute-start(bf16[768,896]{1,0:T(8,128)(2,1)} %add_convert_fusion.1), channel_id=1, source_target_pairs={{0,4},{4,0},{1,5},{5,1},{2,6},{6,2},{3,7},{7,3},{8,12},{12,8},{9,1... | collective-permute-start | bytes 4128776 | tf_op jit(solution)/shard_map/ppermute | solution.py:33
  542.9 15.8 %collective-permute-start.46 = (bf16[112,1280]{1,0:T(8,128)(2,1)S(1)}, bf16[112,1280]{1,0:T(8,128)(2,1)S(1)}, u32[]{:S(2)}, u32[]{:S(2)}) collective-permute-start(bf16[112,1280]{1,0:T(8,128)(2,1)S(1)} %collective-permute-done.45), channel_id=1, source_target_pairs={{8,16},{16,24},{9,17},{17,25},{10,18},{18,26},{11,19},{19,27},{12,... | collective-permute-start | bytes 860168 | tf_op jit(solution)/shard_map/ppermute | solution.py:368
  545.3 15.5 %collective-permute-start.49 = (bf16[112,1280]{1,0:T(8,128)(2,1)S(1)}, bf16[112,1280]{1,0:T(8,128)(2,1)S(1)}, u32[]{:S(2)}, u32[]{:S(2)}) collective-permute-start(bf16[112,1280]{1,0:T(8,128)(2,1)S(1)} %collective-permute-done.48), channel_id=1, source_target_pairs={{8,0},{16,8},{9,1},{17,9},{10,2},{18,10},{11,3},{19,11},{12,4},{20... | collective-permute-start | bytes 860168 | tf_op jit(solution)/shard_map/ppermute | solution.py:369
  560.8 31.3 %collective-permute-start.34 = (bf16[448,896]{1,0:T(8,128)(2,1)}, bf16[448,896]{1,0:T(8,128)(2,1)}, u32[]{:S(2)}, u32[]{:S(2)}) collective-permute-start(bf16[448,896]{1,0:T(8,128)(2,1)} %pad_maximum_fusion.19), channel_id=1, source_target_pairs={{0,4},{4,0},{1,5},{5,1},{2,6},{6,2},{3,7},{7,3},{8,12},{12,8},{9,1... | collective-permute-start | bytes 2408456 | tf_op jit(solution)/shard_map/ppermute | solution.py:381
  560.8 12.0 %collective-permute-start.50 = (bf16[112,1280]{1,0:T(8,128)(2,1)S(1)}, bf16[112,1280]{1,0:T(8,128)(2,1)S(1)}, u32[]{:S(2)}, u32[]{:S(2)}) collective-permute-start(bf16[112,1280]{1,0:T(8,128)(2,1)S(1)} %collective-permute-done.49), channel_id=1, source_target_pairs={{8,0},{9,1},{10,2},{11,3},{12,4},{13,5},{14,6},{15,7}} | collective-permute-start | bytes 860168 | tf_op jit(solution)/shard_map/ppermute | solution.py:369
  577.1 53.7 %collective-permute-start.51 = (bf16[640,896]{1,0:T(8,128)(2,1)}, bf16[640,896]{1,0:T(8,128)(2,1)}, u32[]{:S(2)}, u32[]{:S(2)}) collective-permute-start(bf16[640,896]{1,0:T(8,128)(2,1)} %reshape.429), channel_id=1, source_target_pairs={{0,4},{4,0},{1,5},{5,1},{2,6},{6,2},{3,7},{7,3},{8,12},{12,8},{9,1... | collective-permute-start | bytes 3440648 | tf_op jit(solution)/shard_map/ppermute | solution.py:33
  594.6 30.4 %collective-permute-start.35 = (bf16[448,896]{1,0:T(8,128)(2,1)}, bf16[448,896]{1,0:T(8,128)(2,1)S(1)}, u32[]{:S(2)}, u32[]{:S(2)}) collective-permute-start(bf16[448,896]{1,0:T(8,128)(2,1)} %add_convert_fusion.9), channel_id=1, source_target_pairs={{0,8},{8,0},{16,24},{24,16},{1,9},{9,1},{17,25},{25,17},{2,10},{10... | collective-permute-start | bytes 2408456 | tf_op jit(solution)/shard_map/ppermute | solution.py:381
  626.3 64.5 %collective-permute-start.36 = (bf16[448,896]{1,0:T(8,128)(2,1)S(1)}, bf16[448,896]{1,0:T(8,128)(2,1)S(1)}, u32[]{:S(2)}, u32[]{:S(2)}) collective-permute-start(bf16[448,896]{1,0:T(8,128)(2,1)S(1)} %add_convert_fusion.8), channel_id=1, source_target_pairs={{0,16},{8,24},{16,0},{24,8},{1,17},{9,25},{17,1},{25,9},{2,18},{10... | collective-permute-start | bytes 2408456 | tf_op jit(solution)/shard_map/ppermute | solution.py:381
  634.0 82.4 %collective-permute-start.52 = (bf16[2,640,896]{2,1,0:T(8,128)(2,1)}, bf16[2,640,896]{2,1,0:T(8,128)(2,1)}, u32[]{:S(2)}, u32[]{:S(2)}) collective-permute-start(bf16[2,640,896]{2,1,0:T(8,128)(2,1)} %pad_maximum_fusion.9), channel_id=1, source_target_pairs={{0,2},{2,0},{1,3},{3,1},{4,6},{6,4},{5,7},{7,5},{8,10},{10,8},{9,1... | collective-permute-start | bytes 6881288 | tf_op jit(solution)/shard_map/ppermute | solution.py:33
  649.2 47.2 %collective-permute-start.31 = (bf16[768,896]{1,0:T(8,128)(2,1)S(1)}, bf16[768,896]{1,0:T(8,128)(2,1)S(1)}, u32[]{:S(2)}, u32[]{:S(2)}) collective-permute-start(bf16[768,896]{1,0:T(8,128)(2,1)S(1)} %slice.467), channel_id=1, source_target_pairs={{0,2},{2,0},{1,3},{3,1},{4,6},{6,4},{5,7},{7,5},{8,10},{10,8},{9,1... | collective-permute-start | bytes 4128776 | tf_op jit(solution)/shard_map/ppermute | solution.py:33
  653.9 21.9 %collective-permute-start.40 = (bf16[448,128]{1,0:T(8,128)(2,1)S(1)}, bf16[448,128]{1,0:T(8,128)(2,1)S(1)}, u32[]{:S(2)}, u32[]{:S(2)}) collective-permute-start(bf16[448,128]{1,0:T(8,128)(2,1)S(1)} %add_convert_fusion.12), channel_id=1, source_target_pairs={{0,8},{8,0},{16,24},{24,16},{1,9},{9,1},{17,25},{25,17},{2,10},{10... | collective-permute-start | bytes 344072 | tf_op jit(solution)/shard_map/ppermute | solution.py:381
  675.9 13.1 %collective-permute-start.41 = (bf16[448,128]{1,0:T(8,128)(2,1)S(1)}, bf16[448,128]{1,0:T(8,128)(2,1)S(1)}, u32[]{:S(2)}, u32[]{:S(2)}) collective-permute-start(bf16[448,128]{1,0:T(8,128)(2,1)S(1)} %add_convert_fusion.11), channel_id=1, source_target_pairs={{0,16},{8,24},{16,0},{24,8},{1,17},{9,25},{17,1},{25,9},{2,18},{10... | collective-permute-start | bytes 344072 | tf_op jit(solution)/shard_map/ppermute | solution.py:381
  (80 other events, 539.8 us)
Sparse Core Ops, SparseCore 0:
  53.9 60.0 all-gather.5
  436.6 70.6 reduce-scatter.2
  511.7 68.2 reduce-scatter.4
  582.2 82.8 all-gather.7
  667.2 55.8 all-gather.9

commit v2 on v1

--- a/solution.py
+++ b/solution.py
@@ -274,7 +274,7 @@
     )(rows, grad, gate_w, up_w, down_w)
 
 
-def weight_grad_kernel(a_near, a_far, b_near, b_far, out_ref, acc_ref):
+def weight_grad_kernel(pair_ref, a_near, a_far, b_near, b_far, keep_ref, send_ref, acc_ref):
     step = pl.program_id(0)
     steps = pl.num_programs(0)
 
@@ -286,37 +286,117 @@
     def _():
         acc_ref[...] += dot(a_near[...], b_near[...], TN)
 
-    @pl.when(jnp.logical_and(step >= steps // 2, step < steps - 1))
+    @pl.when(step >= steps // 2)
     def _():
         acc_ref[...] += dot(a_far[...], b_far[...], TN)
 
     @pl.when(step == steps - 1)
     def _():
-        out_ref[...] = (acc_ref[...] + dot(a_far[...], b_far[...], TN)).astype(BF)
-
-
-def weight_grad(near, far):
+        outer, parts, tall, _ = keep_ref.shape
+        tiles = acc_ref.shape[1] // 128
+        high = tall // tiles
+        slab = parts * high
+        for out_ref, which in ((keep_ref, pair_ref[0]), (send_ref, 1 - pair_ref[0])):
+            for o in range(outer):
+                start = pl.multiple_of((2 * o + which) * slab, slab)
+                for t in range(tiles):
+                    tile = acc_ref[pl.ds(start, slab), t * 128 : (t + 1) * 128].astype(BF)
+                    for z in range(parts):
+                        out_ref[o, z, t * high : (t + 1) * high, :] = tile[
+                            z * high : (z + 1) * high
+                        ]
+
+
+def weight_grad(pair, outer, parts, near, far):
     (a_near, b_near), (a_far, b_far) = near, far
     count, high = a_near.shape
     wide = b_near.shape[1]
     half = 2
     step = count // half
-    near_block = lambda n: pl.BlockSpec((step, n), lambda i: (jnp.minimum(i, half - 1), 0))
-    far_block = lambda n: pl.BlockSpec((step, n), lambda i: (jnp.maximum(i - half, 0), 0))
+    tall = high // (2 * outer * parts) * (wide // 128)
+    near_block = lambda n: pl.BlockSpec((step, n), lambda i, p: (jnp.minimum(i, half - 1), 0))
+    far_block = lambda n: pl.BlockSpec((step, n), lambda i, p: (jnp.maximum(i - half, 0), 0))
+    out_spec = pl.BlockSpec((outer, parts, tall, 128), lambda i, p: (0, 0, 0, 0))
+    shape = jax.ShapeDtypeStruct((outer, parts, tall, 128), BF)
     return pl.pallas_call(
         weight_grad_kernel,
-        grid=(2 * half,),
-        in_specs=[near_block(high), far_block(high), near_block(wide), far_block(wide)],
-        out_specs=pl.BlockSpec((high, wide), lambda i: (0, 0)),
-        out_shape=jax.ShapeDtypeStruct((high, wide), BF),
-        scratch_shapes=[pltpu.VMEM((high, wide), F32)],
+        grid_spec=pltpu.PrefetchScalarGridSpec(
+            num_scalar_prefetch=1,
+            grid=(2 * half,),
+            in_specs=[near_block(high), far_block(high), near_block(wide), far_block(wide)],
+            out_specs=[out_spec, out_spec],
+            scratch_shapes=[pltpu.VMEM((high, wide), F32)],
+        ),
+        out_shape=[shape, shape],
         compiler_params=pltpu.CompilerParams(vmem_limit_bytes=VMEM),
         cost_estimate=pl.CostEstimate(
             flops=4 * count * high * wide,
             bytes_accessed=4 * count * (high + wide),
             transcendentals=0,
         ),
-    )(a_near, a_far, b_near, b_far)
+    )(pair, a_near, a_far, b_near, b_far)
+
+
+def spread_rows_kernel(skip, in_ref, out_ref):
+    parts, windows, _, tall, _ = in_ref.shape
+    tiles = out_ref.shape[1] // 128
+    high = tall // tiles
+    for q in range(windows):
+        drop = skip if q == windows - 1 else 0
+        for z in range(parts):
+            lo = max(drop - z * high, 0)
+            if lo >= high:
+                continue
+            at = q * parts * high + z * high + lo - drop
+            for t in range(tiles):
+                out_ref[at : at + high - lo, t * 128 : (t + 1) * 128] = in_ref[
+                    z, q, 0, t * high + lo : (t + 1) * high, :
+                ].astype(F32)
+
+
+def spread_rows(every, skip, part):
+    parts, windows, _, tall, _ = every.shape
+    width = tall * parts * 128 // ((part + skip) // windows)
+    return pl.pallas_call(
+        functools.partial(spread_rows_kernel, skip),
+        grid=(1,),
+        in_specs=[pl.BlockSpec((parts, windows, 1, tall, 128), lambda i: (0, 0, 0, 0, 0))],
+        out_specs=pl.BlockSpec((part, width), lambda i: (0, 0)),
+        out_shape=jax.ShapeDtypeStruct((part, width), F32),
+        compiler_params=pltpu.CompilerParams(vmem_limit_bytes=VMEM),
+    )(every)
+
+
+def spread_columns_kernel(owners, part, begins, skips, gate_ref, up_ref, gate_out, up_out):
+    high = gate_out.shape[0]
+    tiles = gate_ref.shape[3] // high // owners
+    for in_ref, out_ref in ((gate_ref, gate_out), (up_ref, up_out)):
+        for owner in range(owners):
+            for q in range(4):
+                for t in range(skips[q] // 128, tiles):
+                    at = owner * part + begins[q] + 128 * t
+                    row = (owner * tiles + t) * high
+                    out_ref[:, at : at + 128] = in_ref[0, q, 0, row : row + high, :].astype(F32)
+
+
+def spread_columns(every, owners, part, begins, skips):
+    parts, _, _, tall, _ = every.shape
+    window = part - begins[3]
+    high = tall * 128 // (owners * window)
+    block = (1, 4, 1, tall, 128)
+    out_spec = pl.BlockSpec((high, owners * part), lambda z: (z, 0))
+    shape = jax.ShapeDtypeStruct((parts * high, owners * part), F32)
+    return pl.pallas_call(
+        functools.partial(spread_columns_kernel, owners, part, begins, skips),
+        grid=(parts,),
+        in_specs=[
+            pl.BlockSpec(block, lambda z: (z, 0, 1, 0, 0)),
+            pl.BlockSpec(block, lambda z: (z, 0, 2, 0, 0)),
+        ],
+        out_specs=[out_spec, out_spec],
+        out_shape=[shape, shape],
+        compiler_params=pltpu.CompilerParams(vmem_limit_bytes=VMEM),
+    )(every, every)
 
 
 def gather_small(values, axis, size):
@@ -384,8 +464,8 @@
     return values
 
 
-def after(first, *rest):
-    return lax.optimization_barrier((first, *rest))[1:]
+def together(*values):
+    return lax.optimization_barrier(values)
 
 
 def make_body(sizes):
@@ -406,25 +486,48 @@
         both = jnp.stack(ordered("pair", values, swap(values, "pair")), axis=1)
         return both.reshape((owners * rows,) + values.shape[2:])
 
-    def sum_owners(values):
+    def gather_start(values):
+        if outer > 1:
+            values = lax.all_gather(values, "outer", axis=0)
+        else:
+            values = values[None]
+        return swap(values, "pair")
+
+    def gather_finish(values, far):
+        if outer > 1:
+            values = lax.all_gather(values, "outer", axis=0)
+        else:
+            values = values[None]
+        both = jnp.stack(ordered("pair", values, far), axis=1)
+        return both.reshape((owners * values.shape[1],) + values.shape[2:])
+
+    def gather_chips(values):
+        return lax.all_gather(values, CHIPS, axis=0)
+
+    def split_cy(values, axis):
+        half = values.shape[axis] // 2
+        first = lax.slice_in_dim(values, 0, half, axis=axis)
+        last = lax.slice_in_dim(values, half, 2 * half, axis=axis)
+        low = lax.axis_index("cy") == 0
+        return jnp.where(low, first, last), jnp.where(low, last, first)
+
+    def split_owners(values):
         split = values.reshape(outer, 2, -1, values.shape[1])
         if outer > 1:
             split = lax.psum_scatter(split, "outer", scatter_dimension=0)
         else:
             split = split[0]
         low = lax.axis_index("pair") == 0
-        keep = jnp.where(low, split[0], split[1])
-        send = jnp.where(low, split[1], split[0])
-        return (keep.astype(F32) + swap(send, "pair").astype(F32)).astype(BF)
-
-    def gather_chips(values):
-        return lax.all_gather(values, CHIPS, axis=0)
-
-    def scatter_chips(values):
-        return lax.psum_scatter(values, CHIPS, scatter_dimension=0)
-
-    def sum_chips(values):
-        return pair_sum(pair_sum(values, "cy", 2), "cz", cz)
+        return jnp.where(low, split[0], split[1]), jnp.where(low, split[1], split[0])
+
+    def add(left, right):
+        return (left.astype(F32) + right.astype(F32)).astype(left.dtype)
+
+    def bits_of(size):
+        return [1 << b for b in range((size - 1).bit_length())]
+
+    def exchange(values, axis, size, bit):
+        return lax.ppermute(values, axis, [(i, i ^ bit) for i in range(size)])
 
     def body(
         tokens,
@@ -458,6 +561,11 @@
         def heads_of(values, each):
             return jnp.where(core0, values[..., :each], values[..., each:])
 
+        places = jnp.stack([positions, swap(positions, "core")])
+        firsts = places[:, :, ::BLK]
+        starts = gather_small(gather_small(firsts, "cy", 2), "cz", cz)
+        starts = starts.transpose(3, 0, 1, 2, 4).reshape(seqs, -1)
+        qpos = places.transpose(1, 0, 2).reshape(seqs, 1, 2 * run)
         turned = Q_WIDTH + HEAD_DIM
         kv_rows = key_bias.shape[0]
         vectors = jnp.concatenate([query_bias, key_bias, value_bias, first_gain, second_gain])
@@ -500,8 +608,8 @@
         up_own = units(up_weight)
         down_own = by_quarter([down_weight[at : at + window] for at in begins])
         qkv_all = gather_rows(qkv_local)
-        qkv_all, gate_own, up_own, out_own, down_own = lax.optimization_barrier(
-            (qkv_all, gate_own, up_own, out_weight, down_own)
+        qkv_all, gate_own, up_own, out_own, down_own, starts, qpos = lax.optimization_barrier(
+            (qkv_all, gate_own, up_own, out_weight, down_own, starts, qpos)
         )
         qkv_all = qkv_all.reshape(owners, slab + 16, wide)
         qkv = qkv_all[:, :slab].reshape(owners * slab, wide)
@@ -518,17 +626,14 @@
         bias = jnp.concatenate(
             [heads_of(qb, Q_WIDTH), heads_of(kb, HEAD_DIM), heads_of(vb, HEAD_DIM)]
         ).astype(F32)[None]
-        out_full = gather_rows(out_own)
-        out_w = jnp.where(core0, out_full[:Q_WIDTH], out_full[Q_WIDTH:])
+        if outer > 1:
+            out_full = gather_rows(out_own)
+            out_w = jnp.where(core0, out_full[:Q_WIDTH], out_full[Q_WIDTH:])
+        else:
+            out_far = lax.ppermute(out_own, ("core", "pair"), [(0, 1), (3, 2)])
+            out_w = jnp.where(lax.axis_index("core") == pair, out_own, out_far)
         down_w = gather_rows(down_own)
-        gate_w = gather_rows(gate_own)
-        up_w = gather_rows(up_own)
-
-        places = jnp.stack([positions, swap(positions, "core")])
-        firsts = places[:, :, ::BLK]
-        starts = gather_small(gather_small(firsts, "cy", 2), "cz", cz)
-        starts = starts.transpose(3, 0, 1, 2, 4).reshape(seqs, -1)
-        qpos = places.transpose(1, 0, 2).reshape(seqs, 1, 2 * run)
+
         freq = theta ** (-jnp.arange(HALF, dtype=F32) / HALF)
         angles = places.reshape(2 * rows, 1).astype(F32) * freq
         cosine, sine = jnp.cos(angles), jnp.sin(angles)
@@ -548,14 +653,18 @@
         kv = kv.reshape(2, seqs, run, 2 * HEAD_DIM)
         cut = seqs // 2
         kv_all = gather_chips(kv)
-        kv_all, out_w, down_w, gate_w, cot_late = lax.optimization_barrier(
-            (kv_all, out_w, down_w, gate_w, cotangent)
-        )
+        gate_far = gather_start(gate_own)
+        kv_all, out_w, down_w, cot_late, up_own = together(
+            kv_all, out_w, down_w, cotangent, up_own
+        )
+        up_far = gather_start(up_own)
         grad_own = cot_late.reshape(rows, width)
         far_grad = swap(grad_own, "cy")
         attn, lse = attention(False, 0, seqs, starts, qpos, q, kv_all)
         attn_rows = attn.reshape(2 * rows, Q_WIDTH)
-        attn_rows, up_w, far_grad = lax.optimization_barrier((attn_rows, up_w, far_grad))
+        attn_rows, gate_far, up_far, far_grad = together(attn_rows, gate_far, up_far, far_grad)
+        gate_w = gather_finish(gate_own, gate_far)
+        up_w = gather_finish(up_own, up_far)
         attn_part = dot(attn_rows, out_w).astype(BF)
         inputs = own_rows.astype(F32)
         middle = (
@@ -570,70 +679,142 @@
         far_second = swap(second, "cy")
         near_s = jnp.concatenate([second, swap(second, "core")])
         near_h, near_g, near_u, near_mix, near_gs = mlp(near_s, near_c, gate_w, up_w, down_w)
-        far_second, near_h, near_g, near_u, near_mix, near_gs = lax.optimization_barrier(
-            (far_second, near_h, near_g, near_u, near_mix, near_gs)
-        )
-        far_s = jnp.concatenate([far_second, swap(far_second, "core")])
+        far_second, near_h, near_g, near_u, near_mix, near_gs = together(
+            far_second, near_h, near_g, near_u, near_mix, near_gs
+        )
+        far_core, gs_core = together(swap(far_second, "core"), swap(near_gs[rows:], "core"))
+        far_s = jnp.concatenate([far_second, far_core])
         far_h, far_g, far_u, far_mix, far_gs = mlp(far_s, far_c, gate_w, up_w, down_w)
-
-        def sum_back(near, far):
-            far_own = far[:rows].astype(F32) + swap(far[rows:], "core").astype(F32)
-            near_own = near[:rows].astype(F32) + swap(near[rows:], "core").astype(F32)
-            return near_own + swap(far_own.astype(BF), "cy").astype(F32)
-
-        grad_second = sum_back(near_gs, far_gs)
-        near_gs, far_gs, near_g, near_u, near_h = lax.optimization_barrier(
-            (near_gs, far_gs, near_g, near_u, near_h)
-        )
-        grad_down_w = weight_grad((near_h, near_c), (far_h, far_c))
-        grad_gate_w = weight_grad((near_s, near_g), (far_s, far_g))
-        grad_up_w = weight_grad((near_s, near_u), (far_s, far_u))
-        sums = [sum_owners(values) for values in (grad_down_w, grad_gate_w, grad_up_w)]
-        each = slab // cz
-        line = jnp.concatenate([v.reshape(cz, each, owners * window) for v in sums], axis=1)
-
+        own_gs = near_gs[:rows].astype(F32) + gs_core.astype(F32)
+        send_gs = add(far_gs[:rows], swap(far_gs[rows:], "core"))
+
+        send_gs, far_h, far_g, far_u, far_mix = together(send_gs, far_h, far_g, far_u, far_mix)
+        back_gs = swap(send_gs, "cy")
+        pair_index = jnp.reshape(pair, (1,)).astype(jnp.int32)
+
+        def unit_grad(near, far):
+            keep, send = weight_grad(pair_index, outer, cz, near, far)
+            if outer > 1:
+                keep = lax.psum_scatter(keep, "outer", scatter_dimension=0)
+                send = lax.psum_scatter(send, "outer", scatter_dimension=0)
+                return keep, send
+            return keep[0], send[0]
+
+        keep_down, send_down = unit_grad((near_h, near_c), (far_h, far_c))
+        keep_down, send_down, far_g, near_mix, far_mix = together(
+            keep_down, send_down, far_g, near_mix, far_mix
+        )
+        sum_down = swap(send_down, "pair")
+        mix_near_core = swap(near_mix[rows:], "core")
+        mix_far_core = swap(far_mix[rows:], "core")
+        keep_gate, send_gate = unit_grad((near_s, near_g), (far_s, far_g))
+        keep_gate, far_u = together(keep_gate, far_u)
+        keep_up, send_up = unit_grad((near_s, near_u), (far_s, far_u))
+        keep_up, back_gs, sum_down, mix_near_core, mix_far_core, send_gate, send_up = together(
+            keep_up, back_gs, sum_down, mix_near_core, mix_far_core, send_gate, send_up
+        )
+        sum_gate, sum_up = swap(send_gate, "pair"), swap(send_up, "pair")
+        send_mix = add(far_mix[:rows], mix_far_core)
+        back_mix = swap(send_mix, "cy")
+        grad_second = own_gs + back_gs.astype(F32)
         _, pull_second = jax.vjp(rms_scale, middle, sgain)
         grad_middle_part, grad_sgain = pull_second(grad_second)
         grad_middle = grad_own.astype(F32) + grad_middle_part
         grad_branch = grad_middle.astype(BF)
         grad_branch = jnp.concatenate([grad_branch, swap(grad_branch, "core")])
+        grad_attn = dot(grad_branch, out_w, NT).astype(BF).reshape(2, seqs, run, Q_WIDTH)
         grad_out_w = dot(attn_rows, grad_branch, TN).astype(BF)
-        grad_attn = dot(grad_branch, out_w, NT).astype(BF).reshape(2, seqs, run, Q_WIDTH)
-
         cos_t, sin_t = turned_rows(cosine), turned_rows(sine)
 
-        arrived = None
-        parts = []
-        for step in range(cz - 1):
-            loads = line_load(line, "cz", step, arrived)
-            if step < 2:
-                loads, grad_attn = lax.optimization_barrier((loads, grad_attn))
-                grad_q_part, grad_kv_part = attention(
-                    True,
-                    step * cut,
-                    seqs - cut if step else cut,
-                    starts,
-                    qpos,
-                    q,
-                    kv_all,
-                    grad_attn,
-                    lse,
-                    cos_t,
-                    sin_t,
-                )
-            arrived = line_send(loads, "cz", cz, step)
-            if step < 2:
-                grad_q_part, grad_kv_part, arrived = lax.optimization_barrier(
-                    (grad_q_part, grad_kv_part, arrived)
-                )
-                parts.append((grad_q_part, scatter_chips(grad_kv_part)))
-        (grad_q_near, grad_kv_near), (grad_q_far, grad_kv_far) = parts
-        grad_q_near, near_mix, far_mix = lax.optimization_barrier((grad_q_near, near_mix, far_mix))
-        mixed = (middle + sum_back(near_mix, far_mix)).astype(BF).reshape(seqs, run, width)
+        def attend_back(at, count, grad):
+            return attention(True, at, count, starts, qpos, q, kv_all, grad, lse, cos_t, sin_t)
+
+        def keys_cy(values):
+            return split_cy(values.reshape((cz, 2) + values.shape[1:]), 1)
+
+        grad_q_near, grad_kv_near = attend_back(0, cut, grad_attn)
+        grad_q_near, grad_kv_near, back_mix, sum_gate, sum_up = together(
+            grad_q_near, grad_kv_near, back_mix, sum_gate, sum_up
+        )
+        mix_own = near_mix[:rows].astype(F32) + mix_near_core.astype(F32)
+        mixed = (middle + mix_own + back_mix.astype(F32)).astype(BF).reshape(seqs, run, width)
+        line = jnp.concatenate(
+            [add(keep_down, sum_down), add(keep_gate, sum_gate), add(keep_up, sum_up)], axis=1
+        )
+        if outer > 1:
+            every_out = jnp.concatenate(ordered("core", grad_out_w, swap(grad_out_w, "core")))
+            keep_out, send_out = split_owners(every_out)
+            out_rows = add(keep_out, swap(send_out, "pair"))
+        else:
+            far_out = lax.ppermute(grad_out_w, ("core", "pair"), [(1, 0), (2, 3)])
+            out_rows = add(grad_out_w, far_out)
+            mine_here = lax.axis_index("core") == pair
+            out_rows = jnp.where(mine_here, out_rows, swap(out_rows, "core"))
+        out_rows = heads_of(out_rows, width // 2)
+
+        keep_near, send_near = keys_cy(grad_kv_near)
+        load = line_load(line, "cz", 0, None)
+        keep_out, send_out = split_cy(out_rows, 0)
+        load, send_near, grad_late, send_out = together(load, send_near, grad_attn, send_out)
+        far_out = swap(send_out, "cy")
+        arrived = line_send(load, "cz", cz, 0)
+        back_near = swap(send_near, "cy")
+        grad_q_far, grad_kv_far = attend_back(cut, seqs - cut, grad_late)
+        grad_q_far, grad_kv_far, arrived, back_near, far_out = together(
+            grad_q_far, grad_kv_far, arrived, back_near, far_out
+        )
+        out_sum = add(keep_out, far_out)
         grad_q = jnp.concatenate([grad_q_near, grad_q_far], axis=1).reshape(2 * rows, Q_WIDTH)
         grad_q_w = dot(first, grad_q, TN).astype(BF)
-        grad_kv = jnp.concatenate([grad_kv_near, grad_kv_far], axis=1)
-        grad_kv = grad_kv.reshape(2 * rows, 2 * HEAD_DIM).astype(F32)
+        keep_far, send_far = keys_cy(grad_kv_far)
+        keep_early, send_early = split_owners(grad_q_w)
+        bits = bits_of(cz)
+        load = line_load(line, "cz", 1, arrived)
+        load, send_far, out_sum = together(load, send_far, out_sum)
+        arrived, back_far, far_out = together(
+            line_send(load, "cz", cz, 1),
+            swap(send_far, "cy"),
+            exchange(out_sum, "cz", cz, bits[0]),
+        )
+        out_sum = add(out_sum, far_out)
+        keys = [add(keep_near, back_near), add(keep_far, back_far)]
+        keys = jnp.concatenate(keys, axis=3).reshape(cz, 2 * rows, 2 * HEAD_DIM)
+        load, keys_load = line_load(line, "cz", 2, arrived), line_load(keys, "cz", 0, None)
+        load, keys_load, send_early, out_sum = together(load, keys_load, send_early, out_sum)
+        arrived, keys_arrived, far_early, far_out = together(
+            line_send(load, "cz", cz, 2),
+            line_send(keys_load, "cz", cz, 0),
+            swap(send_early, "pair"),
+            exchange(out_sum, "cz", cz, bits[1]),
+        )
+        out_sum = add(out_sum, far_out)
+        for bit in bits[2:]:
+            out_sum = add(out_sum, exchange(out_sum, "cz", cz, bit))
+        for step in range(3, cz - 1):
+            arrived = line_send(line_load(line, "cz", step, arrived), "cz", cz, step)
+        mine = line_total(line, "cz", arrived)
+        early = add(keep_early, far_early)
+        keep_early, send_early = split_cy(early, 0)
+        keys_load = line_load(keys, "cz", 1, keys_arrived)
+        mine, keys_load, send_early, out_sum = together(mine, keys_load, send_early, out_sum)
+        keys_arrived, far_early, far_out = together(
+            line_send(keys_load, "cz", cz, 1), swap(send_early, "cy"), swap(out_sum, "cy")
+        )
+        out_sum = jnp.concatenate(ordered("cy", out_sum, far_out))
+        early = add(keep_early, far_early)
+        for step in range(2, cz - 1):
+            load = line_load(keys, "cz", step, keys_arrived)
+            if step == 2:
+                load, early, out_sum = together(load, early, out_sum)
+                keys_arrived, far_early, far_sum = together(
+                    line_send(load, "cz", cz, step),
+                    exchange(early, "cz", cz, bits[0]),
+                    swap(out_sum, "core"),
+                )
+                early = add(early, far_early)
+            else:
+                keys_arrived = line_send(load, "cz", cz, step)
+        grad_kv = line_total(keys, "cz", keys_arrived).astype(F32)
         front = grad_kv[:, :HALF]
         back = grad_kv[:, HALF:HEAD_DIM]
         grad_kv = jnp.concatenate(
@@ -644,56 +825,17 @@
         grad_kv_w = dot(first, grad_kv, TN).astype(BF)
         grad_biases = jnp.sum(grad_qkv.astype(F32), axis=0)
         grad_first_part = dot(grad_qkv, qkv, NT).astype(BF)
-        grad_first = grad_first_part[:rows].astype(F32) + swap(
-            grad_first_part[rows:], "core"
-        ).astype(F32)
+        keep_kv, send_kv = split_owners(grad_kv_w)
+        for bit in bits[2:]:
+            early = add(early, exchange(early, "cz", cz, bit))
+        send_first, send_kv = together(grad_first_part[rows:], send_kv)
+        far_early = exchange(early, "cz", cz, bits[1])
+        far_first, far_kv = together(swap(send_first, "core"), swap(send_kv, "pair"))
+        total_kv = add(keep_kv, far_kv)
+        grad_first = grad_first_part[:rows].astype(F32) + far_first.astype(F32)
         _, pull_first = jax.vjp(rms_scale, inputs, fgain)
         grad_input_part, grad_fgain = pull_first(grad_first)
         grad_tokens = (grad_middle + grad_input_part).reshape(seqs, run, width)
-
-        mine = line_total(line, "cz", arrived)
-        mine_down = line_gather(mine[:each], "cz", cz).reshape(window, width)
-        near, far = ordered("cy", mine_down, swap(mine_down, "cy"))
-        both = jnp.stack([near, far])
-        low, high = ordered("core", both, swap(both, "core"))
-        down_parts = [low[0], high[0], low[1], high[1]]
-        out_down = jnp.concatenate(
-            [w[n:] for w, n in zip(down_parts, skips) if n < window]
-        ).astype(F32)
-
-        def full_columns(values):
-            every = lax.all_gather(values, CHIPS + ("core",), axis=0)
-            every = every.reshape(cz, 4, each, owners * window)
-            pieces = [
-                every[:, q, :, owner * window + skips[q] : (owner + 1) * window]
-                for owner in range(owners)
-                for q in range(4)
-                if skips[q] < window
-            ]
-            return jnp.concatenate(pieces, axis=2).reshape(slab, ff).astype(F32)
-
-        out_gate = full_columns(mine[each : 2 * each])
-        out_up = full_columns(mine[2 * each :])
-
-        def own_rows_of(values):
-            return sum_chips(sum_owners(values))
-
-        def both_cores(values):
-            return [v.astype(F32) for v in ordered("core", values, swap(values, "core"))]
-
-        all_out = jnp.concatenate(ordered("core", grad_out_w, swap(grad_out_w, "core")))
-        early = sum_owners(jnp.concatenate([all_out, grad_q_w], axis=1))
-        early = jnp.concatenate(
-            [heads_of(early[:, :width], width // 2), early[:, width:]], axis=1
-        )
-        low_early, high_early = both_cores(sum_chips(early))
-        out_out = jnp.concatenate([low_early[:, : width // 2], high_early[:, : width // 2]], axis=1)
-        out_query = jnp.concatenate(
-            [low_early[:, width // 2 :], high_early[:, width // 2 :]], axis=1
-        )
-        low_kv, high_kv = both_cores(own_rows_of(grad_kv_w))
-        out_key = jnp.concatenate([low_kv[:, :HEAD_DIM], high_kv[:, :HEAD_DIM]], axis=1)
-        out_value = jnp.concatenate([low_kv[:, HEAD_DIM:], high_kv[:, HEAD_DIM:]], axis=1)
 
         zeros = jnp.zeros((), F32)
 
@@ -711,16 +853,66 @@
                 grad_sgain,
             ]
         )
-        vector = pair_sum(pair_sum(sum_chips(vector), "core", CORES), "pair", 2)
+        hops = [("cz", cz, bit) for bit in bits] + [("cy", 2, 1)]
+        for count, hop in enumerate(hops):
+            total_kv, vector = together(total_kv, vector)
+            last = count == len(hops) - 1
+            sends = [exchange(total_kv, *hop), exchange(vector, *hop)] + [far_early] * last
+            arrivals = together(*sends)
+            total_kv, vector = add(total_kv, arrivals[0]), vector + arrivals[1]
+            if last:
+                early = add(early, arrivals[2])
+        total_kv, vector = together(total_kv, vector)
+        far_kv, far_vector, far_early = together(
+            swap(total_kv, "core"), swap(vector, "core"), swap(early, "cy")
+        )
+        early = jnp.concatenate(ordered("cy", early, far_early))
+        far_early = swap(early, "core")
+        vector = vector + far_vector
+        vector = pair_sum(vector, "pair", 2)
         if outer > 1:
             vector = pair_sum(vector, "outer", outer)
+        out_query = jnp.concatenate(
+            ordered("core", early.astype(F32), far_early.astype(F32)), axis=1
+        )
+        out_out = jnp.concatenate(
+            ordered("core", out_sum.astype(F32), far_sum.astype(F32)), axis=1
+        )
+        low_kv, high_kv = ordered("core", total_kv.astype(F32), far_kv.astype(F32))
+        out_key = jnp.concatenate([low_kv[:, :HEAD_DIM], high_kv[:, :HEAD_DIM]], axis=1)
+        out_value = jnp.concatenate([low_kv[:, HEAD_DIM:], high_kv[:, HEAD_DIM:]], axis=1)
         owner = 2 * lax.axis_index("outer") + pair
         vectors = []
         at = 0
         for size in (width, KV_HEADS * HEAD_DIM, KV_HEADS * HEAD_DIM, width, width):
-            each = size // owners
-            vectors.append(lax.dynamic_slice(vector, (at + owner * each,), (each,)))
+            share = size // owners
+            vectors.append(lax.dynamic_slice(vector, (at + owner * share,), (share,)))
             at += size
+
+        every = lax.all_gather(mine, CHIPS + ("core",), axis=0)
+        every = every.reshape((cz, 4, 3, -1, 128))
+        if part % 128 == 0 and not any(skips[:3]):
+            out_down = spread_rows(every, skips[3], part)
+            out_gate, out_up = spread_columns(every, owners, part, begins, skips)
+        else:
+
+            def windows(index, q, high):
+                tiles = every[:, q, index].reshape(cz, -1, high // cz, 128)
+                return tiles.transpose(0, 2, 1, 3).reshape(high, -1).astype(F32)
+
+            out_down = jnp.concatenate(
+                [windows(0, q, window)[skips[q] :] for q in range(4)]
+            )
+
+            def full_columns(index):
+                pieces = [
+                    windows(index, q, slab)[:, owner * window + skips[q] : (owner + 1) * window]
+                    for owner in range(owners)
+                    for q in range(4)
+                ]
+                return jnp.concatenate(pieces, axis=1)
+
+            out_gate, out_up = full_columns(1), full_columns(2)
         return (
             mixed,
             grad_tokens,

time: 766 us -> 690 us (0.901)
  other arithmetic: 134 us -> 97.4 us
  waiting for transfers between devices: 224 us -> 188 us
  local copies, waits for them, and re-layouts: 79.2 us -> 47.4 us
  starting transfers between devices: 76.5 us -> 102 us
    ppermute x6 -> x12, waiting for transfers between devices: 15.9 us -> 129 us  [the longest x10 89.4 us: exchange(): return lax.ppermute(values, axis, [(i, i ^ bit) for i in range(size)])]
    ppermute x11 -> x1, waiting for transfers between devices: 74.6 us -> 0.01 us  [pair_sum(): other = lax.ppermute(values, axis, [(i, i ^ bit) for i in range(size)])]
    ppermute x32 -> x37, waiting for transfers between devices: 111 us -> 38.6 us  [swap(): return lax.ppermute(values, axis, SWAP)]
    all_gather x1, waiting for transfers between devices: 0.01 us -> 19 us  [gather_chips(): return lax.all_gather(values, CHIPS, axis=0)]
    convert_element_type x20 -> x21, other arithmetic: 41.9 us -> 23.9 us  [the longest x19 19.7 us: add(): return (left.astype(F32) + right.astype(F32)).astype(left.dtype)]
    pallas_call x3 -> x5, Pallas kernels: 39 us -> 56.2 us  [the longest x3 40 us: weight_grad(): pl.pallas_call(weight_grad_kernel, grid_spec=pltpu.PrefetchScalarGridSpec...]
    ppermute x3 -> x6, waiting for transfers between devices: 15.5 us -> 0.02 us  [line_send(): lax.ppermute(load[1], axis, left)]
    ppermute x32 -> x37, starting transfers between devices: 28.8 us -> 40.9 us  [swap(): return lax.ppermute(values, axis, SWAP)]
  transfers between devices with their start and end apart: 63 -> 67, of which waited for: 26 -> 20; matrix products, arithmetic and copies ran while one was open for 26% -> 15% of each run, Pallas kernels for 26% -> 21%
where the time goes in v2:
time: 690 us; the launch traced here: 680 us
  Pallas kernels  213 us (31%)
  waiting for transfers between devices  188 us (27%)
  starting transfers between devices  102 us (15%)
  other arithmetic  97.4 us (14%)
  local copies, waits for them, and re-layouts  47.4 us (7%)
  matrix products  16.8 us (2%)
  between operations  15.7 us (2%)
    ppermute x10, waiting for transfers between devices, exchange(): return lax.ppermute(values, axis, [(i, i ^ bit) for i in range(size)])  89.4 us
    pallas_call x3, Pallas kernels, attention(): pl.pallas_call(functools.partial(attend_back_kernel if back else attend_k...  87.5 us
    pallas_call x2, Pallas kernels, mlp(): pl.pallas_call(mlp_kernel, grid=(count // step,), in_specs=[row_block(wid...  60.7 us
    ppermute x37, starting transfers between devices, swap(): return lax.ppermute(values, axis, SWAP)  40.9 us
    pallas_call x3, Pallas kernels, weight_grad(): pl.pallas_call(weight_grad_kernel, grid_spec=pltpu.PrefetchScalarGridSpec...  40 us
    ppermute x37, waiting for transfers between devices, swap(): return lax.ppermute(values, axis, SWAP)  38.6 us
    ppermute x1, waiting for transfers between devices, body(): out_far = lax.ppermute(out_own, ('core', 'pair'), [(0, 1), (3, 2)])  34.3 us
    ppermute x6, starting transfers between devices, line_send(): lax.ppermute(load[0], axis, right)  25.2 us
  transfers between devices with their start and end apart: 67, of which 20 were waited for; matrix products, arithmetic and copies ran while one was open for 15% of the time, Pallas kernels for 21%

profile of v2, /device:TPU:1, one launch (start us, length us, event | category | flops | bytes accessed | tf_op | source)
XLA Modules:
  0.0 680.3 jit_solution(1937642574832783795)
XLA Ops:
  7.2 3.5 concatenate.142
  46.2 3.1 pad_maximum_fusion.1.x_ref
  49.3 8.7 %shard_map.254 = (bf16[1536,896]{1,0:T(8,128)(2,1)}, bf16[1536,448]{1,0:T(8,128)(2,1)}, bf16[1536,128]{1,0:T(8,128)(2,1)}) custom-call(bf16[1536,896]{1,0:T(8,128)(2,1)} %pad_maximum_fusion.1.x_ref, f32[1,896]{1,0:T(1,128)} %reshape.379.gain_ref, bf16[896,576]{1,0:T(8,128)(2,1)} %bitcast.154, f32[1,576]{1,0:T(1,128)} %maximum_convert_fusion.b_ref, ...), custom_call_target="tpu_custom_call" | custom-call | flops 1585446912 | bytes 5505024 | tf_op jit(solution)/shard_map/pallas_call | solution.py:69
  59.8 34.3 %collective-permute-done.6 = bf16[448,896]{1,0:T(8,128)(2,1)} collective-permute-done((bf16[448,896]{1,0:T(8,128)(2,1)S(1)}, bf16[448,896]{1,0:T(8,128)(2,1)}, u32[]{:S(2)}, u32[]{:S(2)}) %collective-permute-start.6) | collective-permute-done | bytes 802848 | tf_op jit(solution)/shard_map/ppermute | solution.py:633
  98.1 19.0 %all-gather.4.cloned.1.call-done.kv_ref = bf16[8,2,12,64,128]{4,3,2,1,0:T(8,128)(2,1)} async-done(((bf16[1,2,12,64,128]{4,3,2,1,0:T(8,128)(2,1)}), bf16[8,2,12,64,128]{4,3,2,1,0:T(8,128)(2,1)}) %all-gather.4.cloned.1.call-update) | async-done | bytes 3145744 | tf_op jit(solution)/shard_map/all_gather | solution.py:505
  119.5 35.9 %shard_map.255 = (bf16[2,12,64,448]{3,2,1,0:T(8,128)(2,1)}, f32[12,1,896]{2,1,0:T(1,128)}) custom-call(s32[12,32]{1,0:T(8,128)} %copy.63.starts_ref, s32[12,1,128]{2,1,0:T(1,128)} %reshape.359.qpos_ref, bf16[2,12,64,448]{3,2,1,0:T(8,128)(2,1)} %bitcast.166, bf16[8,2,12,64,128]{4,3,2,1,0:T(8,128)(2,1)} %all-gather.4.cloned.1.call-done.kv_ref), custom_call_target="tpu_custom_call" | custom-call | flops 11274289152 | bytes 6291456 | tf_op jit(solution)/shard_map/pallas_call | solution.py:212
  155.5 11.6 %collective-permute-done.9 = bf16[1,448,1280]{2,1,0:T(8,128)(2,1)} collective-permute-done((bf16[1,448,1280]{2,1,0:T(8,128)(2,1)S(1)}, bf16[1,448,1280]{2,1,0:T(8,128)(2,1)}, u32[]{:S(2)}, u32[]{:S(2)}) %collective-permute-start.9) | collective-permute-done | bytes 1146912 | tf_op jit(solution)/shard_map/ppermute | solution.py:33
  167.1 3.2 convolution_convert_fusion.1
  185.4 3.1 pad_maximum_fusion.3.c_ref.b_near
  191.5 30.3 %shard_map.256 = (bf16[1536,1280]{1,0:T(8,128)(2,1)}, bf16[1536,1280]{1,0:T(8,128)(2,1)}, bf16[1536,1280]{1,0:T(8,128)(2,1)}, bf16[1536,896]{1,0:T(8,128)(2,1)}, bf16[1536,896]{1,0:T(8,128)(2,1)}) custom-call(bf16[1536,896]{1,0:T(8,128)(2,1)} %pad_maximum_fusion.2.s_ref.a_near, bf16[1536,896]{1,0:T(8,128)(2,1)} %pad_maximum_fusion.3.c_ref.b_near, ...), custom_call_target="tpu_custom_call" | custom-call | flops 21139292160 | bytes 22806528 | tf_op jit(solution)/shard_map/pallas_call | solution.py:256
  230.0 30.4 %shard_map.257 = (bf16[1536,1280]{1,0:T(8,128)(2,1)}, bf16[1536,1280]{1,0:T(8,128)(2,1)}, bf16[1536,1280]{1,0:T(8,128)(2,1)}, bf16[1536,896]{1,0:T(8,128)(2,1)}, bf16[1536,896]{1,0:T(8,128)(2,1)}) custom-call(bf16[1536,896]{1,0:T(8,128)(2,1)} %constant_dynamic-update-slice_fusion.s_ref.a_far, bf16[1536,896]{1,0:T(8,128)(2,1)} %copy-done.49, ...), custom_call_target="tpu_custom_call" | custom-call | flops 21139292160 | bytes 22806528 | tf_op jit(solution)/shard_map/pallas_call | solution.py:256
  266.7 13.7 %shard_map.258 = (bf16[1,4,1120,128]{3,2,1,0:T(8,128)(2,1)}, bf16[1,4,1120,128]{3,2,1,0:T(8,128)(2,1)}) custom-call(s32[1]{0:T(128)} %bitcast.26.pair_ref, bf16[1536,1280]{1,0:T(8,128)(2,1)} %get-tuple-element.182.a_near, bf16[1536,1280]{1,0:T(8,128)(2,1)} %get-tuple-element.192.a_far, bf16[1536,896]{1,0:T(8,128)(2,1)} %pad_maximum_fusion.3.c_ref.b_near, ...), custom_call_target="tpu_custom_call" | custom-call | flops 7046430720 | bytes 13369344 | tf_op jit(solution)/shard_map/pallas_call | solution.py:321
  286.3 13.2 %shard_map.259 = (bf16[1,4,1120,128]{3,2,1,0:T(8,128)(2,1)}, bf16[1,4,1120,128]{3,2,1,0:T(8,128)(2,1)}) custom-call(s32[1]{0:T(128)} %bitcast.26.pair_ref, bf16[1536,896]{1,0:T(8,128)(2,1)} %pad_maximum_fusion.2.s_ref.a_near, bf16[1536,896]{1,0:T(8,128)(2,1)} %constant_dynamic-update-slice_fusion.s_ref.a_far, bf16[1536,1280]{1,0:T(8,128)(2,1)} %get-tuple-element.200.b_near, ...), custom_call_target="tpu_custom_call" | custom-call | flops 7046430720 | bytes 13369344 | tf_op jit(solution)/shard_map/pallas_call | solution.py:321
  299.4 13.1 %shard_map.260 = (bf16[1,4,1120,128]{3,2,1,0:T(8,128)(2,1)}, bf16[1,4,1120,128]{3,2,1,0:T(8,128)(2,1)}) custom-call(s32[1]{0:T(128)} %bitcast.26.pair_ref, bf16[1536,896]{1,0:T(8,128)(2,1)} %pad_maximum_fusion.2.s_ref.a_near, bf16[1536,896]{1,0:T(8,128)(2,1)} %constant_dynamic-update-slice_fusion.s_ref.a_far, bf16[1536,1280]{1,0:T(8,128)(2,1)} %get-tuple-element.199.b_near, ...), custom_call_target="tpu_custom_call" | custom-call | flops 7046430720 | bytes 13369344 | tf_op jit(solution)/shard_map/pallas_call | solution.py:321
  312.6 3.9 collective-permute-done.19
  316.5 3.0 multiply_reduce_fusion
  319.5 4.9 fusion.47
  327.2 3.3 add_convert_fusion.1
  334.8 3.4 fusion.14
  338.2 4.0 collective-permute-start.27
  342.3 4.5 convolution_convert_fusion.2
  349.3 25.7 %shard_map.261 = (bf16[2,6,64,448]{3,2,1,0:T(8,128)(2,1)}, bf16[8,2,6,64,128]{4,3,2,1,0:T(8,128)(2,1)}) custom-call(s32[12,32]{1,0:T(8,128)} %copy.63.starts_ref, s32[12,1,128]{2,1,0:T(1,128)} %reshape.359.qpos_ref, bf16[2,12,64,448]{3,2,1,0:T(8,128)(2,1)} %bitcast.167, bf16[8,2,12,64,128]{4,3,2,1,0:T(8,128)(2,1)} %all-gather.4.cloned.1.call-done.kv_ref, ...), custom_call_target="tpu_custom_call" | custom-call | flops 14092861440 | bytes 3145728 | tf_op jit(solution)/shard_map/pallas_call | solution.py:212
  375.0 7.1 %collective-permute-done.26 = bf16[4,1120,128]{2,1,0:T(8,128)(2,1)} collective-permute-done((bf16[4,1120,128]{2,1,0:T(8,128)(2,1)}, bf16[4,1120,128]{2,1,0:T(8,128)(2,1)}, u32[]{:S(2)}, u32[]{:S(2)}) %collective-permute-start.26) | collective-permute-done | bytes 1146912 | tf_op jit(solution)/shard_map/ppermute | solution.py:33
  385.4 4.9 collective-permute-done.27
  402.2 25.9 %shard_map.262 = (bf16[2,6,64,448]{3,2,1,0:T(8,128)(2,1)}, bf16[8,2,6,64,128]{4,3,2,1,0:T(8,128)(2,1)}) custom-call(s32[12,32]{1,0:T(8,128)} %copy.63.starts_ref, s32[12,1,128]{2,1,0:T(1,128)} %reshape.359.qpos_ref, bf16[2,12,64,448]{3,2,1,0:T(8,128)(2,1)} %bitcast.168, bf16[8,2,12,64,128]{4,3,2,1,0:T(8,128)(2,1)} %all-gather.4.cloned.1.call-done.kv_ref, ...), custom_call_target="tpu_custom_call" | custom-call | flops 14092861440 | bytes 3145728 | tf_op jit(solution)/shard_map/pallas_call | solution.py:212
  443.3 13.1 %collective-permute-done.36 = bf16[224,448]{1,0:T(8,128)(2,1)S(1)} collective-permute-done((bf16[224,448]{1,0:T(8,128)(2,1)S(1)}, bf16[224,448]{1,0:T(8,128)(2,1)S(1)}, u32[]{:S(2)}, u32[]{:S(2)}) %collective-permute-start.36) | collective-permute-done | bytes 200736 | tf_op jit(solution)/shard_map/ppermute | solution.py:530
  460.8 5.1 collective-permute-start.37
  467.2 3.0 collective-permute-start.42
  470.2 3.2 collective-permute-start.41
  473.4 3.5 collective-permute-start.39
  476.9 19.3 %collective-permute-done.42 = bf16[224,448]{1,0:T(8,128)(2,1)S(1)} collective-permute-done((bf16[224,448]{1,0:T(8,128)(2,1)S(1)}, bf16[224,448]{1,0:T(8,128)(2,1)S(1)}, u32[]{:S(2)}, u32[]{:S(2)}) %collective-permute-start.42) | collective-permute-done | bytes 200736 | tf_op jit(solution)/shard_map/ppermute | solution.py:530
  510.4 3.6 collective-permute-done.45
  514.1 3.1 collective-permute-done.46
  517.6 5.0 collective-permute-start.50
  522.6 11.0 %collective-permute-start.47 = (bf16[1536,128]{1,0:T(8,128)(2,1)S(1)}, bf16[1536,128]{1,0:T(8,128)(2,1)S(1)}, u32[]{:S(2)}, u32[]{:S(2)}) collective-permute-start(bf16[1536,128]{1,0:T(8,128)(2,1)S(1)} %get-tuple-element.271), channel_id=1, source_target_pairs={{0,8},{8,16},{16,24},{1,9},{9,17},{17,25},{2,10},{10,18},{18,26},{... | collective-permute-start | bytes 1179656 | tf_op jit(solution)/shard_map/ppermute | solution.py:435
  534.9 4.0 collective-permute-start.49
  539.4 32.7 %collective-permute-done.49 = bf16[224,448]{1,0:T(8,128)(2,1)S(1)} collective-permute-done((bf16[224,448]{1,0:T(8,128)(2,1)S(1)}, bf16[224,448]{1,0:T(8,128)(2,1)S(1)}, u32[]{:S(2)}, u32[]{:S(2)}) %collective-permute-start.49) | collective-permute-done | bytes 200736 | tf_op jit(solution)/shard_map/ppermute | solution.py:530
  572.5 3.9 fusion.21
  586.5 4.0 add_convert_fusion
  591.0 4.0 collective-permute-start.52
  604.0 9.0 %collective-permute-done.54 = f32[2944]{0:T(1024)S(1)} collective-permute-done((f32[2944]{0:T(1024)S(1)}, f32[2944]{0:T(1024)S(1)}, u32[]{:S(2)}, u32[]{:S(2)}) %collective-permute-start.54) | collective-permute-done | bytes 11808 | tf_op jit(solution)/shard_map/ppermute | solution.py:530
  613.0 3.6 collective-permute-start.55
  618.2 12.6 %collective-permute-done.56 = f32[2944]{0:T(1024)S(1)} collective-permute-done((f32[2944]{0:T(1024)S(1)}, f32[2944]{0:T(1024)S(1)}, u32[]{:S(2)}, u32[]{:S(2)}) %collective-permute-start.56) | collective-permute-done | bytes 11808 | tf_op jit(solution)/shard_map/ppermute | solution.py:530
  635.1 4.0 collective-permute-start.60
  641.4 3.9 fusion.1
  647.5 3.3 collective-permute-start.64
  656.8 9.8 %shard_map.263 = (f32[448,4864]{1,0:T(8,128)}, f32[448,4864]{1,0:T(8,128)}) custom-call(bf16[4,4,3,1120,128]{4,3,2,1,0:T(8,128)(2,1)} %bitcast.122, bf16[4,4,3,1120,128]{4,3,2,1,0:T(8,128)(2,1)} %bitcast.123), custom_call_target="tpu_custom_call" | custom-call | tf_op jit(solution)/shard_map/pallas_call | solution.py:389
  666.6 6.4 shard_map.264
  (385 shorter events, 179.9 us)
Async XLA Ops:
  7.2 109.9 %all-gather.4.cloned.1.call-start = ((), (), s32[]{:S(2)}) async-start(), calls=%async_computation | async-start | bytes 3538944 | tf_op jit(solution)/shard_map/all_gather | solution.py:505
  14.8 25.0 %collective-permute-start = (bf16[1,464,576]{1,2,0:T(8,128)(2,1)}, bf16[1,464,576]{1,2,0:T(8,128)(2,1)}, u32[]{:S(2)}, u32[]{:S(2)}) collective-permute-start(bf16[1,464,576]{1,2,0:T(8,128)(2,1)} %copy.56), channel_id=1, source_target_pairs={{0,1},{1,0},{2,3},{3,2},{4,5},{5,4},{6,7},{7,6},{8,9},{9,8},{10,11... | collective-permute-start | bytes 1603592 | tf_op jit(solution)/shard_map/ppermute | solution.py:33
  16.8 10.2 %collective-permute-start.1 = (s32[12,64]{1,0:T(8,128)S(1)}, s32[12,64]{1,0:T(8,128)S(1)}, u32[]{:S(2)}, u32[]{:S(2)}) collective-permute-start(s32[12,64]{1,0:T(8,128)S(1)} %copy-done.61), channel_id=1, source_target_pairs={{0,2},{2,0},{1,3},{3,1},{4,6},{6,4},{5,7},{7,5},{8,10},{10,8},{9,1... | collective-permute-start | bytes 9224 | tf_op jit(solution)/shard_map/ppermute | solution.py:33
  17.8 28.4 %collective-permute-start.5 = (bf16[12,64,896]{2,1,0:T(8,128)(2,1)S(1)}, bf16[12,64,896]{2,1,0:T(8,128)(2,1)}, u32[]{:S(2)}, u32[]{:S(2)}) collective-permute-start(bf16[12,64,896]{2,1,0:T(8,128)(2,1)S(1)} %copy-done), channel_id=1, source_target_pairs={{0,2},{2,0},{1,3},{3,1},{4,6},{6,4},{5,7},{7,5},{8,10},{10,8},{9,1... | collective-permute-start | bytes 4128776 | tf_op jit(solution)/shard_map/ppermute | solution.py:33
  58.0 598.8 %all-gather.6.cloned.1.call-start = ((), (), s32[]{:S(2)}) async-start(), calls=%async_computation.1 | async-start | bytes 14622720 | tf_op jit(solution)/shard_map/all_gather | solution.py:892
  58.0 38.2 %collective-permute-start.7 = (bf16[1,640,896]{2,1,0:T(8,128)(2,1)S(1)}, bf16[1,640,896]{2,1,0:T(8,128)(2,1)S(1)}, u32[]{:S(2)}, u32[]{:S(2)}) collective-permute-start(bf16[1,640,896]{2,1,0:T(8,128)(2,1)S(1)} %bitcast.141), channel_id=1, source_target_pairs={{0,1},{1,0},{2,3},{3,2},{4,5},{5,4},{6,7},{7,6},{8,9},{9,8},{10,11... | collective-permute-start | bytes 3440648 | tf_op jit(solution)/shard_map/ppermute | solution.py:33
  58.3 35.7 %collective-permute-start.6 = (bf16[448,896]{1,0:T(8,128)(2,1)S(1)}, bf16[448,896]{1,0:T(8,128)(2,1)}, u32[]{:S(2)}, u32[]{:S(2)}) collective-permute-start(bf16[448,896]{1,0:T(8,128)(2,1)S(1)} %copy-done.44), channel_id=1, source_target_pairs={{0,1},{3,2},{4,5},{7,6},{8,9},{11,10},{12,13},{15,14},{16,17},{19,... | collective-permute-start | bytes 2408456 | tf_op jit(solution)/shard_map/ppermute | solution.py:633
  117.1 49.9 %collective-permute-start.10 = (bf16[768,896]{1,0:T(8,128)(2,1)}, bf16[768,896]{1,0:T(8,128)(2,1)}, u32[]{:S(2)}, u32[]{:S(2)}) collective-permute-start(bf16[768,896]{1,0:T(8,128)(2,1)} %bitcast.25), channel_id=1, source_target_pairs={{0,4},{4,0},{1,5},{5,1},{2,6},{6,2},{3,7},{7,3},{8,12},{12,8},{9,1... | collective-permute-start | bytes 4128776 | tf_op jit(solution)/shard_map/ppermute | solution.py:33
  117.4 38.1 %collective-permute-start.8 = (bf16[1,448,1280]{2,1,0:T(8,128)(2,1)S(1)}, bf16[1,448,1280]{2,1,0:T(8,128)(2,1)S(1)}, u32[]{:S(2)}, u32[]{:S(2)}) collective-permute-start(bf16[1,448,1280]{2,1,0:T(8,128)(2,1)S(1)} %bitcast.142), channel_id=1, source_target_pairs={{0,1},{1,0},{2,3},{3,2},{4,5},{5,4},{6,7},{7,6},{8,9},{9,8},{10,11... | collective-permute-start | bytes 3440648 | tf_op jit(solution)/shard_map/ppermute | solution.py:33
  118.6 48.5 %collective-permute-start.9 = (bf16[1,448,1280]{2,1,0:T(8,128)(2,1)S(1)}, bf16[1,448,1280]{2,1,0:T(8,128)(2,1)}, u32[]{:S(2)}, u32[]{:S(2)}) collective-permute-start(bf16[1,448,1280]{2,1,0:T(8,128)(2,1)S(1)} %bitcast.143), channel_id=1, source_target_pairs={{0,1},{1,0},{2,3},{3,2},{4,5},{5,4},{6,7},{7,6},{8,9},{9,8},{10,11... | collective-permute-start | bytes 3440648 | tf_op jit(solution)/shard_map/ppermute | solution.py:33
  174.8 10.6 %collective-permute-start.14 = (bf16[768,896]{1,0:T(8,128)(2,1)}, bf16[768,896]{1,0:T(8,128)(2,1)S(1)}, u32[]{:S(2)}, u32[]{:S(2)}) collective-permute-start(bf16[768,896]{1,0:T(8,128)(2,1)} %bitcast.25), channel_id=1, source_target_pairs={{0,2},{2,0},{1,3},{3,1},{4,6},{6,4},{5,7},{7,5},{8,10},{10,8},{9,1... | collective-permute-start | bytes 4128776 | tf_op jit(solution)/shard_map/ppermute | solution.py:33
  174.8 50.5 %collective-permute-start.17 = (bf16[768,896]{1,0:T(8,128)(2,1)}, bf16[768,896]{1,0:T(8,128)(2,1)}, u32[]{:S(2)}, u32[]{:S(2)}) collective-permute-start(bf16[768,896]{1,0:T(8,128)(2,1)} %collective-permute-done.10), channel_id=1, source_target_pairs={{0,2},{2,0},{1,3},{3,1},{4,6},{6,4},{5,7},{7,5},{8,10},{10,8},{9,1... | collective-permute-start | bytes 4128776 | tf_op jit(solution)/shard_map/ppermute | solution.py:33
  188.5 33.3 %collective-permute-start.12 = (bf16[768,896]{1,0:T(8,128)(2,1)S(1)}, bf16[768,896]{1,0:T(8,128)(2,1)S(1)}, u32[]{:S(2)}, u32[]{:S(2)}) collective-permute-start(bf16[768,896]{1,0:T(8,128)(2,1)S(1)} %multiply_convert_fusion), channel_id=1, source_target_pairs={{0,4},{4,0},{1,5},{5,1},{2,6},{6,2},{3,7},{7,3},{8,12},{12,8},{9,1... | collective-permute-start | bytes 4128776 | tf_op jit(solution)/shard_map/ppermute | solution.py:33
  283.1 29.5 %collective-permute-start.21 = (bf16[768,896]{1,0:T(8,128)(2,1)}, bf16[768,896]{1,0:T(8,128)(2,1)}, u32[]{:S(2)}, u32[]{:S(2)}) collective-permute-start(bf16[768,896]{1,0:T(8,128)(2,1)} %slice.286), channel_id=1, source_target_pairs={{0,2},{2,0},{1,3},{3,1},{4,6},{6,4},{5,7},{7,5},{8,10},{10,8},{9,1... | collective-permute-start | bytes 4128776 | tf_op jit(solution)/shard_map/ppermute | solution.py:33
  284.7 27.9 %collective-permute-start.22 = (bf16[768,896]{1,0:T(8,128)(2,1)}, bf16[768,896]{1,0:T(8,128)(2,1)}, u32[]{:S(2)}, u32[]{:S(2)}) collective-permute-start(bf16[768,896]{1,0:T(8,128)(2,1)} %slice.287), channel_id=1, source_target_pairs={{0,2},{2,0},{1,3},{3,1},{4,6},{6,4},{5,7},{7,5},{8,10},{10,8},{9,1... | collective-permute-start | bytes 4128776 | tf_op jit(solution)/shard_map/ppermute | solution.py:33
  284.8 31.7 %collective-permute-start.19 = (bf16[768,896]{1,0:T(8,128)(2,1)}, bf16[768,896]{1,0:T(8,128)(2,1)}, u32[]{:S(2)}, u32[]{:S(2)}) collective-permute-start(bf16[768,896]{1,0:T(8,128)(2,1)} %add_convert_fusion.2), channel_id=1, source_target_pairs={{0,4},{4,0},{1,5},{5,1},{2,6},{6,2},{3,7},{7,3},{8,12},{12,8},{9,1... | collective-permute-start | bytes 4128776 | tf_op jit(solution)/shard_map/ppermute | solution.py:33
  285.1 27.5 %collective-permute-start.20 = (bf16[4,1120,128]{2,1,0:T(8,128)(2,1)}, bf16[4,1120,128]{2,1,0:T(8,128)(2,1)}, u32[]{:S(2)}, u32[]{:S(2)}) collective-permute-start(bf16[4,1120,128]{2,1,0:T(8,128)(2,1)} %bitcast.34), channel_id=1, source_target_pairs={{0,1},{1,0},{2,3},{3,2},{4,5},{5,4},{6,7},{7,6},{8,9},{9,8},{10,11... | collective-permute-start | bytes 3440648 | tf_op jit(solution)/shard_map/ppermute | solution.py:33
  324.4 10.4 %collective-permute-start.23 = (bf16[768,896]{1,0:T(8,128)(2,1)}, bf16[768,896]{1,0:T(8,128)(2,1)}, u32[]{:S(2)}, u32[]{:S(2)}) collective-permute-start(bf16[768,896]{1,0:T(8,128)(2,1)} %get-tuple-element.310), channel_id=1, source_target_pairs={{0,2},{2,0},{1,3},{3,1},{4,6},{6,4},{5,7},{7,5},{8,10},{10,8},{9,1... | collective-permute-start | bytes 4128776 | tf_op jit(solution)/shard_map/ppermute | solution.py:33
  330.4 51.7 %collective-permute-start.24 = (bf16[768,896]{1,0:T(8,128)(2,1)}, bf16[768,896]{1,0:T(8,128)(2,1)}, u32[]{:S(2)}, u32[]{:S(2)}) collective-permute-start(bf16[768,896]{1,0:T(8,128)(2,1)} %add_convert_fusion.1), channel_id=1, source_target_pairs={{0,4},{4,0},{1,5},{5,1},{2,6},{6,2},{3,7},{7,3},{8,12},{12,8},{9,1... | collective-permute-start | bytes 4128776 | tf_op jit(solution)/shard_map/ppermute | solution.py:33
  330.7 44.3 %collective-permute-start.25 = (bf16[4,1120,128]{2,1,0:T(8,128)(2,1)}, bf16[4,1120,128]{2,1,0:T(8,128)(2,1)}, u32[]{:S(2)}, u32[]{:S(2)}) collective-permute-start(bf16[4,1120,128]{2,1,0:T(8,128)(2,1)} %bitcast.37), channel_id=1, source_target_pairs={{0,1},{1,0},{2,3},{3,2},{4,5},{5,4},{6,7},{7,6},{8,9},{9,8},{10,11... | collective-permute-start | bytes 3440648 | tf_op jit(solution)/shard_map/ppermute | solution.py:33
  331.9 50.3 %collective-permute-start.26 = (bf16[4,1120,128]{2,1,0:T(8,128)(2,1)}, bf16[4,1120,128]{2,1,0:T(8,128)(2,1)}, u32[]{:S(2)}, u32[]{:S(2)}) collective-permute-start(bf16[4,1120,128]{2,1,0:T(8,128)(2,1)} %bitcast.38), channel_id=1, source_target_pairs={{0,1},{1,0},{2,3},{3,2},{4,5},{5,4},{6,7},{7,6},{8,9},{9,8},{10,11... | collective-permute-start | bytes 3440648 | tf_op jit(solution)/shard_map/ppermute | solution.py:33
  338.2 52.2 %collective-permute-start.27 = (bf16[448,896]{1,0:T(8,128)(2,1)S(1)}, bf16[448,896]{1,0:T(8,128)(2,1)}, u32[]{:S(2)}, u32[]{:S(2)}) collective-permute-start(bf16[448,896]{1,0:T(8,128)(2,1)S(1)} %fusion.14), channel_id=1, source_target_pairs={{1,0},{2,3},{5,4},{6,7},{9,8},{10,11},{13,12},{14,15},{17,16},{18,... | collective-permute-start | bytes 2408456 | tf_op jit(solution)/shard_map/ppermute | solution.py:749
  396.3 31.7 %collective-permute-start.29 = (bf16[3360,128]{1,0:T(8,128)(2,1)}, bf16[3360,128]{1,0:T(8,128)(2,1)S(1)}, u32[]{:S(2)}, u32[]{:S(2)}) collective-permute-start(bf16[3360,128]{1,0:T(8,128)(2,1)} %get-tuple-element.232), channel_id=1, source_target_pairs={{0,8},{1,9},{2,10},{3,11},{4,12},{5,13},{6,14},{7,15}} | collective-permute-start | bytes 2580488 | tf_op jit(solution)/shard_map/ppermute | solution.py:435
  399.1 29.0 %collective-permute-start.30 = (bf16[3360,128]{1,0:T(8,128)(2,1)}, bf16[3360,128]{1,0:T(8,128)(2,1)}, u32[]{:S(2)}, u32[]{:S(2)}) collective-permute-start(bf16[3360,128]{1,0:T(8,128)(2,1)} %get-tuple-element.233), channel_id=1, source_target_pairs={{24,16},{25,17},{26,18},{27,19},{28,20},{29,21},{30,22},{31,23}} | collective-permute-start | bytes 2580488 | tf_op jit(solution)/shard_map/ppermute | solution.py:435
  400.7 27.3 %collective-permute-start.31 = (bf16[4,1,2,6,64,128]{5,4,3,2,1,0:T(8,128)(2,1)S(1)}, bf16[4,1,2,6,64,128]{5,4,3,2,1,0:T(8,128)(2,1)}, u32[]{:S(2)}, u32[]{:S(2)}) collective-permute-start(bf16[4,1,2,6,64,128]{5,4,3,2,1,0:T(8,128)(2,1)S(1)} %broadcast_select_fusion.3), channel_id=1, source_target_pairs={{0,4},{4,0},{1,5},{5,1},{2,6},{6,2},{3,7},{7,3},{8,12},{12,8},{9,1... | collective-permute-start | bytes 2359304 | tf_op jit(solution)/shard_map/ppermute | solution.py:33
  401.9 26.1 %collective-permute-start.32 = (bf16[224,448]{1,0:T(8,128)(2,1)}, bf16[224,448]{1,0:T(8,128)(2,1)}, u32[]{:S(2)}, u32[]{:S(2)}) collective-permute-start(bf16[224,448]{1,0:T(8,128)(2,1)} %broadcast_select_fusion.10), channel_id=1, source_target_pairs={{0,4},{4,0},{1,5},{5,1},{2,6},{6,2},{3,7},{7,3},{8,12},{12,8},{9,1... | collective-permute-start | bytes 602120 | tf_op jit(solution)/shard_map/ppermute | solution.py:33
  433.3 23.1 %collective-permute-start.33 = (bf16[3360,128]{1,0:T(8,128)(2,1)S(1)}, bf16[3360,128]{1,0:T(8,128)(2,1)S(1)}, u32[]{:S(2)}, u32[]{:S(2)}) collective-permute-start(bf16[3360,128]{1,0:T(8,128)(2,1)S(1)} %get-tuple-element.242), channel_id=1, source_target_pairs={{0,8},{8,16},{1,9},{9,17},{2,10},{10,18},{3,11},{11,19},{4,12},{12... | collective-permute-start | bytes 2580488 | tf_op jit(solution)/shard_map/ppermute | solution.py:435
  434.8 21.6 %collective-permute-start.34 = (bf16[3360,128]{1,0:T(8,128)(2,1)S(1)}, bf16[3360,128]{1,0:T(8,128)(2,1)S(1)}, u32[]{:S(2)}, u32[]{:S(2)}) collective-permute-start(bf16[3360,128]{1,0:T(8,128)(2,1)S(1)} %get-tuple-element.243), channel_id=1, source_target_pairs={{16,8},{24,16},{17,9},{25,17},{18,10},{26,18},{19,11},{27,19},{20,... | collective-permute-start | bytes 2580488 | tf_op jit(solution)/shard_map/ppermute | solution.py:435
  435.5 20.9 %collective-permute-start.35 = (bf16[4,1,2,6,64,128]{5,4,3,2,1,0:T(8,128)(2,1)S(1)}, bf16[4,1,2,6,64,128]{5,4,3,2,1,0:T(8,128)(2,1)S(1)}, u32[]{:S(2)}, u32[]{:S(2)}) collective-permute-start(bf16[4,1,2,6,64,128]{5,4,3,2,1,0:T(8,128)(2,1)S(1)} %broadcast_select_fusion.2), channel_id=1, source_target_pairs={{0,4},{4,0},{1,5},{5,1},{2,6},{6,2},{3,7},{7,3},{8,12},{12,8},{9,1... | collective-permute-start | bytes 2359304 | tf_op jit(solution)/shard_map/ppermute | solution.py:33
  436.8 19.7 %collective-permute-start.36 = (bf16[224,448]{1,0:T(8,128)(2,1)S(1)}, bf16[224,448]{1,0:T(8,128)(2,1)S(1)}, u32[]{:S(2)}, u32[]{:S(2)}) collective-permute-start(bf16[224,448]{1,0:T(8,128)(2,1)S(1)} %add_convert_fusion.15), channel_id=1, source_target_pairs={{0,8},{8,0},{16,24},{24,16},{1,9},{9,1},{17,25},{25,17},{2,10},{10... | collective-permute-start | bytes 602120 | tf_op jit(solution)/shard_map/ppermute | solution.py:530
  460.8 37.5 %collective-permute-start.37 = (bf16[3360,128]{1,0:T(8,128)(2,1)}, bf16[3360,128]{1,0:T(8,128)(2,1)}, u32[]{:S(2)}, u32[]{:S(2)}) collective-permute-start(bf16[3360,128]{1,0:T(8,128)(2,1)} %get-tuple-element.251), channel_id=1, source_target_pairs={{0,8},{8,16},{16,24},{1,9},{9,17},{17,25},{2,10},{10,18},{18,26},{... | collective-permute-start | bytes 2580488 | tf_op jit(solution)/shard_map/ppermute | solution.py:435
  465.9 32.4 %collective-permute-start.38 = (bf16[3360,128]{1,0:T(8,128)(2,1)}, bf16[3360,128]{1,0:T(8,128)(2,1)}, u32[]{:S(2)}, u32[]{:S(2)}) collective-permute-start(bf16[3360,128]{1,0:T(8,128)(2,1)} %get-tuple-element.252), channel_id=1, source_target_pairs={{8,0},{16,8},{24,16},{9,1},{17,9},{25,17},{10,2},{18,10},{26,18},{... | collective-permute-start | bytes 2580488 | tf_op jit(solution)/shard_map/ppermute | solution.py:435
  467.2 29.0 %collective-permute-start.42 = (bf16[224,448]{1,0:T(8,128)(2,1)S(1)}, bf16[224,448]{1,0:T(8,128)(2,1)S(1)}, u32[]{:S(2)}, u32[]{:S(2)}) collective-permute-start(bf16[224,448]{1,0:T(8,128)(2,1)S(1)} %add_convert_fusion.14), channel_id=1, source_target_pairs={{0,16},{8,24},{16,0},{24,8},{1,17},{9,25},{17,1},{25,9},{2,18},{10... | collective-permute-start | bytes 602120 | tf_op jit(solution)/shard_map/ppermute | solution.py:530
  470.2 28.1 %collective-permute-start.41 = (bf16[448,448]{1,0:T(8,128)(2,1)S(1)}, bf16[448,448]{1,0:T(8,128)(2,1)}, u32[]{:S(2)}, u32[]{:S(2)}) collective-permute-start(bf16[448,448]{1,0:T(8,128)(2,1)S(1)} %broadcast_select_fusion.4), channel_id=1, source_target_pairs={{0,1},{1,0},{2,3},{3,2},{4,5},{5,4},{6,7},{7,6},{8,9},{9,8},{10,11... | collective-permute-start | bytes 1204232 | tf_op jit(solution)/shard_map/ppermute | solution.py:33
  473.4 24.9 %collective-permute-start.39 = (bf16[1536,128]{1,0:T(8,128)(2,1)}, bf16[1536,128]{1,0:T(8,128)(2,1)}, u32[]{:S(2)}, u32[]{:S(2)}) collective-permute-start(bf16[1536,128]{1,0:T(8,128)(2,1)} %get-tuple-element.253), channel_id=1, source_target_pairs={{0,8},{1,9},{2,10},{3,11},{4,12},{5,13},{6,14},{7,15}} | collective-permute-start | bytes 1179656 | tf_op jit(solution)/shard_map/ppermute | solution.py:435
  506.8 10.4 %collective-permute-start.43 = (bf16[1536,128]{1,0:T(8,128)(2,1)}, bf16[1536,128]{1,0:T(8,128)(2,1)S(1)}, u32[]{:S(2)}, u32[]{:S(2)}) collective-permute-start(bf16[1536,128]{1,0:T(8,128)(2,1)} %get-tuple-element.263), channel_id=1, source_target_pairs={{0,8},{8,16},{1,9},{9,17},{2,10},{10,18},{3,11},{11,19},{4,12},{12... | collective-permute-start | bytes 1179656 | tf_op jit(solution)/shard_map/ppermute | solution.py:435
  508.2 9.0 %collective-permute-start.44 = (bf16[1536,128]{1,0:T(8,128)(2,1)}, bf16[1536,128]{1,0:T(8,128)(2,1)S(1)}, u32[]{:S(2)}, u32[]{:S(2)}) collective-permute-start(bf16[1536,128]{1,0:T(8,128)(2,1)} %get-tuple-element.264), channel_id=1, source_target_pairs={{16,8},{24,16},{17,9},{25,17},{18,10},{26,18},{19,11},{27,19},{20,... | collective-permute-start | bytes 1179656 | tf_op jit(solution)/shard_map/ppermute | solution.py:435
  517.6 54.4 %collective-permute-start.50 = (bf16[448,448]{1,0:T(8,128)(2,1)S(1)}, bf16[448,448]{1,0:T(8,128)(2,1)S(1)}, u32[]{:S(2)}, u32[]{:S(2)}) collective-permute-start(bf16[448,448]{1,0:T(8,128)(2,1)S(1)} %pad_maximum_fusion.20), channel_id=1, source_target_pairs={{0,2},{2,0},{1,3},{3,1},{4,6},{6,4},{5,7},{7,5},{8,10},{10,8},{9,1... | collective-permute-start | bytes 1204232 | tf_op jit(solution)/shard_map/ppermute | solution.py:33
  522.6 49.4 %collective-permute-start.47 = (bf16[1536,128]{1,0:T(8,128)(2,1)S(1)}, bf16[1536,128]{1,0:T(8,128)(2,1)S(1)}, u32[]{:S(2)}, u32[]{:S(2)}) collective-permute-start(bf16[1536,128]{1,0:T(8,128)(2,1)S(1)} %get-tuple-element.271), channel_id=1, source_target_pairs={{0,8},{8,16},{16,24},{1,9},{9,17},{17,25},{2,10},{10,18},{18,26},{... | collective-permute-start | bytes 1179656 | tf_op jit(solution)/shard_map/ppermute | solution.py:435
  533.6 38.4 %collective-permute-start.48 = (bf16[1536,128]{1,0:T(8,128)(2,1)S(1)}, bf16[1536,128]{1,0:T(8,128)(2,1)S(1)}, u32[]{:S(2)}, u32[]{:S(2)}) collective-permute-start(bf16[1536,128]{1,0:T(8,128)(2,1)S(1)} %get-tuple-element.272), channel_id=1, source_target_pairs={{8,0},{16,8},{24,16},{9,1},{17,9},{25,17},{10,2},{18,10},{26,18},{... | collective-permute-start | bytes 1179656 | tf_op jit(solution)/shard_map/ppermute | solution.py:435
  534.9 37.1 %collective-permute-start.49 = (bf16[224,448]{1,0:T(8,128)(2,1)S(1)}, bf16[224,448]{1,0:T(8,128)(2,1)S(1)}, u32[]{:S(2)}, u32[]{:S(2)}) collective-permute-start(bf16[224,448]{1,0:T(8,128)(2,1)S(1)} %add_convert_fusion.12), channel_id=1, source_target_pairs={{0,8},{8,0},{16,24},{24,16},{1,9},{9,1},{17,25},{25,17},{2,10},{10... | collective-permute-start | bytes 602120 | tf_op jit(solution)/shard_map/ppermute | solution.py:530
  584.5 14.0 %collective-permute-start.51 = (bf16[768,896]{1,0:T(8,128)(2,1)}, bf16[768,896]{1,0:T(8,128)(2,1)}, u32[]{:S(2)}, u32[]{:S(2)}) collective-permute-start(bf16[768,896]{1,0:T(8,128)(2,1)} %slice.344), channel_id=1, source_target_pairs={{0,2},{2,0},{1,3},{3,1},{4,6},{6,4},{5,7},{7,5},{8,10},{10,8},{9,1... | collective-permute-start | bytes 4128776 | tf_op jit(solution)/shard_map/ppermute | solution.py:33
  590.6 41.8 %collective-permute-start.59 = (bf16[224,448]{1,0:T(8,128)(2,1)S(1)}, bf16[224,448]{1,0:T(8,128)(2,1)}, u32[]{:S(2)}, u32[]{:S(2)}) collective-permute-start(bf16[224,448]{1,0:T(8,128)(2,1)S(1)} %add_convert_fusion.11), channel_id=1, source_target_pairs={{0,16},{8,24},{16,0},{24,8},{1,17},{9,25},{17,1},{25,9},{2,18},{10... | collective-permute-start | bytes 602120 | tf_op jit(solution)/shard_map/ppermute | solution.py:530
  602.2 10.8 %collective-permute-start.53 = (bf16[448,128]{1,0:T(8,128)(2,1)S(1)}, bf16[448,128]{1,0:T(8,128)(2,1)S(1)}, u32[]{:S(2)}, u32[]{:S(2)}) collective-permute-start(bf16[448,128]{1,0:T(8,128)(2,1)S(1)} %add_convert_fusion.19), channel_id=1, source_target_pairs={{0,8},{8,0},{16,24},{24,16},{1,9},{9,1},{17,25},{25,17},{2,10},{10... | collective-permute-start | bytes 344072 | tf_op jit(solution)/shard_map/ppermute | solution.py:530
  602.2 10.7 %collective-permute-start.54 = (f32[2944]{0:T(1024)S(1)}, f32[2944]{0:T(1024)S(1)}, u32[]{:S(2)}, u32[]{:S(2)}) collective-permute-start(f32[2944]{0:T(1024)S(1)} %concatenate.175), channel_id=1, source_target_pairs={{0,8},{8,0},{16,24},{24,16},{1,9},{9,1},{17,25},{25,17},{2,10},{10... | collective-permute-start | bytes 35336 | tf_op jit(solution)/shard_map/ppermute | solution.py:530
  613.0 17.7 %collective-permute-start.55 = (bf16[448,128]{1,0:T(8,128)(2,1)S(1)}, bf16[448,128]{1,0:T(8,128)(2,1)S(1)}, u32[]{:S(2)}, u32[]{:S(2)}) collective-permute-start(bf16[448,128]{1,0:T(8,128)(2,1)S(1)} %add_convert_fusion.18), channel_id=1, source_target_pairs={{0,16},{8,24},{16,0},{24,8},{1,17},{9,25},{17,1},{25,9},{2,18},{10... | collective-permute-start | bytes 344072 | tf_op jit(solution)/shard_map/ppermute | solution.py:530
  616.6 14.1 %collective-permute-start.56 = (f32[2944]{0:T(1024)S(1)}, f32[2944]{0:T(1024)S(1)}, u32[]{:S(2)}, u32[]{:S(2)}) collective-permute-start(f32[2944]{0:T(1024)S(1)} %add.281), channel_id=1, source_target_pairs={{0,16},{8,24},{16,0},{24,8},{1,17},{9,25},{17,1},{25,9},{2,18},{10... | collective-permute-start | bytes 35336 | tf_op jit(solution)/shard_map/ppermute | solution.py:530
  635.1 10.2 %collective-permute-start.60 = (bf16[448,128]{1,0:T(8,128)(2,1)S(1)}, bf16[448,128]{1,0:T(8,128)(2,1)S(1)}, u32[]{:S(2)}, u32[]{:S(2)}) collective-permute-start(bf16[448,128]{1,0:T(8,128)(2,1)S(1)} %add_convert_fusion.16), channel_id=1, source_target_pairs={{0,2},{2,0},{1,3},{3,1},{4,6},{6,4},{5,7},{7,5},{8,10},{10,8},{9,1... | collective-permute-start | bytes 344072 | tf_op jit(solution)/shard_map/ppermute | solution.py:33
  (88 other events, 1077.9 us)
Sparse Core Ops, SparseCore 0:
  58.1 58.9 all-gather.3
  506.9 146.8 all-gather.5

commit v3 on v2

--- a/solution.py
+++ b/solution.py
@@ -96,45 +96,96 @@
     )
 
 
-def fill_bias(offset, starts_ref, qpos_ref, bias_ref):
-    own = qpos_ref[0]
-    inside = lax.broadcasted_iota(jnp.int32, (BLK, own.shape[1]), 0)
+def run_order(starts_ref, seq, index):
+    one, two = starts_ref[seq, 2 * index], starts_ref[seq, 2 * index + 1]
+    late = jnp.where(one > two, BLK, 0)
+    low = pl.multiple_of(late, BLK)
+    high = pl.multiple_of(BLK - late, BLK)
+    return low, high, jnp.minimum(one, two), jnp.maximum(one, two)
+
+
+def load_rows(own_ref, seq, ref):
+    lows, highs = [], []
+    for i in range(2):
+        low, high, _, _ = run_order(own_ref, seq, i)
+        lows.append(ref[i, 0, pl.ds(low, BLK), :])
+        highs.append(ref[i, 0, pl.ds(high, BLK), :])
+    return [stack_heads(jnp.concatenate(rows, axis=0)) for rows in (lows, highs)]
+
+
+def store_rows(own_ref, seq, ref, lows, highs):
+    for i in range(2):
+        low, high, _, _ = run_order(own_ref, seq, i)
+        ref[i, 0, pl.ds(low, BLK), :] = lows[i * BLK : (i + 1) * BLK].astype(BF)
+        ref[i, 0, pl.ds(high, BLK), :] = highs[i * BLK : (i + 1) * BLK].astype(BF)
+
+
+def load_keys(starts_ref, own_ref, seq, kv_ref, keys_ref, low_ref, high_ref):
+    half = keys_ref.shape[0] // 2
+    wide = low_ref.shape[1]
+    lane = lax.broadcasted_iota(jnp.int32, (1, wide), 1) % (2 * BLK)
+    inside = lax.broadcasted_iota(jnp.int32, (BLK, wide), 0)
+    _, _, low_a, high_a = run_order(own_ref, seq, 0)
+    _, _, low_b, high_b = run_order(own_ref, seq, 1)
+    low_pos = jnp.where(lane < BLK, low_a, low_b) + lane % BLK
+    high_pos = jnp.where(lane < BLK, high_a, high_b) + lane % BLK
+    for r in range(half // BLK):
+        low, high, low_start, high_start = run_order(starts_ref, seq, r)
+        at = r * BLK
+        keys_ref[at : at + BLK, :] = kv_ref[r // 2, r % 2, 0, pl.ds(low, BLK), :]
+        keys_ref[half + at : half + at + BLK, :] = kv_ref[r // 2, r % 2, 0, pl.ds(high, BLK), :]
+        low_ref[at : at + BLK, :] = jnp.where(inside + low_start <= low_pos, 0.0, -1e30)
+        high_ref[at : at + BLK, :] = jnp.where(inside + high_start <= high_pos, 0.0, -1e30)
+
+
+def query_chunks():
+    total = GROUP * 2 * BLK
+    return [(lo, min(lo + 256, total)) for lo in range(0, total, 256)]
+
+
+def head_slices(values):
+    return [values[:, at : at + 2 * BLK] for at in range(0, values.shape[1], 2 * BLK)]
+
+
+def attend_kernel(
+    offset, starts_ref, own_ref, q_ref, kv_ref, o_ref, lse_ref, keys_ref, low_ref, high_ref
+):
     seq = pl.program_id(0) + offset
-    for j in range(bias_ref.shape[0] // BLK):
-        far = inside + starts_ref[seq, j]
-        bias_ref[j * BLK : (j + 1) * BLK, :] = jnp.where(far <= own, 0.0, -1e30)
-
-
-def query_chunks(local):
-    total = GROUP * local
-    return [(lo, min(lo + 2 * local, total)) for lo in range(0, total, 2 * local)]
-
-
-def attend_kernel(offset, starts_ref, qpos_ref, q_ref, kv_ref, o_ref, lse_ref, bias_ref):
-    local = 2 * q_ref.shape[2]
-    keys = bias_ref.shape[0]
-    fill_bias(offset, starts_ref, qpos_ref, bias_ref)
-    kv = kv_ref[...].reshape(keys, 2 * HEAD_DIM)
-    key = kv[:, :HEAD_DIM]
+    half = keys_ref.shape[0] // 2
+    load_keys(starts_ref, own_ref, seq, kv_ref, keys_ref, low_ref, high_ref)
+    kv = keys_ref[...]
+    key_low, key_high = kv[:half, :HEAD_DIM], kv[half:, :HEAD_DIM]
     value_t = kv.astype(F32).T[HEAD_DIM:].astype(BF)
-    query = stack_heads(q_ref[...].reshape(local, Q_WIDTH))
-    heads = []
-    for lo, hi in query_chunks(local):
-        bias = jnp.concatenate([bias_ref[...]] * ((hi - lo) // local), axis=1)
-        scores = dot(key, query[lo:hi], NT) + bias
+    value_low, value_high = value_t[:, :half], value_t[:, half:]
+    query_low, query_high = load_rows(own_ref, seq, q_ref)
+    lows, highs = [], []
+    for lo, hi in query_chunks():
+        scores = dot(key_low, query_low[lo:hi], NT) + low_ref[:, : hi - lo]
         top = jnp.max(scores, axis=0, keepdims=True)
         expo = jnp.exp(scores - top)
         total = jnp.sum(expo, axis=0, keepdims=True)
-        out = dot(value_t, expo.astype(BF)) / total
-        lse_ref[0, :, lo:hi] = top + jnp.log(total)
-        heads += [out[:, at : at + local].T for at in range(0, hi - lo, local)]
-    o_ref[...] = jnp.concatenate(heads, axis=1).astype(BF).reshape(o_ref.shape)
+        out = dot(value_low, expo.astype(BF)) / total
+        lse_ref[0, 0:1, lo:hi] = top + jnp.log(total)
+        lows += [part.T for part in head_slices(out)]
+        first = dot(key_low, query_high[lo:hi], NT)
+        second = dot(key_high, query_high[lo:hi], NT) + high_ref[:, : hi - lo]
+        top = jnp.maximum(
+            jnp.max(first, axis=0, keepdims=True), jnp.max(second, axis=0, keepdims=True)
+        )
+        first, second = jnp.exp(first - top), jnp.exp(second - top)
+        total = jnp.sum(first, axis=0, keepdims=True) + jnp.sum(second, axis=0, keepdims=True)
+        out = (dot(value_low, first.astype(BF)) + dot(value_high, second.astype(BF))) / total
+        lse_ref[0, 1:2, lo:hi] = top + jnp.log(total)
+        highs += [part.T for part in head_slices(out)]
+    store_rows(
+        own_ref, seq, o_ref, jnp.concatenate(lows, axis=1), jnp.concatenate(highs, axis=1)
+    )
 
 
 def attend_back_kernel(
     offset,
     starts_ref,
-    qpos_ref,
+    own_ref,
     q_ref,
     kv_ref,
     do_ref,
@@ -143,76 +194,133 @@
     sin_ref,
     dq_ref,
     dkv_ref,
-    bias_ref,
+    keys_ref,
+    low_ref,
+    high_ref,
     probs_ref,
     grads_ref,
 ):
-    local = 2 * q_ref.shape[2]
-    keys = bias_ref.shape[0]
-    fill_bias(offset, starts_ref, qpos_ref, bias_ref)
-    kv = kv_ref[...].reshape(keys, 2 * HEAD_DIM)
-    key = kv[:, :HEAD_DIM]
-    value = kv[:, HEAD_DIM:]
+    seq = pl.program_id(0) + offset
+    half = keys_ref.shape[0] // 2
+    wide = probs_ref.shape[1] // 2
+    total = GROUP * 2 * BLK
+    load_keys(starts_ref, own_ref, seq, kv_ref, keys_ref, low_ref, high_ref)
+    kv = keys_ref[...]
+    key_low, key_high = kv[:half, :HEAD_DIM], kv[half:, :HEAD_DIM]
+    value_low, value_high = kv[:half, HEAD_DIM:], kv[half:, HEAD_DIM:]
     key_t = kv.astype(F32).T[:HEAD_DIM].astype(BF)
-    query = stack_heads(q_ref[...].reshape(local, Q_WIDTH))
-    grad_o = stack_heads(do_ref[...].reshape(local, Q_WIDTH))
-    cosine = cos_ref[0]
-    sine = sin_ref[0]
-    heads = []
-    for lo, hi in query_chunks(local):
-        bias = jnp.concatenate([bias_ref[...]] * ((hi - lo) // local), axis=1)
-        scores = dot(key, query[lo:hi], NT) + bias
-        probs = jnp.exp(scores - lse_ref[0, :, lo:hi])
-        probs_ref[:, lo:hi] = probs.astype(BF)
-        grad_p = dot(value, grad_o[lo:hi], NT)
+    query_low, query_high = load_rows(own_ref, seq, q_ref)
+    out_low, out_high = load_rows(own_ref, seq, do_ref)
+
+    def tables(ref):
+        table = ref[0]
+        lows, highs = [], []
+        for i in range(2):
+            one, two = own_ref[seq, 2 * i], own_ref[seq, 2 * i + 1]
+            front = table[:, 2 * i * BLK : (2 * i + 1) * BLK]
+            back = table[:, (2 * i + 1) * BLK : (2 * i + 2) * BLK]
+            lows.append(jnp.where(one > two, back, front))
+            highs.append(jnp.where(one > two, front, back))
+        return jnp.concatenate(lows, axis=1), jnp.concatenate(highs, axis=1)
+
+    cos_low, cos_high = tables(cos_ref)
+    sin_low, sin_high = tables(sin_ref)
+
+    def unturned(grad_q, cosine, sine):
+        heads = []
+        for part in head_slices(grad_q):
+            front, back = part[:HALF], part[HALF:]
+            heads.append(
+                jnp.concatenate(
+                    [front * cosine + back * sine, back * cosine - front * sine], axis=0
+                ).T
+            )
+        return heads
+
+    lows, highs = [], []
+    for lo, hi in query_chunks():
+        scores = dot(key_low, query_low[lo:hi], NT) + low_ref[:, : hi - lo]
+        probs = jnp.exp(scores - lse_ref[0, 0:1, lo:hi])
+        probs_ref[:half, lo:hi] = probs.astype(BF)
+        grad_p = dot(value_low, out_low[lo:hi], NT)
         inner = jnp.sum(probs * grad_p, axis=0, keepdims=True)
         grad_s = (probs * (grad_p - inner)).astype(BF)
-        grads_ref[:, lo:hi] = grad_s
-        grad_q = dot(key_t, grad_s) * scale
-        for at in range(0, hi - lo, local):
-            front = grad_q[:HALF, at : at + local]
-            back = grad_q[HALF:, at : at + local]
-            turned = jnp.concatenate(
-                [front * cosine + back * sine, back * cosine - front * sine], axis=0
-            )
-            heads.append(turned.T)
-    dq_ref[...] = jnp.concatenate(heads, axis=1).astype(BF).reshape(dq_ref.shape)
-    grad_k = dot(grads_ref[...], query)
-    grad_v = dot(probs_ref[...], grad_o)
-    dkv_ref[...] = jnp.concatenate([grad_k, grad_v], axis=1).astype(BF).reshape(dkv_ref.shape)
-
-
-def attention(back, offset, seqs, starts, qpos, q, kv, *more):
+        grads_ref[:half, lo:hi] = grad_s
+        lows += unturned(dot(key_t[:, :half], grad_s) * scale, cos_low, sin_low)
+        lse = lse_ref[0, 1:2, lo:hi]
+        at, to = wide + lo, wide + hi
+        first = jnp.exp(dot(key_low, query_high[lo:hi], NT) - lse)
+        second = jnp.exp(dot(key_high, query_high[lo:hi], NT) + high_ref[:, : hi - lo] - lse)
+        probs_ref[:half, at:to] = first.astype(BF)
+        probs_ref[half:, at:to] = second.astype(BF)
+        grad_first = dot(value_low, out_high[lo:hi], NT)
+        grad_second = dot(value_high, out_high[lo:hi], NT)
+        inner = jnp.sum(first * grad_first, axis=0, keepdims=True) + jnp.sum(
+            second * grad_second, axis=0, keepdims=True
+        )
+        grad_first = (first * (grad_first - inner)).astype(BF)
+        grad_second = (second * (grad_second - inner)).astype(BF)
+        grads_ref[:half, at:to] = grad_first
+        grads_ref[half:, at:to] = grad_second
+        grad_q = dot(key_t[:, :half], grad_first) + dot(key_t[:, half:], grad_second)
+        highs += unturned(grad_q * scale, cos_high, sin_high)
+    store_rows(
+        own_ref, seq, dq_ref, jnp.concatenate(lows, axis=1), jnp.concatenate(highs, axis=1)
+    )
+
+    def key_grads(ref, left, right):
+        low = dot(ref[:half, :total], left) + dot(ref[:half, wide : wide + total], right)
+        return low, dot(ref[half:, wide : wide + total], right)
+
+    key_parts = key_grads(grads_ref, query_low, query_high)
+    value_parts = key_grads(probs_ref, out_low, out_high)
+    grad_low, grad_high = [
+        jnp.concatenate([key, value], axis=1).astype(BF)
+        for key, value in zip(key_parts, value_parts)
+    ]
+    for r in range(half // BLK):
+        low, high, _, _ = run_order(starts_ref, seq, r)
+        at = r * BLK
+        dkv_ref[r // 2, r % 2, 0, pl.ds(low, BLK), :] = grad_low[at : at + BLK]
+        dkv_ref[r // 2, r % 2, 0, pl.ds(high, BLK), :] = grad_high[at : at + BLK]
+
+
+def attention(back, offset, seqs, starts, own, q, kv, *more):
     run = q.shape[2]
+    assert run == 2 * BLK
     chips = kv.shape[0]
     local = 2 * run
     keys = chips * local
     total = GROUP * local
-    q_spec = pl.BlockSpec((2, 1, run, Q_WIDTH), lambda s, st: (0, s + offset, 0, 0))
-    part_spec = pl.BlockSpec((2, 1, run, Q_WIDTH), lambda s, st: (0, s, 0, 0))
+    wide = 512
+    q_spec = pl.BlockSpec((2, 1, run, Q_WIDTH), lambda s, st, ow: (0, s + offset, 0, 0))
+    part_spec = pl.BlockSpec((2, 1, run, Q_WIDTH), lambda s, st, ow: (0, s, 0, 0))
     kv_block = (chips, 2, 1, run, 2 * HEAD_DIM)
-    kv_spec = pl.BlockSpec(kv_block, lambda s, st: (0, 0, s + offset, 0, 0))
-    kv_part_spec = pl.BlockSpec(kv_block, lambda s, st: (0, 0, s, 0, 0))
-    lse_spec = pl.BlockSpec((1, 1, total), lambda s, st: (s + offset, 0, 0))
-    qpos_spec = pl.BlockSpec((1, 1, local), lambda s, st: (s + offset, 0, 0))
-    turn_spec = pl.BlockSpec((1, HALF, local), lambda s, st: (s + offset, 0, 0))
-    in_specs = [qpos_spec, q_spec, kv_spec]
-    scratch = [pltpu.VMEM((keys, local), F32)]
+    kv_spec = pl.BlockSpec(kv_block, lambda s, st, ow: (0, 0, s + offset, 0, 0))
+    kv_part_spec = pl.BlockSpec(kv_block, lambda s, st, ow: (0, 0, s, 0, 0))
+    lse_spec = pl.BlockSpec((1, 2, wide), lambda s, st, ow: (s + offset, 0, 0))
+    turn_spec = pl.BlockSpec((1, HALF, local), lambda s, st, ow: (s + offset, 0, 0))
+    in_specs = [q_spec, kv_spec]
+    scratch = [
+        pltpu.VMEM((keys, 2 * HEAD_DIM), BF),
+        pltpu.VMEM((keys // 2, 256), F32),
+        pltpu.VMEM((keys // 2, 256), F32),
+    ]
     part_shape = jax.ShapeDtypeStruct((2, seqs, run, Q_WIDTH), BF)
     if back:
         in_specs += [q_spec, lse_spec, turn_spec, turn_spec]
         out_specs = [part_spec, kv_part_spec]
         kv_shape = kv.shape[:2] + (seqs,) + kv.shape[3:]
         out_shape = [part_shape, jax.ShapeDtypeStruct(kv_shape, BF)]
-        scratch += [pltpu.VMEM((keys, total), BF)] * 2
+        scratch += [pltpu.VMEM((keys, 2 * wide), BF)] * 2
     else:
         out_specs = [part_spec, lse_spec]
-        out_shape = [part_shape, jax.ShapeDtypeStruct((seqs, 1, total), F32)]
+        out_shape = [part_shape, jax.ShapeDtypeStruct((seqs, 2, wide), F32)]
     passes = 5 if back else 2
     return pl.pallas_call(
         functools.partial(attend_back_kernel if back else attend_kernel, offset),
         grid_spec=pltpu.PrefetchScalarGridSpec(
-            num_scalar_prefetch=1,
+            num_scalar_prefetch=2,
             grid=(seqs,),
             in_specs=in_specs,
             out_specs=out_specs,
@@ -225,7 +333,7 @@
             bytes_accessed=seqs * keys * 512,
             transcendentals=seqs * keys * total,
         ),
-    )(starts, qpos, q, kv, *more)
+    )(starts, own, q, kv, *more)
 
 
 def mlp_kernel(s_ref, c_ref, g_ref, u_ref, d_ref, hid_ref, gg_ref, gu_ref, mix_ref, gs_ref):
@@ -565,7 +673,7 @@
         firsts = places[:, :, ::BLK]
         starts = gather_small(gather_small(firsts, "cy", 2), "cz", cz)
         starts = starts.transpose(3, 0, 1, 2, 4).reshape(seqs, -1)
-        qpos = places.transpose(1, 0, 2).reshape(seqs, 1, 2 * run)
+        own_starts = firsts.transpose(1, 0, 2).reshape(seqs, 4)
         turned = Q_WIDTH + HEAD_DIM
         kv_rows = key_bias.shape[0]
         vectors = jnp.concatenate([query_bias, key_bias, value_bias, first_gain, second_gain])
@@ -608,8 +716,8 @@
         up_own = units(up_weight)
         down_own = by_quarter([down_weight[at : at + window] for at in begins])
         qkv_all = gather_rows(qkv_local)
-        qkv_all, gate_own, up_own, out_own, down_own, starts, qpos = lax.optimization_barrier(
-            (qkv_all, gate_own, up_own, out_weight, down_own, starts, qpos)
+        qkv_all, gate_own, up_own, out_own, down_own, starts, own_starts = lax.optimization_barrier(
+            (qkv_all, gate_own, up_own, out_weight, down_own, starts, own_starts)
         )
         qkv_all = qkv_all.reshape(owners, slab + 16, wide)
         qkv = qkv_all[:, :slab].reshape(owners * slab, wide)
@@ -654,15 +762,15 @@
         cut = seqs // 2
         kv_all = gather_chips(kv)
         gate_far = gather_start(gate_own)
-        kv_all, out_w, down_w, cot_late, up_own = together(
-            kv_all, out_w, down_w, cotangent, up_own
+        kv_all, out_w, down_w, gate_far, cot_late, up_own = together(
+            kv_all, out_w, down_w, gate_far, cotangent, up_own
         )
         up_far = gather_start(up_own)
         grad_own = cot_late.reshape(rows, width)
         far_grad = swap(grad_own, "cy")
-        attn, lse = attention(False, 0, seqs, starts, qpos, q, kv_all)
+        attn, lse = attention(False, 0, seqs, starts, own_starts, q, kv_all)
         attn_rows = attn.reshape(2 * rows, Q_WIDTH)
-        attn_rows, gate_far, up_far, far_grad = together(attn_rows, gate_far, up_far, far_grad)
+        attn_rows, up_far, far_grad = together(attn_rows, up_far, far_grad)
         gate_w = gather_finish(gate_own, gate_far)
         up_w = gather_finish(up_own, up_far)
         attn_part = dot(attn_rows, out_w).astype(BF)
@@ -727,14 +835,14 @@
         cos_t, sin_t = turned_rows(cosine), turned_rows(sine)
 
         def attend_back(at, count, grad):
-            return attention(True, at, count, starts, qpos, q, kv_all, grad, lse, cos_t, sin_t)
+            return attention(True, at, count, starts, own_starts, q, kv_all, grad, lse, cos_t, sin_t)
 
         def keys_cy(values):
             return split_cy(values.reshape((cz, 2) + values.shape[1:]), 1)
 
         grad_q_near, grad_kv_near = attend_back(0, cut, grad_attn)
-        grad_q_near, grad_kv_near, back_mix, sum_gate, sum_up = together(
-            grad_q_near, grad_kv_near, back_mix, sum_gate, sum_up
+        grad_q_near, grad_kv_near, back_mix, sum_down, sum_gate, sum_up = together(
+            grad_q_near, grad_kv_near, back_mix, sum_down, sum_gate, sum_up
         )
         mix_own = near_mix[:rows].astype(F32) + mix_near_core.astype(F32)
         mixed = (middle + mix_own + back_mix.astype(F32)).astype(BF).reshape(seqs, run, width)

time: 690 us -> 673 us (0.975)
  waiting for transfers between devices: 188 us -> 173 us
  Pallas kernels: 213 us -> 203 us
    all_gather x1, waiting for transfers between devices: 19 us -> 0.01 us  [gather_chips(): return lax.all_gather(values, CHIPS, axis=0)]
    pallas_call x3, Pallas kernels: 87.5 us -> 77.4 us  [attention(): pl.pallas_call(functools.partial(attend_back_kernel if back else attend_k...]
  transfers between devices with their start and end apart: 67 -> 67, of which waited for: 20 -> 19; matrix products, arithmetic and copies ran while one was open for 15% -> 17% of each run, Pallas kernels for 21% -> 20%
where the time goes in v3:
time: 673 us; the launch traced here: 663 us
  Pallas kernels  203 us (30%)
  waiting for transfers between devices  173 us (26%)
  starting transfers between devices  103 us (15%)
  other arithmetic  101 us (15%)
  local copies, waits for them, and re-layouts  50.2 us (7%)
  matrix products  17.6 us (3%)
  between operations  15.7 us (2%)
    ppermute x10, waiting for transfers between devices, exchange(): return lax.ppermute(values, axis, [(i, i ^ bit) for i in range(size)])  87.7 us
    pallas_call x3, Pallas kernels, attention(): pl.pallas_call(functools.partial(attend_back_kernel if back else attend_k...  77.4 us
    pallas_call x2, Pallas kernels, mlp(): pl.pallas_call(mlp_kernel, grid=(count // step,), in_specs=[row_block(wid...  60.7 us
    ppermute x37, waiting for transfers between devices, swap(): return lax.ppermute(values, axis, SWAP)  43.9 us
    ppermute x37, starting transfers between devices, swap(): return lax.ppermute(values, axis, SWAP)  42.8 us
    pallas_call x3, Pallas kernels, weight_grad(): pl.pallas_call(weight_grad_kernel, grid_spec=pltpu.PrefetchScalarGridSpec...  39.9 us
    ppermute x1, waiting for transfers between devices, body(): out_far = lax.ppermute(out_own, ('core', 'pair'), [(0, 1), (3, 2)])  37.6 us
    ppermute x6, starting transfers between devices, line_send(): lax.ppermute(load[0], axis, right)  25.6 us
  transfers between devices with their start and end apart: 67, of which 19 were waited for; matrix products, arithmetic and copies ran while one was open for 17% of the time, Pallas kernels for 20%

profile of v3, /device:TPU:1, one launch (start us, length us, event | category | flops | bytes accessed | tf_op | source)
XLA Modules:
  0.0 663.4 jit_solution(4494598370395654183)
XLA Ops:
  7.2 3.5 concatenate.142
  17.8 2.8 fusion.49
  46.7 3.1 pad_maximum_fusion.1.x_ref
  49.8 8.7 %shard_map.254 = (bf16[1536,896]{1,0:T(8,128)(2,1)}, bf16[1536,448]{1,0:T(8,128)(2,1)}, bf16[1536,128]{1,0:T(8,128)(2,1)}) custom-call(bf16[1536,896]{1,0:T(8,128)(2,1)} %pad_maximum_fusion.1.x_ref, f32[1,896]{1,0:T(1,128)} %reshape.379.gain_ref, bf16[896,576]{1,0:T(8,128)(2,1)} %bitcast.153, f32[1,576]{1,0:T(1,128)} %maximum_convert_fusion.b_ref, ...), custom_call_target="tpu_custom_call" | custom-call | flops 1585446912 | bytes 5505024 | tf_op jit(solution)/shard_map/pallas_call | solution.py:69
  60.4 3.0 collective-permute-start.8
  63.4 37.6 %collective-permute-done.6 = bf16[448,896]{1,0:T(8,128)(2,1)} collective-permute-done((bf16[448,896]{1,0:T(8,128)(2,1)S(1)}, bf16[448,896]{1,0:T(8,128)(2,1)}, u32[]{:S(2)}, u32[]{:S(2)}) %collective-permute-start.6) | collective-permute-done | bytes 802848 | tf_op jit(solution)/shard_map/ppermute | solution.py:741
  106.1 12.9 %collective-permute-done.8 = bf16[1,448,1280]{2,1,0:T(8,128)(2,1)S(1)} collective-permute-done((bf16[1,448,1280]{2,1,0:T(8,128)(2,1)}, bf16[1,448,1280]{2,1,0:T(8,128)(2,1)S(1)}, u32[]{:S(2)}, u32[]{:S(2)}) %collective-permute-start.8) | collective-permute-done | bytes 1146912 | tf_op jit(solution)/shard_map/ppermute | solution.py:33
  121.4 28.4 %shard_map.255 = (bf16[2,12,64,448]{3,2,1,0:T(8,128)(2,1)}, f32[12,2,512]{2,1,0:T(2,128)}) custom-call(s32[12,32]{1,0:T(8,128)} %copy.72.starts_ref, s32[12,4]{1,0:T(8,128)} %copy.73.own_ref, bf16[2,12,64,448]{3,2,1,0:T(8,128)(2,1)} %bitcast.167, bf16[8,2,12,64,128]{4,3,2,1,0:T(8,128)(2,1)} %all-gather.4.cloned.1.call-done.kv_ref), custom_call_target="tpu_custom_call" | custom-call | flops 11274289152 | bytes 6291456 | tf_op jit(solution)/shard_map/pallas_call | solution.py:320
  150.4 3.2 convolution_convert_fusion.1
  167.7 3.1 pad_maximum_fusion.3.c_ref.b_near
  173.6 30.3 %shard_map.256 = (bf16[1536,1280]{1,0:T(8,128)(2,1)}, bf16[1536,1280]{1,0:T(8,128)(2,1)}, bf16[1536,1280]{1,0:T(8,128)(2,1)}, bf16[1536,896]{1,0:T(8,128)(2,1)}, bf16[1536,896]{1,0:T(8,128)(2,1)}) custom-call(bf16[1536,896]{1,0:T(8,128)(2,1)} %pad_maximum_fusion.2.s_ref.a_near, bf16[1536,896]{1,0:T(8,128)(2,1)} %pad_maximum_fusion.3.c_ref.b_near, ...), custom_call_target="tpu_custom_call" | custom-call | flops 21139292160 | bytes 22806528 | tf_op jit(solution)/shard_map/pallas_call | solution.py:364
  212.4 30.4 %shard_map.257 = (bf16[1536,1280]{1,0:T(8,128)(2,1)}, bf16[1536,1280]{1,0:T(8,128)(2,1)}, bf16[1536,1280]{1,0:T(8,128)(2,1)}, bf16[1536,896]{1,0:T(8,128)(2,1)}, bf16[1536,896]{1,0:T(8,128)(2,1)}) custom-call(bf16[1536,896]{1,0:T(8,128)(2,1)} %constant_dynamic-update-slice_fusion.s_ref.a_far, bf16[1536,896]{1,0:T(8,128)(2,1)} %copy-done.44, ...), custom_call_target="tpu_custom_call" | custom-call | flops 21139292160 | bytes 22806528 | tf_op jit(solution)/shard_map/pallas_call | solution.py:364
  249.2 13.7 %shard_map.258 = (bf16[1,4,1120,128]{3,2,1,0:T(8,128)(2,1)}, bf16[1,4,1120,128]{3,2,1,0:T(8,128)(2,1)}) custom-call(s32[1]{0:T(128)} %bitcast.27.pair_ref, bf16[1536,1280]{1,0:T(8,128)(2,1)} %get-tuple-element.183.a_near, bf16[1536,1280]{1,0:T(8,128)(2,1)} %get-tuple-element.193.a_far, bf16[1536,896]{1,0:T(8,128)(2,1)} %pad_maximum_fusion.3.c_ref.b_near, ...), custom_call_target="tpu_custom_call" | custom-call | flops 7046430720 | bytes 13369344 | tf_op jit(solution)/shard_map/pallas_call | solution.py:429
  268.1 13.2 %shard_map.259 = (bf16[1,4,1120,128]{3,2,1,0:T(8,128)(2,1)}, bf16[1,4,1120,128]{3,2,1,0:T(8,128)(2,1)}) custom-call(s32[1]{0:T(128)} %bitcast.27.pair_ref, bf16[1536,896]{1,0:T(8,128)(2,1)} %pad_maximum_fusion.2.s_ref.a_near, bf16[1536,896]{1,0:T(8,128)(2,1)} %constant_dynamic-update-slice_fusion.s_ref.a_far, bf16[1536,1280]{1,0:T(8,128)(2,1)} %get-tuple-element.201.b_near, ...), custom_call_target="tpu_custom_call" | custom-call | flops 7046430720 | bytes 13369344 | tf_op jit(solution)/shard_map/pallas_call | solution.py:429
  281.3 13.0 %shard_map.260 = (bf16[1,4,1120,128]{3,2,1,0:T(8,128)(2,1)}, bf16[1,4,1120,128]{3,2,1,0:T(8,128)(2,1)}) custom-call(s32[1]{0:T(128)} %bitcast.27.pair_ref, bf16[1536,896]{1,0:T(8,128)(2,1)} %pad_maximum_fusion.2.s_ref.a_near, bf16[1536,896]{1,0:T(8,128)(2,1)} %constant_dynamic-update-slice_fusion.s_ref.a_far, bf16[1536,1280]{1,0:T(8,128)(2,1)} %get-tuple-element.200.b_near, ...), custom_call_target="tpu_custom_call" | custom-call | flops 7046430720 | bytes 13369344 | tf_op jit(solution)/shard_map/pallas_call | solution.py:429
  294.4 4.6 collective-permute-done.19
  299.0 3.0 multiply_reduce_fusion
  302.0 4.9 fusion.46
  313.0 3.3 add_convert_fusion.1
  318.2 4.3 fusion.14
  322.5 3.2 collective-permute-start.27
  325.7 4.5 convolution_convert_fusion.2
  332.7 24.5 %shard_map.261 = (bf16[2,6,64,448]{3,2,1,0:T(8,128)(2,1)}, bf16[8,2,6,64,128]{4,3,2,1,0:T(8,128)(2,1)}) custom-call(s32[12,32]{1,0:T(8,128)} %copy.72.starts_ref, s32[12,4]{1,0:T(8,128)} %copy.73.own_ref, bf16[2,12,64,448]{3,2,1,0:T(8,128)(2,1)} %bitcast.168, bf16[8,2,12,64,128]{4,3,2,1,0:T(8,128)(2,1)} %all-gather.4.cloned.1.call-done.kv_ref, ...), custom_call_target="tpu_custom_call" | custom-call | flops 14092861440 | bytes 3145728 | tf_op jit(solution)/shard_map/pallas_call | solution.py:320
  357.1 11.1 %collective-permute-done.26 = bf16[4,1120,128]{2,1,0:T(8,128)(2,1)} collective-permute-done((bf16[4,1120,128]{2,1,0:T(8,128)(2,1)}, bf16[4,1120,128]{2,1,0:T(8,128)(2,1)}, u32[]{:S(2)}, u32[]{:S(2)}) %collective-permute-start.26) | collective-permute-done | bytes 1146912 | tf_op jit(solution)/shard_map/ppermute | solution.py:33
  388.4 24.6 %shard_map.262 = (bf16[2,6,64,448]{3,2,1,0:T(8,128)(2,1)}, bf16[8,2,6,64,128]{4,3,2,1,0:T(8,128)(2,1)}) custom-call(s32[12,32]{1,0:T(8,128)} %copy.72.starts_ref, s32[12,4]{1,0:T(8,128)} %copy.73.own_ref, bf16[2,12,64,448]{3,2,1,0:T(8,128)(2,1)} %bitcast.169, bf16[8,2,12,64,128]{4,3,2,1,0:T(8,128)(2,1)} %all-gather.4.cloned.1.call-done.kv_ref, ...), custom_call_target="tpu_custom_call" | custom-call | flops 14092861440 | bytes 3145728 | tf_op jit(solution)/shard_map/pallas_call | solution.py:320
  427.8 13.5 %collective-permute-done.36 = bf16[224,448]{1,0:T(8,128)(2,1)S(1)} collective-permute-done((bf16[224,448]{1,0:T(8,128)(2,1)S(1)}, bf16[224,448]{1,0:T(8,128)(2,1)S(1)}, u32[]{:S(2)}, u32[]{:S(2)}) %collective-permute-start.36) | collective-permute-done | bytes 200736 | tf_op jit(solution)/shard_map/ppermute | solution.py:638
  445.7 5.1 collective-permute-start.37
  454.5 3.1 collective-permute-start.41
  457.6 3.6 collective-permute-start.39
  461.1 19.3 %collective-permute-done.42 = bf16[224,448]{1,0:T(8,128)(2,1)S(1)} collective-permute-done((bf16[224,448]{1,0:T(8,128)(2,1)S(1)}, bf16[224,448]{1,0:T(8,128)(2,1)S(1)}, u32[]{:S(2)}, u32[]{:S(2)}) %collective-permute-start.42) | collective-permute-done | bytes 200736 | tf_op jit(solution)/shard_map/ppermute | solution.py:638
  488.1 2.9 fusion.11
  494.8 3.6 collective-permute-done.45
  498.4 3.1 collective-permute-done.46
  501.9 5.0 collective-permute-start.50
  507.0 11.3 %collective-permute-start.47 = (bf16[1536,128]{1,0:T(8,128)(2,1)S(1)}, bf16[1536,128]{1,0:T(8,128)(2,1)S(1)}, u32[]{:S(2)}, u32[]{:S(2)}) collective-permute-start(bf16[1536,128]{1,0:T(8,128)(2,1)S(1)} %get-tuple-element.273), channel_id=1, source_target_pairs={{0,8},{8,16},{16,24},{1,9},{9,17},{17,25},{2,10},{10,18},{18,26},{... | collective-permute-start | bytes 1179656 | tf_op jit(solution)/shard_map/ppermute | solution.py:543
  519.6 5.3 collective-permute-start.49
  525.3 30.1 %collective-permute-done.49 = bf16[224,448]{1,0:T(8,128)(2,1)S(1)} collective-permute-done((bf16[224,448]{1,0:T(8,128)(2,1)S(1)}, bf16[224,448]{1,0:T(8,128)(2,1)S(1)}, u32[]{:S(2)}, u32[]{:S(2)}) %collective-permute-start.49) | collective-permute-done | bytes 200736 | tf_op jit(solution)/shard_map/ppermute | solution.py:638
  555.8 3.9 fusion.21
  569.9 4.0 add_convert_fusion
  574.3 5.0 collective-permute-start.52
  588.2 8.8 %collective-permute-done.54 = f32[2944]{0:T(1024)S(1)} collective-permute-done((f32[2944]{0:T(1024)S(1)}, f32[2944]{0:T(1024)S(1)}, u32[]{:S(2)}, u32[]{:S(2)}) %collective-permute-start.54) | collective-permute-done | bytes 11808 | tf_op jit(solution)/shard_map/ppermute | solution.py:638
  601.0 13.1 %collective-permute-done.56 = f32[2944]{0:T(1024)S(1)} collective-permute-done((f32[2944]{0:T(1024)S(1)}, f32[2944]{0:T(1024)S(1)}, u32[]{:S(2)}, u32[]{:S(2)}) %collective-permute-start.56) | collective-permute-done | bytes 11808 | tf_op jit(solution)/shard_map/ppermute | solution.py:638
  615.9 2.9 collective-permute-done.58
  618.8 3.4 collective-permute-start.60
  624.3 3.9 fusion.1
  630.6 3.3 collective-permute-start.64
  639.9 9.8 %shard_map.263 = (f32[448,4864]{1,0:T(8,128)}, f32[448,4864]{1,0:T(8,128)}) custom-call(bf16[4,4,3,1120,128]{4,3,2,1,0:T(8,128)(2,1)} %bitcast.122, bf16[4,4,3,1120,128]{4,3,2,1,0:T(8,128)(2,1)} %bitcast.123), custom_call_target="tpu_custom_call" | custom-call | tf_op jit(solution)/shard_map/pallas_call | solution.py:497
  649.8 6.4 shard_map.264
  (379 shorter events, 182.8 us)
Async XLA Ops:
  7.2 111.9 %all-gather.4.cloned.1.call-start = ((), (), s32[]{:S(2)}) async-start(), calls=%async_computation | async-start | bytes 3538944 | tf_op jit(solution)/shard_map/all_gather | solution.py:613
  14.8 25.0 %collective-permute-start = (bf16[1,464,576]{1,2,0:T(8,128)(2,1)}, bf16[1,464,576]{1,2,0:T(8,128)(2,1)}, u32[]{:S(2)}, u32[]{:S(2)}) collective-permute-start(bf16[1,464,576]{1,2,0:T(8,128)(2,1)} %copy.65), channel_id=1, source_target_pairs={{0,1},{1,0},{2,3},{3,2},{4,5},{5,4},{6,7},{7,6},{8,9},{9,8},{10,11... | collective-permute-start | bytes 1603592 | tf_op jit(solution)/shard_map/ppermute | solution.py:33
  16.8 10.2 %collective-permute-start.1 = (s32[12,64]{1,0:T(8,128)S(1)}, s32[12,64]{1,0:T(8,128)S(1)}, u32[]{:S(2)}, u32[]{:S(2)}) collective-permute-start(s32[12,64]{1,0:T(8,128)S(1)} %copy-done.58), channel_id=1, source_target_pairs={{0,2},{2,0},{1,3},{3,1},{4,6},{6,4},{5,7},{7,5},{8,10},{10,8},{9,1... | collective-permute-start | bytes 9224 | tf_op jit(solution)/shard_map/ppermute | solution.py:33
  17.8 29.0 %collective-permute-start.5 = (bf16[12,64,896]{2,1,0:T(8,128)(2,1)S(1)}, bf16[12,64,896]{2,1,0:T(8,128)(2,1)}, u32[]{:S(2)}, u32[]{:S(2)}) collective-permute-start(bf16[12,64,896]{2,1,0:T(8,128)(2,1)S(1)} %copy-done), channel_id=1, source_target_pairs={{0,2},{2,0},{1,3},{3,1},{4,6},{6,4},{5,7},{7,5},{8,10},{10,8},{9,1... | collective-permute-start | bytes 4128776 | tf_op jit(solution)/shard_map/ppermute | solution.py:33
  58.5 581.4 %all-gather.6.cloned.1.call-start = ((), (), s32[]{:S(2)}) async-start(), calls=%async_computation.1 | async-start | bytes 14622720 | tf_op jit(solution)/shard_map/all_gather | solution.py:1000
  58.6 44.5 %collective-permute-start.7 = (bf16[1,640,896]{2,1,0:T(8,128)(2,1)S(1)}, bf16[1,640,896]{2,1,0:T(8,128)(2,1)}, u32[]{:S(2)}, u32[]{:S(2)}) collective-permute-start(bf16[1,640,896]{2,1,0:T(8,128)(2,1)S(1)} %bitcast.141), channel_id=1, source_target_pairs={{0,1},{1,0},{2,3},{3,2},{4,5},{5,4},{6,7},{7,6},{8,9},{9,8},{10,11... | collective-permute-start | bytes 3440648 | tf_op jit(solution)/shard_map/ppermute | solution.py:33
  58.9 42.0 %collective-permute-start.6 = (bf16[448,896]{1,0:T(8,128)(2,1)S(1)}, bf16[448,896]{1,0:T(8,128)(2,1)}, u32[]{:S(2)}, u32[]{:S(2)}) collective-permute-start(bf16[448,896]{1,0:T(8,128)(2,1)S(1)} %copy-done.40), channel_id=1, source_target_pairs={{0,1},{3,2},{4,5},{7,6},{8,9},{11,10},{12,13},{15,14},{16,17},{19,... | collective-permute-start | bytes 2408456 | tf_op jit(solution)/shard_map/ppermute | solution.py:741
  60.4 58.7 %collective-permute-start.8 = (bf16[1,448,1280]{2,1,0:T(8,128)(2,1)}, bf16[1,448,1280]{2,1,0:T(8,128)(2,1)S(1)}, u32[]{:S(2)}, u32[]{:S(2)}) collective-permute-start(bf16[1,448,1280]{2,1,0:T(8,128)(2,1)} %bitcast.23), channel_id=1, source_target_pairs={{0,1},{1,0},{2,3},{3,2},{4,5},{5,4},{6,7},{7,6},{8,9},{9,8},{10,11... | collective-permute-start | bytes 3440648 | tf_op jit(solution)/shard_map/ppermute | solution.py:33
  119.0 31.3 %collective-permute-start.10 = (bf16[768,896]{1,0:T(8,128)(2,1)}, bf16[768,896]{1,0:T(8,128)(2,1)}, u32[]{:S(2)}, u32[]{:S(2)}) collective-permute-start(bf16[768,896]{1,0:T(8,128)(2,1)} %bitcast.26), channel_id=1, source_target_pairs={{0,4},{4,0},{1,5},{5,1},{2,6},{6,2},{3,7},{7,3},{8,12},{12,8},{9,1... | collective-permute-start | bytes 4128776 | tf_op jit(solution)/shard_map/ppermute | solution.py:33
  120.0 29.8 %collective-permute-start.9 = (bf16[1,448,1280]{2,1,0:T(8,128)(2,1)S(1)}, bf16[1,448,1280]{2,1,0:T(8,128)(2,1)}, u32[]{:S(2)}, u32[]{:S(2)}) collective-permute-start(bf16[1,448,1280]{2,1,0:T(8,128)(2,1)S(1)} %bitcast.142), channel_id=1, source_target_pairs={{0,1},{1,0},{2,3},{3,2},{4,5},{5,4},{6,7},{7,6},{8,9},{9,8},{10,11... | collective-permute-start | bytes 3440648 | tf_op jit(solution)/shard_map/ppermute | solution.py:33
  157.6 10.1 %collective-permute-start.14 = (bf16[768,896]{1,0:T(8,128)(2,1)}, bf16[768,896]{1,0:T(8,128)(2,1)S(1)}, u32[]{:S(2)}, u32[]{:S(2)}) collective-permute-start(bf16[768,896]{1,0:T(8,128)(2,1)} %bitcast.26), channel_id=1, source_target_pairs={{0,2},{2,0},{1,3},{3,1},{4,6},{6,4},{5,7},{7,5},{8,10},{10,8},{9,1... | collective-permute-start | bytes 4128776 | tf_op jit(solution)/shard_map/ppermute | solution.py:33
  162.5 9.3 %collective-permute-start.13 = (bf16[768,896]{1,0:T(8,128)(2,1)S(1)}, bf16[768,896]{1,0:T(8,128)(2,1)S(1)}, u32[]{:S(2)}, u32[]{:S(2)}) collective-permute-start(bf16[768,896]{1,0:T(8,128)(2,1)S(1)} %multiply_convert_fusion), channel_id=1, source_target_pairs={{0,2},{2,0},{1,3},{3,1},{4,6},{6,4},{5,7},{7,5},{8,10},{10,8},{9,1... | collective-permute-start | bytes 4128776 | tf_op jit(solution)/shard_map/ppermute | solution.py:33
  164.7 43.0 %collective-permute-start.17 = (bf16[768,896]{1,0:T(8,128)(2,1)}, bf16[768,896]{1,0:T(8,128)(2,1)}, u32[]{:S(2)}, u32[]{:S(2)}) collective-permute-start(bf16[768,896]{1,0:T(8,128)(2,1)} %collective-permute-done.10), channel_id=1, source_target_pairs={{0,2},{2,0},{1,3},{3,1},{4,6},{6,4},{5,7},{7,5},{8,10},{10,8},{9,1... | collective-permute-start | bytes 4128776 | tf_op jit(solution)/shard_map/ppermute | solution.py:33
  170.8 33.1 %collective-permute-start.12 = (bf16[768,896]{1,0:T(8,128)(2,1)S(1)}, bf16[768,896]{1,0:T(8,128)(2,1)S(1)}, u32[]{:S(2)}, u32[]{:S(2)}) collective-permute-start(bf16[768,896]{1,0:T(8,128)(2,1)S(1)} %multiply_convert_fusion), channel_id=1, source_target_pairs={{0,4},{4,0},{1,5},{5,1},{2,6},{6,2},{3,7},{7,3},{8,12},{12,8},{9,1... | collective-permute-start | bytes 4128776 | tf_op jit(solution)/shard_map/ppermute | solution.py:33
  265.5 28.8 %collective-permute-start.21 = (bf16[768,896]{1,0:T(8,128)(2,1)}, bf16[768,896]{1,0:T(8,128)(2,1)}, u32[]{:S(2)}, u32[]{:S(2)}) collective-permute-start(bf16[768,896]{1,0:T(8,128)(2,1)} %slice.286), channel_id=1, source_target_pairs={{0,2},{2,0},{1,3},{3,1},{4,6},{6,4},{5,7},{7,5},{8,10},{10,8},{9,1... | collective-permute-start | bytes 4128776 | tf_op jit(solution)/shard_map/ppermute | solution.py:33
  267.1 27.3 %collective-permute-start.22 = (bf16[768,896]{1,0:T(8,128)(2,1)}, bf16[768,896]{1,0:T(8,128)(2,1)}, u32[]{:S(2)}, u32[]{:S(2)}) collective-permute-start(bf16[768,896]{1,0:T(8,128)(2,1)} %slice.287), channel_id=1, source_target_pairs={{0,2},{2,0},{1,3},{3,1},{4,6},{6,4},{5,7},{7,5},{8,10},{10,8},{9,1... | collective-permute-start | bytes 4128776 | tf_op jit(solution)/shard_map/ppermute | solution.py:33
  267.2 31.7 %collective-permute-start.19 = (bf16[768,896]{1,0:T(8,128)(2,1)}, bf16[768,896]{1,0:T(8,128)(2,1)}, u32[]{:S(2)}, u32[]{:S(2)}) collective-permute-start(bf16[768,896]{1,0:T(8,128)(2,1)} %add_convert_fusion.2), channel_id=1, source_target_pairs={{0,4},{4,0},{1,5},{5,1},{2,6},{6,2},{3,7},{7,3},{8,12},{12,8},{9,1... | collective-permute-start | bytes 4128776 | tf_op jit(solution)/shard_map/ppermute | solution.py:33
  267.7 26.6 %collective-permute-start.20 = (bf16[4,1120,128]{2,1,0:T(8,128)(2,1)}, bf16[4,1120,128]{2,1,0:T(8,128)(2,1)}, u32[]{:S(2)}, u32[]{:S(2)}) collective-permute-start(bf16[4,1120,128]{2,1,0:T(8,128)(2,1)} %bitcast.35), channel_id=1, source_target_pairs={{0,1},{1,0},{2,3},{3,2},{4,5},{5,4},{6,7},{7,6},{8,9},{9,8},{10,11... | collective-permute-start | bytes 3440648 | tf_op jit(solution)/shard_map/ppermute | solution.py:33
  306.9 11.4 %collective-permute-start.23 = (bf16[768,896]{1,0:T(8,128)(2,1)}, bf16[768,896]{1,0:T(8,128)(2,1)}, u32[]{:S(2)}, u32[]{:S(2)}) collective-permute-start(bf16[768,896]{1,0:T(8,128)(2,1)} %get-tuple-element.312), channel_id=1, source_target_pairs={{0,2},{2,0},{1,3},{3,1},{4,6},{6,4},{5,7},{7,5},{8,10},{10,8},{9,1... | collective-permute-start | bytes 4128776 | tf_op jit(solution)/shard_map/ppermute | solution.py:33
  316.3 52.0 %collective-permute-start.24 = (bf16[768,896]{1,0:T(8,128)(2,1)}, bf16[768,896]{1,0:T(8,128)(2,1)}, u32[]{:S(2)}, u32[]{:S(2)}) collective-permute-start(bf16[768,896]{1,0:T(8,128)(2,1)} %add_convert_fusion.1), channel_id=1, source_target_pairs={{0,4},{4,0},{1,5},{5,1},{2,6},{6,2},{3,7},{7,3},{8,12},{12,8},{9,1... | collective-permute-start | bytes 4128776 | tf_op jit(solution)/shard_map/ppermute | solution.py:33
  316.8 40.4 %collective-permute-start.25 = (bf16[4,1120,128]{2,1,0:T(8,128)(2,1)}, bf16[4,1120,128]{2,1,0:T(8,128)(2,1)}, u32[]{:S(2)}, u32[]{:S(2)}) collective-permute-start(bf16[4,1120,128]{2,1,0:T(8,128)(2,1)} %bitcast.38), channel_id=1, source_target_pairs={{0,1},{1,0},{2,3},{3,2},{4,5},{5,4},{6,7},{7,6},{8,9},{9,8},{10,11... | collective-permute-start | bytes 3440648 | tf_op jit(solution)/shard_map/ppermute | solution.py:33
  317.1 51.1 %collective-permute-start.26 = (bf16[4,1120,128]{2,1,0:T(8,128)(2,1)}, bf16[4,1120,128]{2,1,0:T(8,128)(2,1)}, u32[]{:S(2)}, u32[]{:S(2)}) collective-permute-start(bf16[4,1120,128]{2,1,0:T(8,128)(2,1)} %bitcast.39), channel_id=1, source_target_pairs={{0,1},{1,0},{2,3},{3,2},{4,5},{5,4},{6,7},{7,6},{8,9},{9,8},{10,11... | collective-permute-start | bytes 3440648 | tf_op jit(solution)/shard_map/ppermute | solution.py:33
  322.5 53.2 %collective-permute-start.27 = (bf16[448,896]{1,0:T(8,128)(2,1)}, bf16[448,896]{1,0:T(8,128)(2,1)}, u32[]{:S(2)}, u32[]{:S(2)}) collective-permute-start(bf16[448,896]{1,0:T(8,128)(2,1)} %fusion.14), channel_id=1, source_target_pairs={{1,0},{2,3},{5,4},{6,7},{9,8},{10,11},{13,12},{14,15},{17,16},{18,... | collective-permute-start | bytes 2408456 | tf_op jit(solution)/shard_map/ppermute | solution.py:857
  382.6 30.4 %collective-permute-start.29 = (bf16[3360,128]{1,0:T(8,128)(2,1)}, bf16[3360,128]{1,0:T(8,128)(2,1)S(1)}, u32[]{:S(2)}, u32[]{:S(2)}) collective-permute-start(bf16[3360,128]{1,0:T(8,128)(2,1)} %get-tuple-element.234), channel_id=1, source_target_pairs={{0,8},{1,9},{2,10},{3,11},{4,12},{5,13},{6,14},{7,15}} | collective-permute-start | bytes 2580488 | tf_op jit(solution)/shard_map/ppermute | solution.py:543
  385.3 27.7 %collective-permute-start.30 = (bf16[3360,128]{1,0:T(8,128)(2,1)}, bf16[3360,128]{1,0:T(8,128)(2,1)}, u32[]{:S(2)}, u32[]{:S(2)}) collective-permute-start(bf16[3360,128]{1,0:T(8,128)(2,1)} %get-tuple-element.235), channel_id=1, source_target_pairs={{24,16},{25,17},{26,18},{27,19},{28,20},{29,21},{30,22},{31,23}} | collective-permute-start | bytes 2580488 | tf_op jit(solution)/shard_map/ppermute | solution.py:543
  386.9 26.0 %collective-permute-start.31 = (bf16[4,1,2,6,64,128]{5,4,3,2,1,0:T(8,128)(2,1)S(1)}, bf16[4,1,2,6,64,128]{5,4,3,2,1,0:T(8,128)(2,1)}, u32[]{:S(2)}, u32[]{:S(2)}) collective-permute-start(bf16[4,1,2,6,64,128]{5,4,3,2,1,0:T(8,128)(2,1)S(1)} %broadcast_select_fusion.3), channel_id=1, source_target_pairs={{0,4},{4,0},{1,5},{5,1},{2,6},{6,2},{3,7},{7,3},{8,12},{12,8},{9,1... | collective-permute-start | bytes 2359304 | tf_op jit(solution)/shard_map/ppermute | solution.py:33
  388.1 24.8 %collective-permute-start.32 = (bf16[224,448]{1,0:T(8,128)(2,1)}, bf16[224,448]{1,0:T(8,128)(2,1)}, u32[]{:S(2)}, u32[]{:S(2)}) collective-permute-start(bf16[224,448]{1,0:T(8,128)(2,1)} %broadcast_select_fusion.10), channel_id=1, source_target_pairs={{0,4},{4,0},{1,5},{5,1},{2,6},{6,2},{3,7},{7,3},{8,12},{12,8},{9,1... | collective-permute-start | bytes 602120 | tf_op jit(solution)/shard_map/ppermute | solution.py:33
  418.2 23.1 %collective-permute-start.33 = (bf16[3360,128]{1,0:T(8,128)(2,1)S(1)}, bf16[3360,128]{1,0:T(8,128)(2,1)S(1)}, u32[]{:S(2)}, u32[]{:S(2)}) collective-permute-start(bf16[3360,128]{1,0:T(8,128)(2,1)S(1)} %get-tuple-element.244), channel_id=1, source_target_pairs={{0,8},{8,16},{1,9},{9,17},{2,10},{10,18},{3,11},{11,19},{4,12},{12... | collective-permute-start | bytes 2580488 | tf_op jit(solution)/shard_map/ppermute | solution.py:543
  419.7 21.6 %collective-permute-start.34 = (bf16[3360,128]{1,0:T(8,128)(2,1)S(1)}, bf16[3360,128]{1,0:T(8,128)(2,1)S(1)}, u32[]{:S(2)}, u32[]{:S(2)}) collective-permute-start(bf16[3360,128]{1,0:T(8,128)(2,1)S(1)} %get-tuple-element.245), channel_id=1, source_target_pairs={{16,8},{24,16},{17,9},{25,17},{18,10},{26,18},{19,11},{27,19},{20,... | collective-permute-start | bytes 2580488 | tf_op jit(solution)/shard_map/ppermute | solution.py:543
  420.4 20.9 %collective-permute-start.35 = (bf16[4,1,2,6,64,128]{5,4,3,2,1,0:T(8,128)(2,1)S(1)}, bf16[4,1,2,6,64,128]{5,4,3,2,1,0:T(8,128)(2,1)S(1)}, u32[]{:S(2)}, u32[]{:S(2)}) collective-permute-start(bf16[4,1,2,6,64,128]{5,4,3,2,1,0:T(8,128)(2,1)S(1)} %broadcast_select_fusion.2), channel_id=1, source_target_pairs={{0,4},{4,0},{1,5},{5,1},{2,6},{6,2},{3,7},{7,3},{8,12},{12,8},{9,1... | collective-permute-start | bytes 2359304 | tf_op jit(solution)/shard_map/ppermute | solution.py:33
  421.7 19.6 %collective-permute-start.36 = (bf16[224,448]{1,0:T(8,128)(2,1)S(1)}, bf16[224,448]{1,0:T(8,128)(2,1)S(1)}, u32[]{:S(2)}, u32[]{:S(2)}) collective-permute-start(bf16[224,448]{1,0:T(8,128)(2,1)S(1)} %add_convert_fusion.15), channel_id=1, source_target_pairs={{0,8},{8,0},{16,24},{24,16},{1,9},{9,1},{17,25},{25,17},{2,10},{10... | collective-permute-start | bytes 602120 | tf_op jit(solution)/shard_map/ppermute | solution.py:638
  445.7 36.9 %collective-permute-start.37 = (bf16[3360,128]{1,0:T(8,128)(2,1)}, bf16[3360,128]{1,0:T(8,128)(2,1)}, u32[]{:S(2)}, u32[]{:S(2)}) collective-permute-start(bf16[3360,128]{1,0:T(8,128)(2,1)} %get-tuple-element.253), channel_id=1, source_target_pairs={{0,8},{8,16},{16,24},{1,9},{9,17},{17,25},{2,10},{10,18},{18,26},{... | collective-permute-start | bytes 2580488 | tf_op jit(solution)/shard_map/ppermute | solution.py:543
  450.8 31.8 %collective-permute-start.38 = (bf16[3360,128]{1,0:T(8,128)(2,1)}, bf16[3360,128]{1,0:T(8,128)(2,1)}, u32[]{:S(2)}, u32[]{:S(2)}) collective-permute-start(bf16[3360,128]{1,0:T(8,128)(2,1)} %get-tuple-element.254), channel_id=1, source_target_pairs={{8,0},{16,8},{24,16},{9,1},{17,9},{25,17},{10,2},{18,10},{26,18},{... | collective-permute-start | bytes 2580488 | tf_op jit(solution)/shard_map/ppermute | solution.py:543
  452.1 28.4 %collective-permute-start.42 = (bf16[224,448]{1,0:T(8,128)(2,1)S(1)}, bf16[224,448]{1,0:T(8,128)(2,1)S(1)}, u32[]{:S(2)}, u32[]{:S(2)}) collective-permute-start(bf16[224,448]{1,0:T(8,128)(2,1)S(1)} %add_convert_fusion.14), channel_id=1, source_target_pairs={{0,16},{8,24},{16,0},{24,8},{1,17},{9,25},{17,1},{25,9},{2,18},{10... | collective-permute-start | bytes 602120 | tf_op jit(solution)/shard_map/ppermute | solution.py:638
  454.5 28.1 %collective-permute-start.41 = (bf16[448,448]{1,0:T(8,128)(2,1)S(1)}, bf16[448,448]{1,0:T(8,128)(2,1)}, u32[]{:S(2)}, u32[]{:S(2)}) collective-permute-start(bf16[448,448]{1,0:T(8,128)(2,1)S(1)} %broadcast_select_fusion.4), channel_id=1, source_target_pairs={{0,1},{1,0},{2,3},{3,2},{4,5},{5,4},{6,7},{7,6},{8,9},{9,8},{10,11... | collective-permute-start | bytes 1204232 | tf_op jit(solution)/shard_map/ppermute | solution.py:33
  457.6 25.0 %collective-permute-start.39 = (bf16[1536,128]{1,0:T(8,128)(2,1)}, bf16[1536,128]{1,0:T(8,128)(2,1)}, u32[]{:S(2)}, u32[]{:S(2)}) collective-permute-start(bf16[1536,128]{1,0:T(8,128)(2,1)} %get-tuple-element.255), channel_id=1, source_target_pairs={{0,8},{1,9},{2,10},{3,11},{4,12},{5,13},{6,14},{7,15}} | collective-permute-start | bytes 1179656 | tf_op jit(solution)/shard_map/ppermute | solution.py:543
  491.1 10.4 %collective-permute-start.43 = (bf16[1536,128]{1,0:T(8,128)(2,1)}, bf16[1536,128]{1,0:T(8,128)(2,1)S(1)}, u32[]{:S(2)}, u32[]{:S(2)}) collective-permute-start(bf16[1536,128]{1,0:T(8,128)(2,1)} %get-tuple-element.265), channel_id=1, source_target_pairs={{0,8},{8,16},{1,9},{9,17},{2,10},{10,18},{3,11},{11,19},{4,12},{12... | collective-permute-start | bytes 1179656 | tf_op jit(solution)/shard_map/ppermute | solution.py:543
  501.9 53.4 %collective-permute-start.50 = (bf16[448,448]{1,0:T(8,128)(2,1)S(1)}, bf16[448,448]{1,0:T(8,128)(2,1)S(1)}, u32[]{:S(2)}, u32[]{:S(2)}) collective-permute-start(bf16[448,448]{1,0:T(8,128)(2,1)S(1)} %pad_maximum_fusion.20), channel_id=1, source_target_pairs={{0,2},{2,0},{1,3},{3,1},{4,6},{6,4},{5,7},{7,5},{8,10},{10,8},{9,1... | collective-permute-start | bytes 1204232 | tf_op jit(solution)/shard_map/ppermute | solution.py:33
  507.0 48.4 %collective-permute-start.47 = (bf16[1536,128]{1,0:T(8,128)(2,1)S(1)}, bf16[1536,128]{1,0:T(8,128)(2,1)S(1)}, u32[]{:S(2)}, u32[]{:S(2)}) collective-permute-start(bf16[1536,128]{1,0:T(8,128)(2,1)S(1)} %get-tuple-element.273), channel_id=1, source_target_pairs={{0,8},{8,16},{16,24},{1,9},{9,17},{17,25},{2,10},{10,18},{18,26},{... | collective-permute-start | bytes 1179656 | tf_op jit(solution)/shard_map/ppermute | solution.py:543
  518.3 37.1 %collective-permute-start.48 = (bf16[1536,128]{1,0:T(8,128)(2,1)S(1)}, bf16[1536,128]{1,0:T(8,128)(2,1)S(1)}, u32[]{:S(2)}, u32[]{:S(2)}) collective-permute-start(bf16[1536,128]{1,0:T(8,128)(2,1)S(1)} %get-tuple-element.274), channel_id=1, source_target_pairs={{8,0},{16,8},{24,16},{9,1},{17,9},{25,17},{10,2},{18,10},{26,18},{... | collective-permute-start | bytes 1179656 | tf_op jit(solution)/shard_map/ppermute | solution.py:543
  519.6 35.8 %collective-permute-start.49 = (bf16[224,448]{1,0:T(8,128)(2,1)S(1)}, bf16[224,448]{1,0:T(8,128)(2,1)S(1)}, u32[]{:S(2)}, u32[]{:S(2)}) collective-permute-start(bf16[224,448]{1,0:T(8,128)(2,1)S(1)} %add_convert_fusion.12), channel_id=1, source_target_pairs={{0,8},{8,0},{16,24},{24,16},{1,9},{9,1},{17,25},{25,17},{2,10},{10... | collective-permute-start | bytes 602120 | tf_op jit(solution)/shard_map/ppermute | solution.py:638
  567.8 15.0 %collective-permute-start.51 = (bf16[768,896]{1,0:T(8,128)(2,1)}, bf16[768,896]{1,0:T(8,128)(2,1)}, u32[]{:S(2)}, u32[]{:S(2)}) collective-permute-start(bf16[768,896]{1,0:T(8,128)(2,1)} %slice.344), channel_id=1, source_target_pairs={{0,2},{2,0},{1,3},{3,1},{4,6},{6,4},{5,7},{7,5},{8,10},{10,8},{9,1... | collective-permute-start | bytes 4128776 | tf_op jit(solution)/shard_map/ppermute | solution.py:33
  573.9 42.0 %collective-permute-start.59 = (bf16[224,448]{1,0:T(8,128)(2,1)S(1)}, bf16[224,448]{1,0:T(8,128)(2,1)}, u32[]{:S(2)}, u32[]{:S(2)}) collective-permute-start(bf16[224,448]{1,0:T(8,128)(2,1)S(1)} %add_convert_fusion.11), channel_id=1, source_target_pairs={{0,16},{8,24},{16,0},{24,8},{1,17},{9,25},{17,1},{25,9},{2,18},{10... | collective-permute-start | bytes 602120 | tf_op jit(solution)/shard_map/ppermute | solution.py:638
  586.4 10.6 %collective-permute-start.53 = (bf16[448,128]{1,0:T(8,128)(2,1)S(1)}, bf16[448,128]{1,0:T(8,128)(2,1)S(1)}, u32[]{:S(2)}, u32[]{:S(2)}) collective-permute-start(bf16[448,128]{1,0:T(8,128)(2,1)S(1)} %add_convert_fusion.19), channel_id=1, source_target_pairs={{0,8},{8,0},{16,24},{24,16},{1,9},{9,1},{17,25},{25,17},{2,10},{10... | collective-permute-start | bytes 344072 | tf_op jit(solution)/shard_map/ppermute | solution.py:638
  586.7 10.3 %collective-permute-start.54 = (f32[2944]{0:T(1024)S(1)}, f32[2944]{0:T(1024)S(1)}, u32[]{:S(2)}, u32[]{:S(2)}) collective-permute-start(f32[2944]{0:T(1024)S(1)} %concatenate.175), channel_id=1, source_target_pairs={{0,8},{8,0},{16,24},{24,16},{1,9},{9,1},{17,25},{25,17},{2,10},{10... | collective-permute-start | bytes 35336 | tf_op jit(solution)/shard_map/ppermute | solution.py:638
  597.1 17.0 %collective-permute-start.55 = (bf16[448,128]{1,0:T(8,128)(2,1)S(1)}, bf16[448,128]{1,0:T(8,128)(2,1)S(1)}, u32[]{:S(2)}, u32[]{:S(2)}) collective-permute-start(bf16[448,128]{1,0:T(8,128)(2,1)S(1)} %add_convert_fusion.18), channel_id=1, source_target_pairs={{0,16},{8,24},{16,0},{24,8},{1,17},{9,25},{17,1},{25,9},{2,18},{10... | collective-permute-start | bytes 344072 | tf_op jit(solution)/shard_map/ppermute | solution.py:638
  599.4 14.7 %collective-permute-start.56 = (f32[2944]{0:T(1024)S(1)}, f32[2944]{0:T(1024)S(1)}, u32[]{:S(2)}, u32[]{:S(2)}) collective-permute-start(f32[2944]{0:T(1024)S(1)} %add.281), channel_id=1, source_target_pairs={{0,16},{8,24},{16,0},{24,8},{1,17},{9,25},{17,1},{25,9},{2,18},{10... | collective-permute-start | bytes 35336 | tf_op jit(solution)/shard_map/ppermute | solution.py:638
  618.8 9.4 %collective-permute-start.60 = (bf16[448,128]{1,0:T(8,128)(2,1)S(1)}, bf16[448,128]{1,0:T(8,128)(2,1)S(1)}, u32[]{:S(2)}, u32[]{:S(2)}) collective-permute-start(bf16[448,128]{1,0:T(8,128)(2,1)S(1)} %add_convert_fusion.16), channel_id=1, source_target_pairs={{0,2},{2,0},{1,3},{3,1},{4,6},{6,4},{5,7},{7,5},{8,10},{10,8},{9,1... | collective-permute-start | bytes 344072 | tf_op jit(solution)/shard_map/ppermute | solution.py:33
  (85 other events, 719.8 us)
Sparse Core Ops, SparseCore 0:
  58.6 59.5 all-gather.3
  491.2 145.9 all-gather.5

commit v4 on v3

--- a/solution.py
+++ b/solution.py
@@ -42,8 +42,11 @@
     return rows * inverse * gain
 
 
-def project_kernel(x_ref, gain_ref, w_ref, b_ref, cos_ref, sin_ref, first_ref, q_ref, kv_ref):
-    rows = x_ref[...].astype(F32)
+def project_kernel(
+    own_ref, far_ref, gain_ref, w_ref, b_ref, cos_ref, sin_ref, first_ref, q_ref, kv_ref
+):
+    own = pl.program_id(0) < pl.num_programs(0) // 2
+    rows = jnp.where(own, own_ref[...].astype(F32), far_ref[...].astype(F32))
     first = rms_scale(rows, gain_ref[...]).astype(BF)
     first_ref[...] = first
     pre = dot(first, w_ref[...]) + b_ref[...]
@@ -60,17 +63,19 @@
     kv_ref[...] = jnp.concatenate([rot[:, Q_WIDTH:], pre[:, turned:]], axis=1).astype(BF)
 
 
-def project(rows, gain, weight, bias, cosine, sine):
-    count, width = rows.shape
+def project(own, far, gain, weight, bias, cosine, sine):
+    count, width = 2 * own.shape[0], own.shape[1]
     wide = weight.shape[1]
     step = 256
+    last = own.shape[0] // step - 1
     row_block = lambda n: pl.BlockSpec((step, n), lambda i: (i, 0))
     whole = lambda a, b: pl.BlockSpec((a, b), lambda i: (0, 0))
     return pl.pallas_call(
         project_kernel,
         grid=(count // step,),
         in_specs=[
-            row_block(width),
+            pl.BlockSpec((step, width), lambda i: (jnp.minimum(i, last), 0)),
+            pl.BlockSpec((step, width), lambda i: (jnp.maximum(i - last - 1, 0), 0)),
             whole(1, width),
             whole(width, wide),
             whole(1, wide),
@@ -87,7 +92,7 @@
         cost_estimate=pl.CostEstimate(
             flops=2 * count * width * wide, bytes_accessed=count * width * 4, transcendentals=0
         ),
-    )(rows, gain, weight, bias, cosine, sine)
+    )(own, far, gain, weight, bias, cosine, sine)
 
 
 def stack_heads(flat):
@@ -753,9 +758,8 @@
             return table.reshape(seqs, HALF, 2 * run)
 
         own_rows = tokens.reshape(rows, width)
-        chip_rows = jnp.concatenate([own_rows, tokens_far.reshape(rows, width)])
         first, q, kv = project(
-            chip_rows, fgain[None], qkv, bias, cos_wide, sin_wide
+            own_rows, tokens_far.reshape(rows, width), fgain[None], qkv, bias, cos_wide, sin_wide
         )
         q = q.reshape(2, seqs, run, Q_WIDTH)
         kv = kv.reshape(2, seqs, run, 2 * HEAD_DIM)

time: 673 us -> 670 us (level)
  transfers between devices with their start and end apart: 67 -> 67, of which waited for: 19 -> 20; matrix products, arithmetic and copies ran while one was open for 17% -> 17% of each run, Pallas kernels for 20% -> 20%
where the time goes in v4:
time: 670 us; the launch traced here: 661 us
  Pallas kernels  203 us (30%)
  waiting for transfers between devices  173 us (26%)
  starting transfers between devices  103 us (15%)
  other arithmetic  98 us (15%)
  local copies, waits for them, and re-layouts  50.3 us (8%)
  matrix products  17.6 us (3%)
  between operations  15.7 us (2%)
    ppermute x10, waiting for transfers between devices, exchange(): return lax.ppermute(values, axis, [(i, i ^ bit) for i in range(size)])  87.3 us
    pallas_call x3, Pallas kernels, attention(): pl.pallas_call(functools.partial(attend_back_kernel if back else attend_k...  77.5 us
    pallas_call x2, Pallas kernels, mlp(): pl.pallas_call(mlp_kernel, grid=(count // step,), in_specs=[row_block(wid...  60.7 us
    ppermute x37, waiting for transfers between devices, swap(): return lax.ppermute(values, axis, SWAP)  43.9 us
    ppermute x37, starting transfers between devices, swap(): return lax.ppermute(values, axis, SWAP)  42.5 us
    pallas_call x3, Pallas kernels, weight_grad(): pl.pallas_call(weight_grad_kernel, grid_spec=pltpu.PrefetchScalarGridSpec...  39.9 us
    ppermute x1, waiting for transfers between devices, body(): out_far = lax.ppermute(out_own, ('core', 'pair'), [(0, 1), (3, 2)])  37.6 us
    ppermute x6, starting transfers between devices, line_send(): lax.ppermute(load[0], axis, right)  26.1 us
  transfers between devices with their start and end apart: 67, of which 20 were waited for; matrix products, arithmetic and copies ran while one was open for 17% of the time, Pallas kernels for 20%

profile of v4, /device:TPU:1, one launch (start us, length us, event | category | flops | bytes accessed | tf_op | source)
XLA Modules:
  0.0 660.8 jit_solution(11195831774377541277)
XLA Ops:
  7.2 3.5 concatenate.139
  17.8 2.8 fusion.49
  46.7 9.1 %shard_map.254 = (bf16[1536,896]{1,0:T(8,128)(2,1)}, bf16[1536,448]{1,0:T(8,128)(2,1)}, bf16[1536,128]{1,0:T(8,128)(2,1)}) custom-call(bf16[768,896]{1,0:T(8,128)(2,1)} %bitcast.125, bf16[768,896]{1,0:T(8,128)(2,1)} %bitcast.14.far_ref, f32[1,896]{1,0:T(1,128)} %reshape.379.gain_ref, bf16[896,576]{1,0:T(8,128)(2,1)} %bitcast.153, ...), custom_call_target="tpu_custom_call" | custom-call | flops 1585446912 | bytes 5505024 | tf_op jit(solution)/shard_map/pallas_call | solution.py:73
  57.6 3.0 collective-permute-start.8
  60.6 37.6 %collective-permute-done.6 = bf16[448,896]{1,0:T(8,128)(2,1)} collective-permute-done((bf16[448,896]{1,0:T(8,128)(2,1)S(1)}, bf16[448,896]{1,0:T(8,128)(2,1)}, u32[]{:S(2)}, u32[]{:S(2)}) %collective-permute-start.6) | collective-permute-done | bytes 802848 | tf_op jit(solution)/shard_map/ppermute | solution.py:746
  103.4 12.9 %collective-permute-done.8 = bf16[1,448,1280]{2,1,0:T(8,128)(2,1)S(1)} collective-permute-done((bf16[1,448,1280]{2,1,0:T(8,128)(2,1)}, bf16[1,448,1280]{2,1,0:T(8,128)(2,1)S(1)}, u32[]{:S(2)}, u32[]{:S(2)}) %collective-permute-start.8) | collective-permute-done | bytes 1146912 | tf_op jit(solution)/shard_map/ppermute | solution.py:33
  118.7 28.4 %shard_map.255 = (bf16[2,12,64,448]{3,2,1,0:T(8,128)(2,1)}, f32[12,2,512]{2,1,0:T(2,128)}) custom-call(s32[12,32]{1,0:T(8,128)} %copy.72.starts_ref, s32[12,4]{1,0:T(8,128)} %copy.73.own_ref, bf16[2,12,64,448]{3,2,1,0:T(8,128)(2,1)} %bitcast.167, bf16[8,2,12,64,128]{4,3,2,1,0:T(8,128)(2,1)} %all-gather.4.cloned.1.call-done.kv_ref), custom_call_target="tpu_custom_call" | custom-call | flops 11274289152 | bytes 6291456 | tf_op jit(solution)/shard_map/pallas_call | solution.py:325
  147.7 3.2 convolution_convert_fusion.1
  165.0 3.2 pad_maximum_fusion.2.c_ref.b_near
  171.0 30.3 %shard_map.256 = (bf16[1536,1280]{1,0:T(8,128)(2,1)}, bf16[1536,1280]{1,0:T(8,128)(2,1)}, bf16[1536,1280]{1,0:T(8,128)(2,1)}, bf16[1536,896]{1,0:T(8,128)(2,1)}, bf16[1536,896]{1,0:T(8,128)(2,1)}) custom-call(bf16[1536,896]{1,0:T(8,128)(2,1)} %pad_maximum_fusion.1.s_ref.a_near, bf16[1536,896]{1,0:T(8,128)(2,1)} %pad_maximum_fusion.2.c_ref.b_near, ...), custom_call_target="tpu_custom_call" | custom-call | flops 21139292160 | bytes 22806528 | tf_op jit(solution)/shard_map/pallas_call | solution.py:369
  209.9 30.4 %shard_map.257 = (bf16[1536,1280]{1,0:T(8,128)(2,1)}, bf16[1536,1280]{1,0:T(8,128)(2,1)}, bf16[1536,1280]{1,0:T(8,128)(2,1)}, bf16[1536,896]{1,0:T(8,128)(2,1)}, bf16[1536,896]{1,0:T(8,128)(2,1)}) custom-call(bf16[1536,896]{1,0:T(8,128)(2,1)} %constant_dynamic-update-slice_fusion.s_ref.a_far, bf16[1536,896]{1,0:T(8,128)(2,1)} %copy-done.44, ...), custom_call_target="tpu_custom_call" | custom-call | flops 21139292160 | bytes 22806528 | tf_op jit(solution)/shard_map/pallas_call | solution.py:369
  246.6 13.7 %shard_map.258 = (bf16[1,4,1120,128]{3,2,1,0:T(8,128)(2,1)}, bf16[1,4,1120,128]{3,2,1,0:T(8,128)(2,1)}) custom-call(s32[1]{0:T(128)} %bitcast.27.pair_ref, bf16[1536,1280]{1,0:T(8,128)(2,1)} %get-tuple-element.183.a_near, bf16[1536,1280]{1,0:T(8,128)(2,1)} %get-tuple-element.193.a_far, bf16[1536,896]{1,0:T(8,128)(2,1)} %pad_maximum_fusion.2.c_ref.b_near, ...), custom_call_target="tpu_custom_call" | custom-call | flops 7046430720 | bytes 13369344 | tf_op jit(solution)/shard_map/pallas_call | solution.py:434
  265.5 13.2 %shard_map.259 = (bf16[1,4,1120,128]{3,2,1,0:T(8,128)(2,1)}, bf16[1,4,1120,128]{3,2,1,0:T(8,128)(2,1)}) custom-call(s32[1]{0:T(128)} %bitcast.27.pair_ref, bf16[1536,896]{1,0:T(8,128)(2,1)} %pad_maximum_fusion.1.s_ref.a_near, bf16[1536,896]{1,0:T(8,128)(2,1)} %constant_dynamic-update-slice_fusion.s_ref.a_far, bf16[1536,1280]{1,0:T(8,128)(2,1)} %get-tuple-element.201.b_near, ...), custom_call_target="tpu_custom_call" | custom-call | flops 7046430720 | bytes 13369344 | tf_op jit(solution)/shard_map/pallas_call | solution.py:434
  278.7 13.0 %shard_map.260 = (bf16[1,4,1120,128]{3,2,1,0:T(8,128)(2,1)}, bf16[1,4,1120,128]{3,2,1,0:T(8,128)(2,1)}) custom-call(s32[1]{0:T(128)} %bitcast.27.pair_ref, bf16[1536,896]{1,0:T(8,128)(2,1)} %pad_maximum_fusion.1.s_ref.a_near, bf16[1536,896]{1,0:T(8,128)(2,1)} %constant_dynamic-update-slice_fusion.s_ref.a_far, bf16[1536,1280]{1,0:T(8,128)(2,1)} %get-tuple-element.200.b_near, ...), custom_call_target="tpu_custom_call" | custom-call | flops 7046430720 | bytes 13369344 | tf_op jit(solution)/shard_map/pallas_call | solution.py:434
  291.8 4.6 collective-permute-done.19
  296.4 3.0 multiply_reduce_fusion
  299.4 4.9 fusion.46
  310.4 3.3 add_convert_fusion.1
  315.7 4.3 fusion.14
  320.0 3.2 collective-permute-start.27
  323.2 4.5 convolution_convert_fusion.2
  330.2 24.5 %shard_map.261 = (bf16[2,6,64,448]{3,2,1,0:T(8,128)(2,1)}, bf16[8,2,6,64,128]{4,3,2,1,0:T(8,128)(2,1)}) custom-call(s32[12,32]{1,0:T(8,128)} %copy.72.starts_ref, s32[12,4]{1,0:T(8,128)} %copy.73.own_ref, bf16[2,12,64,448]{3,2,1,0:T(8,128)(2,1)} %bitcast.168, bf16[8,2,12,64,128]{4,3,2,1,0:T(8,128)(2,1)} %all-gather.4.cloned.1.call-done.kv_ref, ...), custom_call_target="tpu_custom_call" | custom-call | flops 14092861440 | bytes 3145728 | tf_op jit(solution)/shard_map/pallas_call | solution.py:325
  354.7 11.0 %collective-permute-done.26 = bf16[4,1120,128]{2,1,0:T(8,128)(2,1)} collective-permute-done((bf16[4,1120,128]{2,1,0:T(8,128)(2,1)}, bf16[4,1120,128]{2,1,0:T(8,128)(2,1)}, u32[]{:S(2)}, u32[]{:S(2)}) %collective-permute-start.26) | collective-permute-done | bytes 1146912 | tf_op jit(solution)/shard_map/ppermute | solution.py:33
  385.8 24.6 %shard_map.262 = (bf16[2,6,64,448]{3,2,1,0:T(8,128)(2,1)}, bf16[8,2,6,64,128]{4,3,2,1,0:T(8,128)(2,1)}) custom-call(s32[12,32]{1,0:T(8,128)} %copy.72.starts_ref, s32[12,4]{1,0:T(8,128)} %copy.73.own_ref, bf16[2,12,64,448]{3,2,1,0:T(8,128)(2,1)} %bitcast.169, bf16[8,2,12,64,128]{4,3,2,1,0:T(8,128)(2,1)} %all-gather.4.cloned.1.call-done.kv_ref, ...), custom_call_target="tpu_custom_call" | custom-call | flops 14092861440 | bytes 3145728 | tf_op jit(solution)/shard_map/pallas_call | solution.py:325
  425.2 13.6 %collective-permute-done.36 = bf16[224,448]{1,0:T(8,128)(2,1)S(1)} collective-permute-done((bf16[224,448]{1,0:T(8,128)(2,1)S(1)}, bf16[224,448]{1,0:T(8,128)(2,1)S(1)}, u32[]{:S(2)}, u32[]{:S(2)}) %collective-permute-start.36) | collective-permute-done | bytes 200736 | tf_op jit(solution)/shard_map/ppermute | solution.py:643
  443.3 5.0 collective-permute-start.37
  452.1 2.9 collective-permute-start.41
  455.0 3.6 collective-permute-start.39
  458.6 19.5 %collective-permute-done.42 = bf16[224,448]{1,0:T(8,128)(2,1)S(1)} collective-permute-done((bf16[224,448]{1,0:T(8,128)(2,1)S(1)}, bf16[224,448]{1,0:T(8,128)(2,1)S(1)}, u32[]{:S(2)}, u32[]{:S(2)}) %collective-permute-start.42) | collective-permute-done | bytes 200736 | tf_op jit(solution)/shard_map/ppermute | solution.py:643
  485.8 2.9 fusion.11
  492.4 3.6 collective-permute-done.45
  496.0 3.1 collective-permute-done.46
  499.6 5.0 collective-permute-start.50
  504.6 11.9 %collective-permute-start.47 = (bf16[1536,128]{1,0:T(8,128)(2,1)S(1)}, bf16[1536,128]{1,0:T(8,128)(2,1)S(1)}, u32[]{:S(2)}, u32[]{:S(2)}) collective-permute-start(bf16[1536,128]{1,0:T(8,128)(2,1)S(1)} %get-tuple-element.273), channel_id=1, source_target_pairs={{0,8},{8,16},{16,24},{1,9},{9,17},{17,25},{2,10},{10,18},{18,26},{... | collective-permute-start | bytes 1179656 | tf_op jit(solution)/shard_map/ppermute | solution.py:548
  517.8 5.3 collective-permute-start.49
  523.5 29.4 %collective-permute-done.49 = bf16[224,448]{1,0:T(8,128)(2,1)S(1)} collective-permute-done((bf16[224,448]{1,0:T(8,128)(2,1)S(1)}, bf16[224,448]{1,0:T(8,128)(2,1)S(1)}, u32[]{:S(2)}, u32[]{:S(2)}) %collective-permute-start.49) | collective-permute-done | bytes 200736 | tf_op jit(solution)/shard_map/ppermute | solution.py:643
  553.3 3.9 fusion.21
  557.2 2.8 convolution_convert_fusion
  567.3 4.0 add_convert_fusion
  571.7 5.0 collective-permute-start.52
  585.6 8.7 %collective-permute-done.54 = f32[2944]{0:T(1024)S(1)} collective-permute-done((f32[2944]{0:T(1024)S(1)}, f32[2944]{0:T(1024)S(1)}, u32[]{:S(2)}, u32[]{:S(2)}) %collective-permute-start.54) | collective-permute-done | bytes 11808 | tf_op jit(solution)/shard_map/ppermute | solution.py:643
  598.3 13.2 %collective-permute-done.56 = f32[2944]{0:T(1024)S(1)} collective-permute-done((f32[2944]{0:T(1024)S(1)}, f32[2944]{0:T(1024)S(1)}, u32[]{:S(2)}, u32[]{:S(2)}) %collective-permute-start.56) | collective-permute-done | bytes 11808 | tf_op jit(solution)/shard_map/ppermute | solution.py:643
  613.3 2.9 collective-permute-done.58
  616.2 3.4 collective-permute-start.60
  621.7 3.9 fusion.1
  628.0 3.2 collective-permute-start.64
  637.3 9.8 %shard_map.263 = (f32[448,4864]{1,0:T(8,128)}, f32[448,4864]{1,0:T(8,128)}) custom-call(bf16[4,4,3,1120,128]{4,3,2,1,0:T(8,128)(2,1)} %bitcast.122, bf16[4,4,3,1120,128]{4,3,2,1,0:T(8,128)(2,1)} %bitcast.123), custom_call_target="tpu_custom_call" | custom-call | tf_op jit(solution)/shard_map/pallas_call | solution.py:502
  647.1 6.4 shard_map.264
  (378 shorter events, 180.0 us)
Async XLA Ops:
  7.2 109.2 %all-gather.4.cloned.1.call-start = ((), (), s32[]{:S(2)}) async-start(), calls=%async_computation | async-start | bytes 3538944 | tf_op jit(solution)/shard_map/all_gather | solution.py:618
  14.8 25.0 %collective-permute-start = (bf16[1,464,576]{1,2,0:T(8,128)(2,1)}, bf16[1,464,576]{1,2,0:T(8,128)(2,1)}, u32[]{:S(2)}, u32[]{:S(2)}) collective-permute-start(bf16[1,464,576]{1,2,0:T(8,128)(2,1)} %copy.65), channel_id=1, source_target_pairs={{0,1},{1,0},{2,3},{3,2},{4,5},{5,4},{6,7},{7,6},{8,9},{9,8},{10,11... | collective-permute-start | bytes 1603592 | tf_op jit(solution)/shard_map/ppermute | solution.py:33
  16.8 10.2 %collective-permute-start.1 = (s32[12,64]{1,0:T(8,128)S(1)}, s32[12,64]{1,0:T(8,128)S(1)}, u32[]{:S(2)}, u32[]{:S(2)}) collective-permute-start(s32[12,64]{1,0:T(8,128)S(1)} %copy-done.58), channel_id=1, source_target_pairs={{0,2},{2,0},{1,3},{3,1},{4,6},{6,4},{5,7},{7,5},{8,10},{10,8},{9,1... | collective-permute-start | bytes 9224 | tf_op jit(solution)/shard_map/ppermute | solution.py:33
  17.8 29.0 %collective-permute-start.5 = (bf16[12,64,896]{2,1,0:T(8,128)(2,1)S(1)}, bf16[12,64,896]{2,1,0:T(8,128)(2,1)}, u32[]{:S(2)}, u32[]{:S(2)}) collective-permute-start(bf16[12,64,896]{2,1,0:T(8,128)(2,1)S(1)} %copy-done.1), channel_id=1, source_target_pairs={{0,2},{2,0},{1,3},{3,1},{4,6},{6,4},{5,7},{7,5},{8,10},{10,8},{9,1... | collective-permute-start | bytes 4128776 | tf_op jit(solution)/shard_map/ppermute | solution.py:33
  55.8 581.5 %all-gather.6.cloned.1.call-start = ((), (), s32[]{:S(2)}) async-start(), calls=%async_computation.1 | async-start | bytes 14622720 | tf_op jit(solution)/shard_map/all_gather | solution.py:1004
  55.9 44.5 %collective-permute-start.7 = (bf16[1,640,896]{2,1,0:T(8,128)(2,1)S(1)}, bf16[1,640,896]{2,1,0:T(8,128)(2,1)}, u32[]{:S(2)}, u32[]{:S(2)}) collective-permute-start(bf16[1,640,896]{2,1,0:T(8,128)(2,1)S(1)} %bitcast.141), channel_id=1, source_target_pairs={{0,1},{1,0},{2,3},{3,2},{4,5},{5,4},{6,7},{7,6},{8,9},{9,8},{10,11... | collective-permute-start | bytes 3440648 | tf_op jit(solution)/shard_map/ppermute | solution.py:33
  56.2 42.1 %collective-permute-start.6 = (bf16[448,896]{1,0:T(8,128)(2,1)S(1)}, bf16[448,896]{1,0:T(8,128)(2,1)}, u32[]{:S(2)}, u32[]{:S(2)}) collective-permute-start(bf16[448,896]{1,0:T(8,128)(2,1)S(1)} %copy-done.40), channel_id=1, source_target_pairs={{0,1},{3,2},{4,5},{7,6},{8,9},{11,10},{12,13},{15,14},{16,17},{19,... | collective-permute-start | bytes 2408456 | tf_op jit(solution)/shard_map/ppermute | solution.py:746
  57.6 58.7 %collective-permute-start.8 = (bf16[1,448,1280]{2,1,0:T(8,128)(2,1)}, bf16[1,448,1280]{2,1,0:T(8,128)(2,1)S(1)}, u32[]{:S(2)}, u32[]{:S(2)}) collective-permute-start(bf16[1,448,1280]{2,1,0:T(8,128)(2,1)} %bitcast.23), channel_id=1, source_target_pairs={{0,1},{1,0},{2,3},{3,2},{4,5},{5,4},{6,7},{7,6},{8,9},{9,8},{10,11... | collective-permute-start | bytes 3440648 | tf_op jit(solution)/shard_map/ppermute | solution.py:33
  116.3 31.3 %collective-permute-start.10 = (bf16[768,896]{1,0:T(8,128)(2,1)}, bf16[768,896]{1,0:T(8,128)(2,1)}, u32[]{:S(2)}, u32[]{:S(2)}) collective-permute-start(bf16[768,896]{1,0:T(8,128)(2,1)} %bitcast.26), channel_id=1, source_target_pairs={{0,4},{4,0},{1,5},{5,1},{2,6},{6,2},{3,7},{7,3},{8,12},{12,8},{9,1... | collective-permute-start | bytes 4128776 | tf_op jit(solution)/shard_map/ppermute | solution.py:33
  117.3 29.8 %collective-permute-start.9 = (bf16[1,448,1280]{2,1,0:T(8,128)(2,1)S(1)}, bf16[1,448,1280]{2,1,0:T(8,128)(2,1)}, u32[]{:S(2)}, u32[]{:S(2)}) collective-permute-start(bf16[1,448,1280]{2,1,0:T(8,128)(2,1)S(1)} %bitcast.142), channel_id=1, source_target_pairs={{0,1},{1,0},{2,3},{3,2},{4,5},{5,4},{6,7},{7,6},{8,9},{9,8},{10,11... | collective-permute-start | bytes 3440648 | tf_op jit(solution)/shard_map/ppermute | solution.py:33
  154.9 10.1 %collective-permute-start.14 = (bf16[768,896]{1,0:T(8,128)(2,1)}, bf16[768,896]{1,0:T(8,128)(2,1)S(1)}, u32[]{:S(2)}, u32[]{:S(2)}) collective-permute-start(bf16[768,896]{1,0:T(8,128)(2,1)} %bitcast.26), channel_id=1, source_target_pairs={{0,2},{2,0},{1,3},{3,1},{4,6},{6,4},{5,7},{7,5},{8,10},{10,8},{9,1... | collective-permute-start | bytes 4128776 | tf_op jit(solution)/shard_map/ppermute | solution.py:33
  159.8 9.4 %collective-permute-start.13 = (bf16[768,896]{1,0:T(8,128)(2,1)S(1)}, bf16[768,896]{1,0:T(8,128)(2,1)S(1)}, u32[]{:S(2)}, u32[]{:S(2)}) collective-permute-start(bf16[768,896]{1,0:T(8,128)(2,1)S(1)} %multiply_convert_fusion), channel_id=1, source_target_pairs={{0,2},{2,0},{1,3},{3,1},{4,6},{6,4},{5,7},{7,5},{8,10},{10,8},{9,1... | collective-permute-start | bytes 4128776 | tf_op jit(solution)/shard_map/ppermute | solution.py:33
  162.0 43.1 %collective-permute-start.17 = (bf16[768,896]{1,0:T(8,128)(2,1)}, bf16[768,896]{1,0:T(8,128)(2,1)}, u32[]{:S(2)}, u32[]{:S(2)}) collective-permute-start(bf16[768,896]{1,0:T(8,128)(2,1)} %collective-permute-done.10), channel_id=1, source_target_pairs={{0,2},{2,0},{1,3},{3,1},{4,6},{6,4},{5,7},{7,5},{8,10},{10,8},{9,1... | collective-permute-start | bytes 4128776 | tf_op jit(solution)/shard_map/ppermute | solution.py:33
  168.2 33.1 %collective-permute-start.12 = (bf16[768,896]{1,0:T(8,128)(2,1)S(1)}, bf16[768,896]{1,0:T(8,128)(2,1)S(1)}, u32[]{:S(2)}, u32[]{:S(2)}) collective-permute-start(bf16[768,896]{1,0:T(8,128)(2,1)S(1)} %multiply_convert_fusion), channel_id=1, source_target_pairs={{0,4},{4,0},{1,5},{5,1},{2,6},{6,2},{3,7},{7,3},{8,12},{12,8},{9,1... | collective-permute-start | bytes 4128776 | tf_op jit(solution)/shard_map/ppermute | solution.py:33
  263.0 28.8 %collective-permute-start.21 = (bf16[768,896]{1,0:T(8,128)(2,1)}, bf16[768,896]{1,0:T(8,128)(2,1)}, u32[]{:S(2)}, u32[]{:S(2)}) collective-permute-start(bf16[768,896]{1,0:T(8,128)(2,1)} %slice.286), channel_id=1, source_target_pairs={{0,2},{2,0},{1,3},{3,1},{4,6},{6,4},{5,7},{7,5},{8,10},{10,8},{9,1... | collective-permute-start | bytes 4128776 | tf_op jit(solution)/shard_map/ppermute | solution.py:33
  264.5 27.2 %collective-permute-start.22 = (bf16[768,896]{1,0:T(8,128)(2,1)}, bf16[768,896]{1,0:T(8,128)(2,1)}, u32[]{:S(2)}, u32[]{:S(2)}) collective-permute-start(bf16[768,896]{1,0:T(8,128)(2,1)} %slice.287), channel_id=1, source_target_pairs={{0,2},{2,0},{1,3},{3,1},{4,6},{6,4},{5,7},{7,5},{8,10},{10,8},{9,1... | collective-permute-start | bytes 4128776 | tf_op jit(solution)/shard_map/ppermute | solution.py:33
  264.7 31.7 %collective-permute-start.19 = (bf16[768,896]{1,0:T(8,128)(2,1)}, bf16[768,896]{1,0:T(8,128)(2,1)}, u32[]{:S(2)}, u32[]{:S(2)}) collective-permute-start(bf16[768,896]{1,0:T(8,128)(2,1)} %add_convert_fusion.2), channel_id=1, source_target_pairs={{0,4},{4,0},{1,5},{5,1},{2,6},{6,2},{3,7},{7,3},{8,12},{12,8},{9,1... | collective-permute-start | bytes 4128776 | tf_op jit(solution)/shard_map/ppermute | solution.py:33
  265.2 26.6 %collective-permute-start.20 = (bf16[4,1120,128]{2,1,0:T(8,128)(2,1)}, bf16[4,1120,128]{2,1,0:T(8,128)(2,1)}, u32[]{:S(2)}, u32[]{:S(2)}) collective-permute-start(bf16[4,1120,128]{2,1,0:T(8,128)(2,1)} %bitcast.35), channel_id=1, source_target_pairs={{0,1},{1,0},{2,3},{3,2},{4,5},{5,4},{6,7},{7,6},{8,9},{9,8},{10,11... | collective-permute-start | bytes 3440648 | tf_op jit(solution)/shard_map/ppermute | solution.py:33
  304.3 11.4 %collective-permute-start.23 = (bf16[768,896]{1,0:T(8,128)(2,1)}, bf16[768,896]{1,0:T(8,128)(2,1)}, u32[]{:S(2)}, u32[]{:S(2)}) collective-permute-start(bf16[768,896]{1,0:T(8,128)(2,1)} %get-tuple-element.312), channel_id=1, source_target_pairs={{0,2},{2,0},{1,3},{3,1},{4,6},{6,4},{5,7},{7,5},{8,10},{10,8},{9,1... | collective-permute-start | bytes 4128776 | tf_op jit(solution)/shard_map/ppermute | solution.py:33
  313.7 52.0 %collective-permute-start.24 = (bf16[768,896]{1,0:T(8,128)(2,1)}, bf16[768,896]{1,0:T(8,128)(2,1)}, u32[]{:S(2)}, u32[]{:S(2)}) collective-permute-start(bf16[768,896]{1,0:T(8,128)(2,1)} %add_convert_fusion.1), channel_id=1, source_target_pairs={{0,4},{4,0},{1,5},{5,1},{2,6},{6,2},{3,7},{7,3},{8,12},{12,8},{9,1... | collective-permute-start | bytes 4128776 | tf_op jit(solution)/shard_map/ppermute | solution.py:33
  314.2 40.5 %collective-permute-start.25 = (bf16[4,1120,128]{2,1,0:T(8,128)(2,1)}, bf16[4,1120,128]{2,1,0:T(8,128)(2,1)}, u32[]{:S(2)}, u32[]{:S(2)}) collective-permute-start(bf16[4,1120,128]{2,1,0:T(8,128)(2,1)} %bitcast.38), channel_id=1, source_target_pairs={{0,1},{1,0},{2,3},{3,2},{4,5},{5,4},{6,7},{7,6},{8,9},{9,8},{10,11... | collective-permute-start | bytes 3440648 | tf_op jit(solution)/shard_map/ppermute | solution.py:33
  314.6 51.1 %collective-permute-start.26 = (bf16[4,1120,128]{2,1,0:T(8,128)(2,1)}, bf16[4,1120,128]{2,1,0:T(8,128)(2,1)}, u32[]{:S(2)}, u32[]{:S(2)}) collective-permute-start(bf16[4,1120,128]{2,1,0:T(8,128)(2,1)} %bitcast.39), channel_id=1, source_target_pairs={{0,1},{1,0},{2,3},{3,2},{4,5},{5,4},{6,7},{7,6},{8,9},{9,8},{10,11... | collective-permute-start | bytes 3440648 | tf_op jit(solution)/shard_map/ppermute | solution.py:33
  320.0 53.2 %collective-permute-start.27 = (bf16[448,896]{1,0:T(8,128)(2,1)}, bf16[448,896]{1,0:T(8,128)(2,1)}, u32[]{:S(2)}, u32[]{:S(2)}) collective-permute-start(bf16[448,896]{1,0:T(8,128)(2,1)} %fusion.14), channel_id=1, source_target_pairs={{1,0},{2,3},{5,4},{6,7},{9,8},{10,11},{13,12},{14,15},{17,16},{18,... | collective-permute-start | bytes 2408456 | tf_op jit(solution)/shard_map/ppermute | solution.py:861
  380.0 30.4 %collective-permute-start.29 = (bf16[3360,128]{1,0:T(8,128)(2,1)}, bf16[3360,128]{1,0:T(8,128)(2,1)S(1)}, u32[]{:S(2)}, u32[]{:S(2)}) collective-permute-start(bf16[3360,128]{1,0:T(8,128)(2,1)} %get-tuple-element.234), channel_id=1, source_target_pairs={{0,8},{1,9},{2,10},{3,11},{4,12},{5,13},{6,14},{7,15}} | collective-permute-start | bytes 2580488 | tf_op jit(solution)/shard_map/ppermute | solution.py:548
  382.7 27.7 %collective-permute-start.30 = (bf16[3360,128]{1,0:T(8,128)(2,1)}, bf16[3360,128]{1,0:T(8,128)(2,1)}, u32[]{:S(2)}, u32[]{:S(2)}) collective-permute-start(bf16[3360,128]{1,0:T(8,128)(2,1)} %get-tuple-element.235), channel_id=1, source_target_pairs={{24,16},{25,17},{26,18},{27,19},{28,20},{29,21},{30,22},{31,23}} | collective-permute-start | bytes 2580488 | tf_op jit(solution)/shard_map/ppermute | solution.py:548
  384.3 26.0 %collective-permute-start.31 = (bf16[4,1,2,6,64,128]{5,4,3,2,1,0:T(8,128)(2,1)S(1)}, bf16[4,1,2,6,64,128]{5,4,3,2,1,0:T(8,128)(2,1)}, u32[]{:S(2)}, u32[]{:S(2)}) collective-permute-start(bf16[4,1,2,6,64,128]{5,4,3,2,1,0:T(8,128)(2,1)S(1)} %broadcast_select_fusion.3), channel_id=1, source_target_pairs={{0,4},{4,0},{1,5},{5,1},{2,6},{6,2},{3,7},{7,3},{8,12},{12,8},{9,1... | collective-permute-start | bytes 2359304 | tf_op jit(solution)/shard_map/ppermute | solution.py:33
  385.5 24.8 %collective-permute-start.32 = (bf16[224,448]{1,0:T(8,128)(2,1)}, bf16[224,448]{1,0:T(8,128)(2,1)}, u32[]{:S(2)}, u32[]{:S(2)}) collective-permute-start(bf16[224,448]{1,0:T(8,128)(2,1)} %broadcast_select_fusion.10), channel_id=1, source_target_pairs={{0,4},{4,0},{1,5},{5,1},{2,6},{6,2},{3,7},{7,3},{8,12},{12,8},{9,1... | collective-permute-start | bytes 602120 | tf_op jit(solution)/shard_map/ppermute | solution.py:33
  415.6 23.2 %collective-permute-start.33 = (bf16[3360,128]{1,0:T(8,128)(2,1)S(1)}, bf16[3360,128]{1,0:T(8,128)(2,1)S(1)}, u32[]{:S(2)}, u32[]{:S(2)}) collective-permute-start(bf16[3360,128]{1,0:T(8,128)(2,1)S(1)} %get-tuple-element.244), channel_id=1, source_target_pairs={{0,8},{8,16},{1,9},{9,17},{2,10},{10,18},{3,11},{11,19},{4,12},{12... | collective-permute-start | bytes 2580488 | tf_op jit(solution)/shard_map/ppermute | solution.py:548
  417.1 21.7 %collective-permute-start.34 = (bf16[3360,128]{1,0:T(8,128)(2,1)S(1)}, bf16[3360,128]{1,0:T(8,128)(2,1)S(1)}, u32[]{:S(2)}, u32[]{:S(2)}) collective-permute-start(bf16[3360,128]{1,0:T(8,128)(2,1)S(1)} %get-tuple-element.245), channel_id=1, source_target_pairs={{16,8},{24,16},{17,9},{25,17},{18,10},{26,18},{19,11},{27,19},{20,... | collective-permute-start | bytes 2580488 | tf_op jit(solution)/shard_map/ppermute | solution.py:548
  417.8 21.0 %collective-permute-start.35 = (bf16[4,1,2,6,64,128]{5,4,3,2,1,0:T(8,128)(2,1)S(1)}, bf16[4,1,2,6,64,128]{5,4,3,2,1,0:T(8,128)(2,1)S(1)}, u32[]{:S(2)}, u32[]{:S(2)}) collective-permute-start(bf16[4,1,2,6,64,128]{5,4,3,2,1,0:T(8,128)(2,1)S(1)} %broadcast_select_fusion.2), channel_id=1, source_target_pairs={{0,4},{4,0},{1,5},{5,1},{2,6},{6,2},{3,7},{7,3},{8,12},{12,8},{9,1... | collective-permute-start | bytes 2359304 | tf_op jit(solution)/shard_map/ppermute | solution.py:33
  419.1 19.7 %collective-permute-start.36 = (bf16[224,448]{1,0:T(8,128)(2,1)S(1)}, bf16[224,448]{1,0:T(8,128)(2,1)S(1)}, u32[]{:S(2)}, u32[]{:S(2)}) collective-permute-start(bf16[224,448]{1,0:T(8,128)(2,1)S(1)} %add_convert_fusion.15), channel_id=1, source_target_pairs={{0,8},{8,0},{16,24},{24,16},{1,9},{9,1},{17,25},{25,17},{2,10},{10... | collective-permute-start | bytes 602120 | tf_op jit(solution)/shard_map/ppermute | solution.py:643
  443.3 37.0 %collective-permute-start.37 = (bf16[3360,128]{1,0:T(8,128)(2,1)}, bf16[3360,128]{1,0:T(8,128)(2,1)}, u32[]{:S(2)}, u32[]{:S(2)}) collective-permute-start(bf16[3360,128]{1,0:T(8,128)(2,1)} %get-tuple-element.253), channel_id=1, source_target_pairs={{0,8},{8,16},{16,24},{1,9},{9,17},{17,25},{2,10},{10,18},{18,26},{... | collective-permute-start | bytes 2580488 | tf_op jit(solution)/shard_map/ppermute | solution.py:548
  448.3 32.0 %collective-permute-start.38 = (bf16[3360,128]{1,0:T(8,128)(2,1)}, bf16[3360,128]{1,0:T(8,128)(2,1)}, u32[]{:S(2)}, u32[]{:S(2)}) collective-permute-start(bf16[3360,128]{1,0:T(8,128)(2,1)} %get-tuple-element.254), channel_id=1, source_target_pairs={{8,0},{16,8},{24,16},{9,1},{17,9},{25,17},{10,2},{18,10},{26,18},{... | collective-permute-start | bytes 2580488 | tf_op jit(solution)/shard_map/ppermute | solution.py:548
  449.6 28.5 %collective-permute-start.42 = (bf16[224,448]{1,0:T(8,128)(2,1)S(1)}, bf16[224,448]{1,0:T(8,128)(2,1)S(1)}, u32[]{:S(2)}, u32[]{:S(2)}) collective-permute-start(bf16[224,448]{1,0:T(8,128)(2,1)S(1)} %add_convert_fusion.14), channel_id=1, source_target_pairs={{0,16},{8,24},{16,0},{24,8},{1,17},{9,25},{17,1},{25,9},{2,18},{10... | collective-permute-start | bytes 602120 | tf_op jit(solution)/shard_map/ppermute | solution.py:643
  452.1 28.2 %collective-permute-start.41 = (bf16[448,448]{1,0:T(8,128)(2,1)S(1)}, bf16[448,448]{1,0:T(8,128)(2,1)}, u32[]{:S(2)}, u32[]{:S(2)}) collective-permute-start(bf16[448,448]{1,0:T(8,128)(2,1)S(1)} %broadcast_select_fusion.4), channel_id=1, source_target_pairs={{0,1},{1,0},{2,3},{3,2},{4,5},{5,4},{6,7},{7,6},{8,9},{9,8},{10,11... | collective-permute-start | bytes 1204232 | tf_op jit(solution)/shard_map/ppermute | solution.py:33
  455.0 25.2 %collective-permute-start.39 = (bf16[1536,128]{1,0:T(8,128)(2,1)}, bf16[1536,128]{1,0:T(8,128)(2,1)}, u32[]{:S(2)}, u32[]{:S(2)}) collective-permute-start(bf16[1536,128]{1,0:T(8,128)(2,1)} %get-tuple-element.255), channel_id=1, source_target_pairs={{0,8},{1,9},{2,10},{3,11},{4,12},{5,13},{6,14},{7,15}} | collective-permute-start | bytes 1179656 | tf_op jit(solution)/shard_map/ppermute | solution.py:548
  488.7 10.4 %collective-permute-start.43 = (bf16[1536,128]{1,0:T(8,128)(2,1)}, bf16[1536,128]{1,0:T(8,128)(2,1)S(1)}, u32[]{:S(2)}, u32[]{:S(2)}) collective-permute-start(bf16[1536,128]{1,0:T(8,128)(2,1)} %get-tuple-element.265), channel_id=1, source_target_pairs={{0,8},{8,16},{1,9},{9,17},{2,10},{10,18},{3,11},{11,19},{4,12},{12... | collective-permute-start | bytes 1179656 | tf_op jit(solution)/shard_map/ppermute | solution.py:548
  499.6 53.3 %collective-permute-start.50 = (bf16[448,448]{1,0:T(8,128)(2,1)S(1)}, bf16[448,448]{1,0:T(8,128)(2,1)S(1)}, u32[]{:S(2)}, u32[]{:S(2)}) collective-permute-start(bf16[448,448]{1,0:T(8,128)(2,1)S(1)} %pad_maximum_fusion.19), channel_id=1, source_target_pairs={{0,2},{2,0},{1,3},{3,1},{4,6},{6,4},{5,7},{7,5},{8,10},{10,8},{9,1... | collective-permute-start | bytes 1204232 | tf_op jit(solution)/shard_map/ppermute | solution.py:33
  504.6 48.3 %collective-permute-start.47 = (bf16[1536,128]{1,0:T(8,128)(2,1)S(1)}, bf16[1536,128]{1,0:T(8,128)(2,1)S(1)}, u32[]{:S(2)}, u32[]{:S(2)}) collective-permute-start(bf16[1536,128]{1,0:T(8,128)(2,1)S(1)} %get-tuple-element.273), channel_id=1, source_target_pairs={{0,8},{8,16},{16,24},{1,9},{9,17},{17,25},{2,10},{10,18},{18,26},{... | collective-permute-start | bytes 1179656 | tf_op jit(solution)/shard_map/ppermute | solution.py:548
  516.5 36.4 %collective-permute-start.48 = (bf16[1536,128]{1,0:T(8,128)(2,1)S(1)}, bf16[1536,128]{1,0:T(8,128)(2,1)S(1)}, u32[]{:S(2)}, u32[]{:S(2)}) collective-permute-start(bf16[1536,128]{1,0:T(8,128)(2,1)S(1)} %get-tuple-element.274), channel_id=1, source_target_pairs={{8,0},{16,8},{24,16},{9,1},{17,9},{25,17},{10,2},{18,10},{26,18},{... | collective-permute-start | bytes 1179656 | tf_op jit(solution)/shard_map/ppermute | solution.py:548
  517.8 35.1 %collective-permute-start.49 = (bf16[224,448]{1,0:T(8,128)(2,1)S(1)}, bf16[224,448]{1,0:T(8,128)(2,1)S(1)}, u32[]{:S(2)}, u32[]{:S(2)}) collective-permute-start(bf16[224,448]{1,0:T(8,128)(2,1)S(1)} %add_convert_fusion.12), channel_id=1, source_target_pairs={{0,8},{8,0},{16,24},{24,16},{1,9},{9,1},{17,25},{25,17},{2,10},{10... | collective-permute-start | bytes 602120 | tf_op jit(solution)/shard_map/ppermute | solution.py:643
  565.3 14.8 %collective-permute-start.51 = (bf16[768,896]{1,0:T(8,128)(2,1)}, bf16[768,896]{1,0:T(8,128)(2,1)}, u32[]{:S(2)}, u32[]{:S(2)}) collective-permute-start(bf16[768,896]{1,0:T(8,128)(2,1)} %slice.344), channel_id=1, source_target_pairs={{0,2},{2,0},{1,3},{3,1},{4,6},{6,4},{5,7},{7,5},{8,10},{10,8},{9,1... | collective-permute-start | bytes 4128776 | tf_op jit(solution)/shard_map/ppermute | solution.py:33
  571.3 42.0 %collective-permute-start.59 = (bf16[224,448]{1,0:T(8,128)(2,1)S(1)}, bf16[224,448]{1,0:T(8,128)(2,1)}, u32[]{:S(2)}, u32[]{:S(2)}) collective-permute-start(bf16[224,448]{1,0:T(8,128)(2,1)S(1)} %add_convert_fusion.11), channel_id=1, source_target_pairs={{0,16},{8,24},{16,0},{24,8},{1,17},{9,25},{17,1},{25,9},{2,18},{10... | collective-permute-start | bytes 602120 | tf_op jit(solution)/shard_map/ppermute | solution.py:643
  583.8 10.5 %collective-permute-start.53 = (bf16[448,128]{1,0:T(8,128)(2,1)S(1)}, bf16[448,128]{1,0:T(8,128)(2,1)S(1)}, u32[]{:S(2)}, u32[]{:S(2)}) collective-permute-start(bf16[448,128]{1,0:T(8,128)(2,1)S(1)} %add_convert_fusion.19), channel_id=1, source_target_pairs={{0,8},{8,0},{16,24},{24,16},{1,9},{9,1},{17,25},{25,17},{2,10},{10... | collective-permute-start | bytes 344072 | tf_op jit(solution)/shard_map/ppermute | solution.py:643
  584.1 10.2 %collective-permute-start.54 = (f32[2944]{0:T(1024)S(1)}, f32[2944]{0:T(1024)S(1)}, u32[]{:S(2)}, u32[]{:S(2)}) collective-permute-start(f32[2944]{0:T(1024)S(1)} %concatenate.171), channel_id=1, source_target_pairs={{0,8},{8,0},{16,24},{24,16},{1,9},{9,1},{17,25},{25,17},{2,10},{10... | collective-permute-start | bytes 35336 | tf_op jit(solution)/shard_map/ppermute | solution.py:643
  594.3 17.2 %collective-permute-start.55 = (bf16[448,128]{1,0:T(8,128)(2,1)S(1)}, bf16[448,128]{1,0:T(8,128)(2,1)S(1)}, u32[]{:S(2)}, u32[]{:S(2)}) collective-permute-start(bf16[448,128]{1,0:T(8,128)(2,1)S(1)} %add_convert_fusion.18), channel_id=1, source_target_pairs={{0,16},{8,24},{16,0},{24,8},{1,17},{9,25},{17,1},{25,9},{2,18},{10... | collective-permute-start | bytes 344072 | tf_op jit(solution)/shard_map/ppermute | solution.py:643
  596.8 14.7 %collective-permute-start.56 = (f32[2944]{0:T(1024)S(1)}, f32[2944]{0:T(1024)S(1)}, u32[]{:S(2)}, u32[]{:S(2)}) collective-permute-start(f32[2944]{0:T(1024)S(1)} %add.281), channel_id=1, source_target_pairs={{0,16},{8,24},{16,0},{24,8},{1,17},{9,25},{17,1},{25,9},{2,18},{10... | collective-permute-start | bytes 35336 | tf_op jit(solution)/shard_map/ppermute | solution.py:643
  616.2 9.4 %collective-permute-start.60 = (bf16[448,128]{1,0:T(8,128)(2,1)S(1)}, bf16[448,128]{1,0:T(8,128)(2,1)S(1)}, u32[]{:S(2)}, u32[]{:S(2)}) collective-permute-start(bf16[448,128]{1,0:T(8,128)(2,1)S(1)} %add_convert_fusion.16), channel_id=1, source_target_pairs={{0,2},{2,0},{1,3},{3,1},{4,6},{6,4},{5,7},{7,5},{8,10},{10,8},{9,1... | collective-permute-start | bytes 344072 | tf_op jit(solution)/shard_map/ppermute | solution.py:33
  (85 other events, 717.2 us)
Sparse Core Ops, SparseCore 0:
  55.9 59.5 all-gather.3
  488.8 145.7 all-gather.5
